TPU v7x, 32 devices: a whole 2x2x4 slice. The times are simulated.
32 devices in a mesh: shot: 4 (over y, core), brick: 8 (over z, x).
Axes of the slice: x: 2, y: 2, z: 4, core: 2. Of those that a mesh axis runs over, the one named last changes fastest.
Arguments:
- pressure: float32 [32, 256, 512], P('shot', 'brick'), may hold values from -6 to 6
- auxiliary: float32 [32, 256, 512], P('shot', 'brick'), may hold values from -6 to 6
- pressure_prior: float32 [32, 256, 512], P('shot', 'brick'), may hold values from -6 to 6
- auxiliary_prior: float32 [32, 256, 512], P('shot', 'brick'), may hold values from -6 to 6
- courant_sq: float32 [256, 512], P('brick'), may hold values from 0.05 to 0.2
- thomsen_epsilon: float32 [256, 512], P('brick'), may hold values from 0.1 to 0.35
- thomsen_delta: float32 [256, 512], P('brick'), may hold values from 0 to 0.1
- tilt_angle: float32 [256, 512], P('brick'), may hold values from -3.140625 to 3.140625
- frequencies: float32 [16], replicated, may hold values from 0.05 to 1.5
- spectra: float32 [32, 32, 4096], P('shot', None, 'brick'), may hold values from -6 to 6
- target_cells: int32 [4096], P('brick'), may hold values from 0 to 16383, as said below
- patch_lists: int32 [8, 4, 3, 128], P('brick'), may hold values from 0 to 511, as said below
- patch_counts: int32 [8, 4], P('brick', 'shot'), may hold values from 1 to 3, as said below
Outputs:
- pressure_out: float32 [32, 256, 512], P('shot', 'brick')
- auxiliary_out: float32 [32, 256, 512], P('shot', 'brick')
- spectra_out: float32 [32, 32, 4096], P('shot', None, 'brick')
- gram_tiles: float32 [8, 4, 3, 128, 128], P('brick', 'shot')
Inputs may be any that keep to these rules, and one draw needn't show every extreme that they name: `target_cells`: the block of each brick holds distinct cells of that brick. `patch_lists`: target numbers within the owner's brick; the cells of one patch slot are distinct. `patch_counts`: in every brick some owner has all 3 slots live.
All inputs are finite; a program needn't handle non-finite values.
Results may differ from a plain program's by a relative error of at most 0.00077.
Values may be sent and summed in bfloat16 or wider, within the bound.
No kernel may reach another device: no remote copies, remote signals or barrier semaphores. Data moves between devices by JAX's collectives and lax.ppermute only.
A program may use at most 64 MiB of HBM per device.

v0:
```python
import jax
import jax.numpy as jnp
from jax import lax
from jax.sharding import PartitionSpec as P

STEPS = 4
PATCH = 128
P_MAX = 3


def with_halo(cells, sides, width):
    for axis, dim in sides:
        count = lax.axis_size(axis)
        ends = count - 1
        head = lax.slice_in_dim(cells, 0, width, axis=dim)
        tail = lax.slice_in_dim(cells, cells.shape[dim] - width, cells.shape[dim], axis=dim)
        cells = jnp.concatenate(
            [
                lax.ppermute(tail, axis, [(i, (i + 1) % count) for i in range(ends)]),
                cells,
                lax.ppermute(head, axis, [((i + 1) % count, i) for i in range(ends)]),
            ],
            axis=dim,
        )
    return cells


def tilt_terms(tilt_angle):
    sine = jnp.sin(tilt_angle)
    cosine = jnp.cos(tilt_angle)
    return (sine * sine, cosine * cosine, 2.0 * sine * cosine)


def derivatives(field, sine_sq, cosine_sq, double_sin):
    widths = [(0, 0)] * (field.ndim - 1) + [(1, 1)]
    padded = jnp.pad(field, widths)
    centre = padded[..., 1:-1, 1:-1]
    second_x = padded[..., 2:, 1:-1] - 2.0 * centre + padded[..., :-2, 1:-1]
    second_z = padded[..., 1:-1, 2:] - 2.0 * centre + padded[..., 1:-1, :-2]
    mixed = 0.25 * (
        padded[..., 2:, 2:] - padded[..., 2:, :-2] - padded[..., :-2, 2:] + padded[..., :-2, :-2]
    )
    along_axis = sine_sq * second_x + cosine_sq * second_z + double_sin * mixed
    across_axis = second_x + second_z - along_axis
    return (along_axis, across_axis)


def leapfrog(extended, former, coefficients):
    courant_sq, epsilon, delta_value, sine_sq, cosine_sq, double_sin = coefficients
    along_p, across_p = derivatives(extended[0], sine_sq, cosine_sq, double_sin)
    along_q, across_q = derivatives(extended[1], sine_sq, cosine_sq, double_sin)
    pressure = extended[0][..., 1:-1, :]
    auxiliary = extended[1][..., 1:-1, :]
    pressure_next = (
        2.0 * pressure - former[0] + courant_sq * ((1.0 + 2.0 * epsilon) * across_p + along_q)
    )
    auxiliary_next = (
        2.0 * auxiliary - former[1] + courant_sq * ((1.0 + 2.0 * delta_value) * across_p + along_q)
    )
    return jnp.stack([pressure_next, auxiliary_next])


def shards(
    pressure,
    auxiliary,
    pressure_prior,
    auxiliary_prior,
    courant_sq,
    thomsen_epsilon,
    thomsen_delta,
    tilt_angle,
    frequencies,
    spectra,
    target_cells,
    patch_lists,
    patch_counts,
):
    shots_here, width_x, depth = pressure.shape
    samples = []
    packed = jnp.concatenate(
        [
            jnp.stack([pressure, auxiliary, pressure_prior, auxiliary_prior]).reshape(
                4 * shots_here, width_x, depth
            ),
            jnp.stack([courant_sq, thomsen_epsilon, thomsen_delta, tilt_angle]),
        ],
        0,
    )
    widened = with_halo(packed, (("brick", 1),), STEPS)
    states = widened[: 4 * shots_here].reshape(4, shots_here, width_x + 2 * STEPS, depth)
    params = widened[4 * shots_here :]
    sine_sq, cosine_sq, double_sin = tilt_terms(params[3])
    full_coefficients = (params[0], params[1], params[2], sine_sq, cosine_sq, double_sin)
    current = states[:2]
    former = states[2:]
    for moment in range(STEPS):
        trimmed = moment + 1
        coefficients = tuple(
            (item[trimmed : item.shape[0] - trimmed] for item in full_coefficients)
        )
        advanced = leapfrog(current, former[:, :, 1:-1], coefficients)
        former = current[:, :, 1:-1]
        current = advanced
        margin = STEPS - moment - 1
        interior = current[0][:, margin : margin + width_x]
        samples.append(
            jnp.take(interior.reshape(shots_here, width_x * depth), target_cells, axis=1)
        )
    spectra_out = spectra
    for moment in range(STEPS):
        angle = frequencies * (moment + 1.0)
        table = jnp.concatenate([jnp.cos(angle), -jnp.sin(angle)])
        spectra_out = spectra_out + table[None, :, None] * samples[moment][:, None, :]
    local_features = spectra_out.shape[0] * spectra_out.shape[1]
    features = spectra_out.reshape(local_features, spectra_out.shape[2]).astype(jnp.bfloat16)
    owners = patch_lists.shape[1]
    total_features = local_features * owners
    live_slots = (jnp.arange(P_MAX, dtype=jnp.int32) < patch_counts[0, 0]).astype(jnp.float32)
    columns = patch_lists[0].reshape(-1)
    chosen = jnp.take(features, columns, axis=1).reshape(local_features, owners, P_MAX, PATCH)
    blocks = lax.all_to_all(chosen, "shot", split_axis=1, concat_axis=1, tiled=True)
    grams = jnp.einsum("fgpa,fgpb->pab", blocks, blocks, preferred_element_type=jnp.float32)
    gram_tiles = grams / total_features * live_slots[:, None, None]
    return (current[0], current[1], spectra_out, gram_tiles.reshape(1, 1, P_MAX, PATCH, PATCH))


def solution(mesh):
    return jax.shard_map(
        shards,
        mesh=mesh,
        in_specs=(
            P("shot", "brick", None),
            P("shot", "brick", None),
            P("shot", "brick", None),
            P("shot", "brick", None),
            P("brick", None),
            P("brick", None),
            P("brick", None),
            P("brick", None),
            P(),
            P("shot", None, "brick"),
            P("brick"),
            P("brick", None, None, None),
            P("brick", "shot"),
        ),
        out_specs=(
            P("shot", "brick", None),
            P("shot", "brick", None),
            P("shot", None, "brick"),
            P("brick", "shot", None, None, None),
        ),
        check_vma=False,
    )
```

profile of v0, /device:TPU:16, one launch (start us, length us, event | category | flops | bytes accessed | tf_op | source)
XLA Modules:
  0.0 96.5 jit_solution(2708596510205092356)
XLA Ops:
  0.6 1.7 %pad_maximum_fusion.1 = f32[4,8,32,512]{3,2,1,0:T(8,128)S(1)} fusion(f32[1,8,32,512]{3,2,1,0:T(8,128)} %bitcast.156, f32[1,8,32,512]{3,2,1,0:T(8,128)} %bitcast.157, f32[1,8,32,512]{3,2,1,0:T(8,128)} %bitcast.158, f32[1,8,32,512]{3,2,1,0:T(8,128)} %bitcast.159), kind=kLoop, calls=%fused_computation.6 | loop fusion | flops 1572864 | bytes 4194304 | tf_op jit(solution)/shard_map/stack | solution.py:82
  2.4 0.2 constant_dynamic-update-slice_fusion
  2.7 0.5 copy-done.2
  3.3 0.8 fusion.119
  4.1 3.4 %collective-permute-start = (f32[36,4,512]{2,1,0:T(4,128)}, f32[36,4,512]{2,1,0:T(4,128)S(1)}, u32[]{:S(2)}, u32[]{:S(2)}) collective-permute-start(f32[36,4,512]{2,1,0:T(4,128)} %get-tuple-element.34), channel_id=1, source_target_pairs={{0,1},{1,2},{2,3},{3,4},{4,5},{5,6},{6,7},{8,9},{9,10},{10,11},{11... | collective-permute-start | bytes 884744 | tf_op jit(solution)/shard_map/ppermute | solution.py:19
  7.5 3.3 %collective-permute-start.1 = (f32[36,4,512]{2,1,0:T(4,128)S(1)}, f32[36,4,512]{2,1,0:T(4,128)S(1)}, u32[]{:S(2)}, u32[]{:S(2)}) collective-permute-start(f32[36,4,512]{2,1,0:T(4,128)S(1)} %get-tuple-element.35), channel_id=1, source_target_pairs={{1,0},{2,1},{3,2},{4,3},{5,4},{6,5},{7,6},{9,8},{10,9},{11,10},{12... | collective-permute-start | bytes 884744 | tf_op jit(solution)/shard_map/ppermute | solution.py:21
  10.9 0.6 compare_and_fusion.1
  11.5 0.6 multiply_add_fusion.2
  12.1 0.1 fusion.121
  12.3 0.6 pad_maximum_fusion.3
  12.9 0.6 pad_maximum_fusion.5
  13.5 6.9 %collective-permute-done = f32[36,4,512]{2,1,0:T(4,128)S(1)} collective-permute-done((f32[36,4,512]{2,1,0:T(4,128)}, f32[36,4,512]{2,1,0:T(4,128)S(1)}, u32[]{:S(2)}, u32[]{:S(2)}) %collective-permute-start) | collective-permute-done | bytes 294944 | tf_op jit(solution)/shard_map/ppermute | solution.py:19
  20.4 1.8 %collective-permute-done.1 = f32[36,4,512]{2,1,0:T(4,128)S(1)} collective-permute-done((f32[36,4,512]{2,1,0:T(4,128)S(1)}, f32[36,4,512]{2,1,0:T(4,128)S(1)}, u32[]{:S(2)}, u32[]{:S(2)}) %collective-permute-start.1) | collective-permute-done | bytes 294944 | tf_op jit(solution)/shard_map/ppermute | solution.py:21
  22.2 0.3 fusion.116
  22.5 0.3 multiply_multiply_fusion
  22.9 0.4 pad_maximum_fusion
  23.3 0.1 fusion.117
  23.4 0.3 fusion.118
  23.8 2.3 %fusion.67 = (f32[8,38,512]{2,1,0:T(8,128)S(1)}, f32[8,38,512]{2,1,0:T(8,128)S(1)}, f32[8,38,512]{2,1,0:T(8,128)S(1)}) fusion(f32[2,8,40,512]{3,2,1,0:T(8,128)S(1)} %bitcast.152, f32[36,40,512]{2,1,0:T(8,128)S(1)} %pad_maximum_fusion, f32[38,512]{1,0:T(8,128)S(1)} %get-tuple-element.28, f32[38,512]{1,0:T(8,128)S(1)} %get-tuple-element.29, ...), kind=kLoop, calls=%fused_computation.147 | loop fusion | flops 5136384 | bytes 7925760 | tf_op jit(solution)/shard_map/add | solution.py:55
  26.1 0.3 fusion.62
  26.5 2.3 %fusion.57 = (f32[8,36,512]{2,1,0:T(8,128)S(1)}, f32[8,36,512]{2,1,0:T(8,128)S(1)}, f32[8,36,512]{2,1,0:T(8,128)S(1)}) fusion(f32[2,8,40,512]{3,2,1,0:T(8,128)S(1)} %bitcast.150, f32[8,38,512]{2,1,0:T(8,128)S(1)} %fusion.62, f32[36,512]{1,0:T(8,128)S(1)} %get-tuple-element.25, f32[36,512]{1,0:T(8,128)S(1)} %get-tuple-element.26, ...), kind=kLoop, calls=%fused_computation.119 | loop fusion | flops 4866048 | bytes 8077312 | tf_op jit(solution)/shard_map/add | solution.py:58
  28.8 0.3 fusion.64
  29.2 0.9 slice.655
  30.1 2.3 %fusion.59 = (f32[8,34,512]{2,1,0:T(8,128)S(1)}, f32[8,34,512]{2,1,0:T(8,128)S(1)}, f32[8,34,512]{2,1,0:T(8,128)S(1)}) fusion(f32[1,8,38,512]{3,2,1,0:T(8,128)S(1)} %bitcast.141, f32[8,36,512]{2,1,0:T(8,128)S(1)} %fusion.64, f32[34,512]{1,0:T(8,128)S(1)} %get-tuple-element.22, f32[34,512]{1,0:T(8,128)S(1)} %get-tuple-element.23, ...), kind=kLoop, calls=%fused_computation.124 | loop fusion | flops 4595712 | bytes 7979008 | tf_op jit(solution)/shard_map/add | solution.py:55
  32.4 0.3 fusion.54
  32.7 2.6 %fusion.86 = (f32[8,32,512]{2,1,0:T(8,128)}, f32[8,32,512]{2,1,0:T(8,128)S(1)}, f32[8,32,512]{2,1,0:T(8,128)S(1)}) fusion(f32[1,8,36,512]{3,2,1,0:T(8,128)S(1)} %bitcast.142, f32[8,34,512]{2,1,0:T(8,128)S(1)} %fusion.54, f32[32,512]{1,0:T(8,128)S(1)} %multiply_add_fusion.1, f32[32,512]{1,0:T(8,128)S(1)} %copy-done.2, f32[32,512]{1,0:T(8,128)S(1)} %get-tuple-element.59, ...), kind=kLoop, calls=%fused_computation.168 | loop fusion | flops 4325376 | bytes 6881280 | tf_op jit(solution)/shard_map/add | solution.py:58
  35.3 0.5 fusion.120
  35.8 4.6 %copy.43 = f32[8,32,512]{0,2,1:T(8,128)} copy(f32[8,32,512]{2,1,0:T(8,128)S(1)} %get-tuple-element.36) | data formatting | bytes 1048576 | tf_op jit(solution)/shard_map/slice | solution.py:52
  40.5 4.7 %copy.41 = f32[8,32,512]{0,2,1:T(8,128)} copy(f32[8,32,512]{2,1,0:T(8,128)S(1)} %copy-done.1) | data formatting | bytes 1048576 | tf_op jit(solution)/shard_map/slice | solution.py:105
  45.1 4.4 %gather_fusion.3 = f32[512,8]{1,0:T(8,128)S(1)} fusion(f32[8,16384]{0,1:T(8,128)} %bitcast.145, s32[1024]{0:T(1024)S(1)} %pad_clamp_fusion.1), kind=kCustom, calls=%fused_computation.2.clone | custom fusion | bytes 34816 | tf_op jit(solution)/shard_map/jit(_take)/gather | solution.py:107
  49.6 4.4 %gather_fusion.2 = f32[512,8]{1,0:T(8,128)S(1)} fusion(f32[8,16384]{0,1:T(8,128)} %bitcast.146, s32[1024]{0:T(1024)S(1)} %pad_clamp_fusion.1), kind=kCustom, calls=%fused_computation.1.clone | custom fusion | bytes 34816 | tf_op jit(solution)/shard_map/jit(_take)/gather | solution.py:107
  54.0 4.7 %copy.39 = f32[8,32,512]{0,2,1:T(8,128)} copy(f32[8,32,512]{2,1,0:T(8,128)S(1)} %slice.654) | data formatting | bytes 1048576 | tf_op jit(solution)/shard_map/slice | solution.py:105
  58.6 4.4 %gather_fusion.1 = f32[512,8]{1,0:T(8,128)S(1)} fusion(f32[8,16384]{0,1:T(8,128)} %bitcast.147, s32[1024]{0:T(1024)S(1)} %pad_clamp_fusion.1), kind=kCustom, calls=%fused_computation.clone | custom fusion | bytes 34816 | tf_op jit(solution)/shard_map/jit(_take)/gather | solution.py:107
  63.1 4.7 %copy.45 = f32[8,32,512]{0,2,1:T(8,128)} copy(f32[8,32,512]{2,1,0:T(8,128)S(1)} %get-tuple-element.37) | data formatting | bytes 1048576 | tf_op jit(solution)/shard_map/add | solution.py:55
  67.8 4.5 %gather_fusion.4 = f32[512,8]{1,0:T(8,128)S(1)} fusion(f32[8,16384]{0,1:T(8,128)} %bitcast.148, s32[1024]{0:T(1024)S(1)} %pad_clamp_fusion.1), kind=kCustom, calls=%fused_computation.3.clone | custom fusion | bytes 34816 | tf_op jit(solution)/shard_map/jit(_take)/gather | solution.py:107
  72.3 0.1 select_bitcast_fusion.3
  72.4 0.1 copy.40
  72.5 0.1 copy.42
  72.6 0.1 copy.44
  72.7 0.1 copy.46
  72.9 1.0 %fusion.107 = (bf16[8,32,512]{2,1,0:T(8,128)(2,1)S(1)}, f32[8,32,512]{2,1,0:T(8,128)}) fusion(f32[8,512]{1,0:T(8,128)S(1)} %copy.46, f32[32]{0:T(128)S(1)} %copy-done.14, f32[8,512]{1,0:T(8,128)S(1)} %copy.44, f32[32]{0:T(128)S(1)} %copy-done.13, f32[8,512]{1,0:T(8,128)S(1)} %copy.42, f32[32]{0:T(128)S(1)} %copy-done.12, f32[8,32,512]{2,1,0:T(8,128)S(1)} %copy-done.3, ...), kind=kLoop, calls=%fused_computation.249 | loop fusion | flops 1179648 | bytes 1376768 | tf_op jit(solution)/shard_map/convert_element_type | solution.py:115
  73.9 0.1 copy.49
  74.0 4.8 %gather_fusion = bf16[1536,256]{1,0:T(8,128)(2,1)S(1)} fusion(bf16[256,512]{0,1:T(8,128)(2,1)S(1)} %copy.49, s32[2048]{0:T(1024)S(1)} %pad_clamp_fusion), kind=kCustom, calls=%fused_computation.4 | custom fusion | bytes 1579008 | tf_op jit(solution)/shard_map/jit(_take)/gather | solution.py:120
  78.8 0.3 broadcast_select_fusion
  79.1 1.2 %copy.50 = bf16[256,4,3,128]{3,0,2,1:T(8,128)(2,1)} copy(bf16[256,4,3,128]{0,3,2,1:T(8,128)(2,1)S(1)} %broadcast_select_fusion) | data formatting | bytes 1572864 | tf_op jit(solution)/shard_map/jit(_take)/select_n | solution.py:120
  80.2 3.5 %all-to-all-start = ((bf16[256,4,3,128]{3,0,2,1:T(8,128)(2,1)}), bf16[256,4,3,128]{3,0,2,1:T(8,128)(2,1)S(1)}, u32[]{:S(2)}, u32[]{:S(2)}) async-start(bf16[256,4,3,128]{3,0,2,1:T(8,128)(2,1)} %copy.50), calls=%async_computation | async-start | bytes 1572864 | tf_op jit(solution)/shard_map/all_to_all | solution.py:121
  84.4 11.0 %all-to-all-done = bf16[256,4,3,128]{3,0,2,1:T(8,128)(2,1)S(1)} async-done(((bf16[256,4,3,128]{3,0,2,1:T(8,128)(2,1)}), bf16[256,4,3,128]{3,0,2,1:T(8,128)(2,1)S(1)}, u32[]{:S(2)}, u32[]{:S(2)}) %all-to-all-start) | async-done | bytes 786464 | tf_op jit(solution)/shard_map/all_to_all | solution.py:121
  95.3 1.1 %fusion.1 = f32[1,1,3,128,128]{4,3,2,1,0:T(8,128)} fusion(bf16[256,4,3,128]{3,0,2,1:T(8,128)(2,1)S(1)} %all-to-all-done, f32[3]{0:T(128)S(1)} %compare_select_fusion.3), kind=kOutput, calls=%fused_computation.9 | convolution fusion | flops 100712448 | bytes 983052 | tf_op jit(solution)/shard_map/fgpa,fgpb->pab/dot_general | solution.py:122
  (54 shorter events, 0.6 us)
Async XLA Ops:
  2.3 0.8 copy-start.2
  2.3 0.9 copy-start.5
  2.4 0.9 copy-start.6
  2.4 0.9 copy-start.7
  2.4 8.5 %copy-start.9 = (s32[512]{0:T(512)S(1)}, s32[512]{0:T(512)}, u32[]{:S(2)}) copy-start(s32[512]{0:T(512)} %param.25) | copy-start | bytes 6148
  2.4 9.1 %copy-start.8 = (s32[1,4,3,128]{3,1,2,0:T(4,128)S(1)}, s32[1,4,3,128]{3,1,2,0:T(4,128)}, u32[]{:S(2)}) copy-start(s32[1,4,3,128]{3,1,2,0:T(4,128)} %param.26) | copy-start | bytes 18436
  2.4 9.7 %copy-start.15 = (f32[16]{0:T(128)S(1)}, f32[16]{0:T(128)}, u32[]{:S(2)}) copy-start(f32[16]{0:T(128)} %param.23) | copy-start | bytes 196
  4.1 16.3 %collective-permute-start = (f32[36,4,512]{2,1,0:T(4,128)}, f32[36,4,512]{2,1,0:T(4,128)S(1)}, u32[]{:S(2)}, u32[]{:S(2)}) collective-permute-start(f32[36,4,512]{2,1,0:T(4,128)} %get-tuple-element.34), channel_id=1, source_target_pairs={{0,1},{1,2},{2,3},{3,4},{4,5},{5,6},{6,7},{8,9},{9,10},{10,11},{11... | collective-permute-start | bytes 884744 | tf_op jit(solution)/shard_map/ppermute | solution.py:19
  7.5 14.7 %collective-permute-start.1 = (f32[36,4,512]{2,1,0:T(4,128)S(1)}, f32[36,4,512]{2,1,0:T(4,128)S(1)}, u32[]{:S(2)}, u32[]{:S(2)}) collective-permute-start(f32[36,4,512]{2,1,0:T(4,128)S(1)} %get-tuple-element.35), channel_id=1, source_target_pairs={{1,0},{2,1},{3,2},{4,3},{5,4},{6,5},{7,6},{9,8},{10,9},{11,10},{12... | collective-permute-start | bytes 884744 | tf_op jit(solution)/shard_map/ppermute | solution.py:21
  32.7 2.6 %copy-start.4 = (f32[32,512]{1,0:T(8,128)S(1)}, f32[32,512]{1,0:T(8,128)}, u32[]{:S(2)}) copy-start(f32[32,512]{1,0:T(8,128)} %multiply_add_fusion.2) | copy-start | bytes 196612
  35.8 27.3 %copy-start = (f32[8,32,512]{2,1,0:T(8,128)}, f32[8,32,512]{2,1,0:T(8,128)S(1)}, u32[]{:S(2)}) copy-start(f32[8,32,512]{2,1,0:T(8,128)S(1)} %get-tuple-element.37) | copy-start | bytes 1572868
  35.8 4.6 %copy-start.1 = (f32[8,32,512]{2,1,0:T(8,128)S(1)}, f32[8,32,512]{2,1,0:T(8,128)}, u32[]{:S(2)}) copy-start(f32[8,32,512]{2,1,0:T(8,128)} %slice.655) | copy-start | bytes 1572868
  63.1 9.2 %copy-start.10 = (pred[512]{0:T(512)(128)(4,1)S(1)}, pred[512]{0:T(512)(128)(4,1)}, u32[]{:S(2)}) copy-start(pred[512]{0:T(512)(128)(4,1)} %compare_and_fusion.1) | copy-start | bytes 1540
  67.8 5.1 %copy-start.3 = (f32[8,32,512]{2,1,0:T(8,128)S(1)}, f32[8,32,512]{2,1,0:T(8,128)}, u32[]{:S(2)}) copy-start(f32[8,32,512]{2,1,0:T(8,128)} %param.24) | copy-start | bytes 1572868
  67.8 5.1 %copy-start.11 = (f32[32]{0:T(128)S(1)}, f32[32]{0:T(128)}, u32[]{:S(2)}) copy-start(f32[32]{0:T(128)} %get-tuple-element.64) | copy-start | bytes 388
  67.8 5.1 %copy-start.12 = (f32[32]{0:T(128)S(1)}, f32[32]{0:T(128)}, u32[]{:S(2)}) copy-start(f32[32]{0:T(128)} %get-tuple-element.65) | copy-start | bytes 388
  67.8 5.1 %copy-start.13 = (f32[32]{0:T(128)S(1)}, f32[32]{0:T(128)}, u32[]{:S(2)}) copy-start(f32[32]{0:T(128)} %get-tuple-element.66) | copy-start | bytes 388
  67.8 5.1 %copy-start.14 = (f32[32]{0:T(128)S(1)}, f32[32]{0:T(128)}, u32[]{:S(2)}) copy-start(f32[32]{0:T(128)} %get-tuple-element.67) | copy-start | bytes 388
  80.2 15.1 %all-to-all-start = ((bf16[256,4,3,128]{3,0,2,1:T(8,128)(2,1)}), bf16[256,4,3,128]{3,0,2,1:T(8,128)(2,1)S(1)}, u32[]{:S(2)}, u32[]{:S(2)}) async-start(bf16[256,4,3,128]{3,0,2,1:T(8,128)(2,1)} %copy.50), calls=%async_computation | async-start | bytes 1572864 | tf_op jit(solution)/shard_map/all_to_all | solution.py:121
where the time goes:
time: 96.9 us; the launch traced here: 96.5 us
  local copies, waits for them, and re-layouts  45.9 us (47%)
  waiting for transfers between devices  19.6 us (20%)
  other arithmetic  17.9 us (18%)
  starting transfers between devices  10.2 us (11%)
  between operations  1.73 us (2%)
  matrix products  1.13 us (1%)
    gather x4, local copies, waits for them, and re-layouts, shards(): jnp.take(interior.reshape(shots_here, width_x * depth), target_cells, axi...  17.7 us
    all_to_all x1, waiting for transfers between devices, shards(): lax.all_to_all(chosen, 'shot', split_axis=1, concat_axis=1, tiled=True)  11 us
    slice x4, local copies, waits for them, and re-layouts, shards(): interior = current[0][:, margin:margin + width_x]  10.3 us
    ppermute x1, waiting for transfers between devices, with_halo(): lax.ppermute(tail, axis, [(i, (i + 1) % count) for i in range(ends)])  6.87 us
    add x4, other arithmetic, leapfrog(): 2.0 * auxiliary - former[1]  5.57 us
    add x3, other arithmetic, leapfrog(): 2.0 * pressure - former[0]  4.87 us
    gather x1, local copies, waits for them, and re-layouts, shards(): jnp.take(features, columns, axis=1)  4.76 us
    add x1, local copies, waits for them, and re-layouts, leapfrog(): 2.0 * pressure - former[0]  4.68 us
  transfers between devices with their start and end apart: 3, of which 3 were waited for; matrix products, arithmetic and copies ran while one was open for 3% of the time, Pallas kernels for 0%

commit v1 on v0

v1 whole, which is shorter than its diff:
```python
import functools
import math

import jax
import jax.numpy as jnp
from jax import lax
from jax.experimental import pallas as pl
from jax.experimental.pallas import tpu as pltpu
from jax.sharding import PartitionSpec as P

STEPS = 4
MIB = 1024 * 1024
NT = (((1,), (1,)), ((), ()))


TILE = 8
LANES = 128


def tiled(field):
    shots, width, depth = field.shape
    parts = field.reshape(shots, width // TILE, TILE, depth // LANES, LANES)
    return parts.transpose(0, 1, 3, 2, 4)


def untiled(parts):
    shots, across, along, tile, lanes = parts.shape
    return parts.transpose(0, 1, 3, 2, 4).reshape(shots, across * tile, along * lanes)


class ShotRows:
    def __init__(self, ref):
        self.shots, self.across, self.along, tile, lanes = ref.shape
        self.stride = self.across * self.along * tile
        self.flat = ref.reshape(self.shots * self.stride, lanes)

    def place(self, x, j):
        if isinstance(x, int):
            start = (x // TILE * self.along + j) * TILE + x % TILE
        else:
            start = (lax.div(x, TILE) * self.along + j) * TILE + lax.rem(x, TILE)
        return pl.ds(start, self.shots, stride=self.stride)

    def __getitem__(self, x):
        return jnp.concatenate([self.flat[self.place(x, j), :] for j in range(self.along)], 1)

    def __setitem__(self, x, row):
        for j in range(self.along):
            self.flat[self.place(x, j), :] = row[:, j * LANES : (j + 1) * LANES]


def compiler_params(mib):
    return pltpu.CompilerParams(vmem_limit_bytes=mib * MIB)


def tilt_coefficients(courant, epsilon, delta, tilt):
    turns = jnp.round(tilt * (2.0 / math.pi))
    rest = (tilt - turns * 1.5703125) - turns * (math.pi / 2 - 1.5703125)
    odd = turns - 2.0 * jnp.floor(turns * 0.5)
    sign = 1.0 - 2.0 * odd
    double = 2.0 * rest
    square = double * double
    sine = double * (
        1.0
        + square
        * (
            -1.0 / 6
            + square
            * (1.0 / 120 + square * (-1.0 / 5040 + square * (1.0 / 362880 - square / 39916800.0)))
        )
    )
    versine = square * (
        0.5
        + square
        * (
            -1.0 / 24
            + square
            * (1.0 / 720 + square * (-1.0 / 40320 + square * (1.0 / 3628800 - square / 479001600.0)))
        )
    )
    sine_sq = jnp.where(odd > 0.5, 1.0 - 0.5 * versine, 0.5 * versine)
    quarter_sin = 0.25 * sign * sine
    gain_p = courant * (1.0 + 2.0 * epsilon)
    gain_q = courant * (1.0 + 2.0 * delta)
    return sine_sq, quarter_sin, courant, gain_p, gain_q


def depth_terms(row):
    depth = row.shape[-1]
    lane = lax.broadcasted_iota(jnp.int32, row.shape, 1)
    deeper = jnp.where(lane < depth - 1, pltpu.roll(row, depth - 1, 1), 0.0)
    upper = jnp.where(lane > 0, pltpu.roll(row, 1, 1), 0.0)
    return deeper + upper, deeper - upper


def advance(count, p_row, q_row, p_prior, q_prior, coefficient, put):
    p_back, p_here = p_row(-1), p_row(0)
    q_back, q_here = q_row(-1), q_row(0)
    _, p_back_d = depth_terms(p_back)
    _, q_back_d = depth_terms(q_back)
    p_sum, p_here_d = depth_terms(p_here)
    q_sum, q_here_d = depth_terms(q_here)
    for row in range(count):
        p_next, q_next = p_row(row + 1), q_row(row + 1)
        p_next_sum, p_next_d = depth_terms(p_next)
        q_next_sum, q_next_d = depth_terms(q_next)
        sine_sq, quarter_sin, courant, gain_p, gain_q = coefficient(row)
        twice_p, twice_q = p_here + p_here, q_here + q_here
        side = p_next + p_back
        across = (side - twice_p) + sine_sq * (p_sum - side) - quarter_sin * (p_next_d - p_back_d)
        side = q_next + q_back
        along = (q_sum - twice_q) + sine_sq * (side - q_sum) + quarter_sin * (q_next_d - q_back_d)
        along = courant * along
        put(
            row,
            (twice_p - p_prior(row)) + (gain_p * across + along),
            (twice_q - q_prior(row)) + (gain_q * across + along),
        )
        p_back, p_here, p_back_d, p_here_d, p_sum = p_here, p_next, p_here_d, p_next_d, p_next_sum
        q_back, q_here, q_back_d, q_here_d, q_sum = q_here, q_next, q_here_d, q_next_d, q_next_sum


def split_bf16(values):
    high = values.astype(jnp.bfloat16)
    low = (values - high.astype(jnp.float32)).astype(jnp.bfloat16)
    return high, low


def outer_kernel(*refs):
    fields, params, outs = refs[:8], refs[8:16], refs[16:]
    shots, tile = fields[0].shape[0], fields[0].shape[3]
    depth = params[0].shape[1]
    for side in range(2):
        views = [ShotRows(ref) for ref in fields[4 * side : 4 * side + 4]]
        out = outs[side]

        def row(field, distance):
            place = distance if side == 0 else tile - 1 - distance
            return views[field][place]

        position = 0

        def put(first, second):
            nonlocal position
            out[pl.ds(position, 2 * shots), :] = jnp.concatenate([first, second], 0).astype(
                jnp.bfloat16
            )
            position += 2 * shots

        for field in range(4):
            near = row(field, 0)
            put(near, near - near.astype(jnp.bfloat16).astype(jnp.float32))
        for first, second in far_items():
            put(row(*first), row(*second))
        terms = tilt_coefficients(*[ref[...] for ref in params[4 * side : 4 * side + 4]])
        rows = []
        for term in terms:
            for distance in range(STEPS - 1):
                place = distance if side == 0 else tile - 1 - distance
                rows.append(term[place : place + 1, :])
        while len(rows) < 2 * shots:
            rows.append(jnp.zeros((1, depth), jnp.float32))
        out[pl.ds(position, 2 * shots), :] = jnp.concatenate(rows, 0).astype(jnp.bfloat16)


def far_items():
    items = []
    for field in range(2):
        items += [(field, distance) for distance in range(1, STEPS)]
    for field in range(2, 4):
        items += [(field, distance) for distance in range(1, STEPS - 1)]
    return list(zip(items[0::2], items[1::2]))


def outer_rows(fields, params):
    shots, across, along, tile, lanes = fields[0].shape
    depth = along * lanes
    last = across - 1
    field_specs, param_specs = [], []
    for place in (0, last):
        field_specs += [
            pl.BlockSpec((shots, 1, along, tile, lanes), lambda i, place=place: (0, place, 0, 0, 0))
        ] * 4
        param_specs += [pl.BlockSpec((tile, depth), lambda i, place=place: (place, 0))] * 4
    rows = 2 * shots * (4 + len(far_items()) + 1)
    shape = jax.ShapeDtypeStruct((rows, depth), jnp.bfloat16)
    return pl.pallas_call(
        outer_kernel,
        grid=(1,),
        in_specs=field_specs + param_specs,
        out_specs=[pl.BlockSpec((rows, depth), lambda i: (0, 0))] * 2,
        out_shape=[shape, shape],
        compiler_params=compiler_params(16),
        name="outer_rows",
    )(*fields, *fields, *params, *params)


def sample_rows(values, one_hot):
    high, low = split_bf16(values)
    return jnp.dot(jnp.concatenate([high, low], 1), one_hot, preferred_element_type=jnp.float32)


def interior_kernel(
    p_ref,
    q_ref,
    pp_ref,
    qq_ref,
    courant_ref,
    epsilon_ref,
    delta_ref,
    tilt_ref,
    cells_ref,
    lists_ref,
    edge_ref,
    prior_edge_ref,
    coef_edge_ref,
    p_inner_ref,
    q_inner_ref,
    sample_ref,
    depth_hot_ref,
    column_ref,
    list_hot_ref,
    level_ref,
    coef_ref,
):
    shots = p_ref.shape[0]
    width, depth = courant_ref.shape
    p_rows, q_rows, pp_rows, qq_rows = [ShotRows(ref) for ref in (p_ref, q_ref, pp_ref, qq_ref)]

    terms = tilt_coefficients(courant_ref[...], epsilon_ref[...], delta_ref[...], tilt_ref[...])
    for index, term in enumerate(terms):
        for x in range(width):
            coef_ref[index, x] = jnp.broadcast_to(term[x : x + 1, :], (shots, depth))
        flip = -term if index == 1 else term
        coef_edge_ref[0, index] = term[:8, :]
        coef_edge_ref[1, index] = flip[width - 8 :, :]

    @pl.loop(0, width)
    def _(x):
        level_ref[0, 0, x] = p_rows[x]
        level_ref[0, 1, x] = q_rows[x]

    cells = cells_ref[...]
    column = cells // depth
    z_of = cells - column * depth
    column_ref[...] = column
    targets = cells.shape[1]
    for half in range(2):
        for base in range(0, depth, 64):
            lanes = lax.broadcasted_iota(jnp.int32, (64, targets), 0) + base
            depth_hot_ref[pl.ds(half * depth + base, 64), :] = jnp.where(
                lanes == z_of, 1.0, 0.0
            ).astype(jnp.bfloat16)

    owners, slots, patch = lists_ref.shape[1:]
    rows = [lists_ref[0, g, s : s + 1, :] for g in range(owners) for s in range(slots)]
    count = len(rows)
    while len(rows) % 8:
        rows.append(rows[0])
    upright = jnp.transpose(jnp.concatenate(rows, 0).astype(jnp.float32))
    lanes = lax.broadcasted_iota(jnp.int32, (patch, targets), 1).astype(jnp.float32)
    for k in range(count):
        list_hot_ref[pl.ds(k * patch, patch), :] = jnp.where(
            upright[:, k : k + 1] == lanes, 1.0, 0.0
        ).astype(jnp.bfloat16)

    for side in range(2):
        x = 0 if side == 0 else width - 1
        prior_edge_ref[side, 0] = pp_rows[x]
        prior_edge_ref[side, 1] = qq_rows[x]

    chunk = 8
    for step in range(1, STEPS + 1):
        low, high = step, width - step
        chunks = -(-(high - low) // chunk)

        @pl.loop(0, chunks)
        def _(index):
            start = jnp.minimum(low + chunk * index, high - chunk)

            def prior(field):
                if step == 1:
                    rows = (pp_rows, qq_rows)[field]
                    return lambda r: rows[start + r]
                return lambda r: level_ref[step - 2, field, start + r]

            def put(r, p_new, q_new):
                if step < STEPS:
                    level_ref[step, 0, start + r] = p_new
                    level_ref[step, 1, start + r] = q_new
                else:
                    p_inner_ref[start + r - STEPS] = p_new
                    q_inner_ref[start + r - STEPS] = q_new

            advance(
                chunk,
                lambda r: level_ref[step - 1, 0, start + r],
                lambda r: level_ref[step - 1, 1, start + r],
                prior(0),
                prior(1),
                lambda r: [coef_ref[i, start + r] for i in range(5)],
                put,
            )

    for step in range(STEPS):
        for field in range(2):
            for near in range(2):
                edge_ref[0, field, step, near] = level_ref[step, field, step + near]
                edge_ref[1, field, step, near] = level_ref[step, field, width - 1 - step - near]

    for step in range(1, STEPS + 1):
        low, high = step, width - step
        if step < STEPS:
            values = level_ref[step, 0, low:high]
        else:
            values = p_inner_ref[...]
        found = sample_rows(values.reshape((high - low) * shots, depth), depth_hot_ref[...])
        total = jnp.zeros((shots, targets), jnp.float32)
        for r in range(high - low):
            total = total + jnp.where(column == low + r, found[r * shots : (r + 1) * shots], 0.0)
        sample_ref[step - 1] = total


def interior(fields, params, target_cells, patch_lists):
    shots = fields[0].shape[0]
    width, depth = params[0].shape
    targets = target_cells.shape[0]
    _, owners, slots, patch = patch_lists.shape
    f32 = functools.partial(jax.ShapeDtypeStruct, dtype=jnp.float32)
    out_shape = [
        f32((2, 2, STEPS, 2, shots, depth)),
        f32((2, 2, shots, depth)),
        f32((2, 5, 8, depth)),
        f32((width - 2 * STEPS, shots, depth)),
        f32((width - 2 * STEPS, shots, depth)),
        f32((STEPS, shots, targets)),
        jax.ShapeDtypeStruct((2 * depth, targets), jnp.bfloat16),
        jax.ShapeDtypeStruct((1, targets), jnp.int32),
        jax.ShapeDtypeStruct((owners * slots * patch, targets), jnp.bfloat16),
    ]
    vmem = pl.BlockSpec(memory_space=pltpu.VMEM)
    return pl.pallas_call(
        interior_kernel,
        in_specs=[vmem] * 10,
        out_specs=[vmem] * len(out_shape),
        out_shape=out_shape,
        scratch_shapes=[
            pltpu.VMEM((STEPS, 2, width, shots, depth), jnp.float32),
            pltpu.VMEM((5, width, shots, depth), jnp.float32),
        ],
        compiler_params=compiler_params(40),
        cost_estimate=pl.CostEstimate(
            flops=200 * STEPS * shots * width * depth, bytes_accessed=8 * MIB, transcendentals=0
        ),
        name="interior",
    )(*fields, *params, target_cells.reshape(1, targets), patch_lists)


def finish_kernel(
    lower_ref,
    upper_ref,
    edge_ref,
    prior_edge_ref,
    coef_edge_ref,
    sample_ref,
    depth_hot_ref,
    column_ref,
    list_hot_ref,
    spectra_ref,
    table_ref,
    spectra_out_ref,
    packed_ref,
    final_ref,
    level_ref,
    prior_ref,
    coef_ref,
    feature_ref,
    *,
    width,
):
    shots, depth = edge_ref.shape[-2:]
    targets = column_ref.shape[1]
    first = -STEPS
    pair = 2 * shots
    for side, ref in enumerate((lower_ref, upper_ref)):
        for field in range(4):
            both = ref[pl.ds(field * pair, pair), :].astype(jnp.float32)
            value = both[:shots] + both[shots:]
            if field < 2:
                level_ref[side, field, 0, -1 - first] = value
            else:
                prior_ref[side, field - 2, -1 - (1 - STEPS)] = value
        for index, items in enumerate(far_items()):
            both = ref[pl.ds((4 + index) * pair, pair), :].astype(jnp.float32)
            for half, (field, distance) in enumerate(items):
                value = both[half * shots : (half + 1) * shots]
                if field < 2:
                    level_ref[side, field, 0, -1 - distance - first] = value
                else:
                    prior_ref[side, field - 2, -1 - distance - (1 - STEPS)] = value
        params = ref[pl.ds((4 + len(far_items())) * pair, pair), :].astype(jnp.float32)
        for index in range(5):
            for distance in range(STEPS - 1):
                line = index * (STEPS - 1) + distance
                row = params[line : line + 1, :]
                if index == 1 and side == 1:
                    row = -row
                coef_ref[side, index, STEPS - 2 - distance] = jnp.broadcast_to(row, (shots, depth))
            for k in range(STEPS):
                coef_ref[side, index, STEPS - 1 + k] = jnp.broadcast_to(
                    coef_edge_ref[side, index, pl.ds(k if side == 0 else 7 - k, 1), :],
                    (shots, depth),
                )
        for field in range(2):
            prior_ref[side, field, STEPS - 1] = prior_edge_ref[side, field]
            for step in range(STEPS):
                for near in range(2):
                    level_ref[side, field, step, step + near - first] = edge_ref[
                        side, field, step, near
                    ]

    for step in range(1, STEPS + 1):
        low = step - STEPS

        for side in range(2):

            def prior(field):
                if step == 1:
                    return lambda r: prior_ref[side, field, low + r - (1 - STEPS)]
                return lambda r: level_ref[side, field, step - 2, low + r - first]

            def put(r, p_new, q_new):
                if step < STEPS:
                    level_ref[side, 0, step, low + r - first] = p_new
                    level_ref[side, 1, step, low + r - first] = q_new
                else:
                    final_ref[side, 0, r] = p_new
                    final_ref[side, 1, r] = q_new

            advance(
                STEPS,
                lambda r: level_ref[side, 0, step - 1, low + r - first],
                lambda r: level_ref[side, 1, step - 1, low + r - first],
                prior(0),
                prior(1),
                lambda r: [coef_ref[side, i, low + r - (1 - STEPS) + 0] for i in range(5)],
                put,
            )

    column = column_ref[...]
    places, values = [], []
    for step in range(1, STEPS + 1):
        for side in range(2):
            for k in range(step):
                places.append((step, k if side == 0 else width - 1 - k))
                if step < STEPS:
                    values.append(level_ref[side, 0, step, k - first])
                else:
                    values.append(final_ref[side, 0, k])
    found = sample_rows(jnp.concatenate(values, 0), depth_hot_ref[...])
    samples = [sample_ref[step] for step in range(STEPS)]
    for index, (step, x) in enumerate(places):
        samples[step - 1] = samples[step - 1] + jnp.where(
            column == x, found[index * shots : (index + 1) * shots], 0.0
        )

    parts = spectra_ref.shape[0] // shots
    lanes = table_ref.shape[-1]
    for s in range(shots):
        for base in range(0, targets, lanes):
            value = spectra_ref[pl.ds(s * parts, parts), pl.ds(base, lanes)]
            for step in range(STEPS):
                value = value + table_ref[step] * samples[step][s : s + 1, base : base + lanes]
            spectra_out_ref[pl.ds(s * parts, parts), pl.ds(base, lanes)] = value
            feature_ref[pl.ds(s * parts, parts), pl.ds(base, lanes)] = value.astype(jnp.bfloat16)

    owners = packed_ref.shape[0]
    patch = packed_ref.shape[2]
    slots = list_hot_ref.shape[0] // (owners * patch)
    half = patch // 2
    row = lax.broadcasted_iota(jnp.int32, (half, patch), 0)
    lane = lax.broadcasted_iota(jnp.int32, (half, patch), 1)
    from_last = (lane < half) & (row > lane)
    for g in range(owners):
        chosen = lax.dot_general(
            list_hot_ref[pl.ds(g * slots * patch, slots * patch), :],
            feature_ref[...],
            NT,
            preferred_element_type=jnp.float32,
        ).astype(jnp.bfloat16)
        diagonals = []
        for s in range(slots):
            mine = chosen[s * patch : (s + 1) * patch]
            gram = lax.dot_general(mine, mine, NT, preferred_element_type=jnp.float32)
            last = pltpu.roll(gram[half:], half, 1)
            packed_ref[g, pl.ds(s * half, half), :] = jnp.where(from_last, last, gram[:half])
            diagonals.append(jnp.sum(jnp.where(row == lane, last, 0.0), 0, keepdims=True))
        while len(diagonals) % 8:
            diagonals.append(jnp.zeros((1, patch), jnp.float32))
        packed_ref[g, pl.ds(slots * half, len(diagonals)), :] = jnp.concatenate(diagonals, 0)


def finish(lower, upper, inner, spectra, table, width, owners, slots, patch):
    edge, prior_edge, coef_edge, sample, depth_hot, column, list_hot = inner
    shots, depth = edge.shape[-2:]
    targets = column.shape[1]
    features = spectra.shape[0]
    f32 = functools.partial(jax.ShapeDtypeStruct, dtype=jnp.float32)
    rows = slots * (patch // 2) + -(-slots // 8) * 8
    out_shape = [
        f32((features, targets)),
        f32((owners, rows, patch)),
        f32((2, 2, STEPS, shots, depth)),
    ]
    vmem = pl.BlockSpec(memory_space=pltpu.VMEM)
    return pl.pallas_call(
        functools.partial(finish_kernel, width=width),
        in_specs=[vmem] * 11,
        out_specs=[vmem] * len(out_shape),
        out_shape=out_shape,
        scratch_shapes=[
            pltpu.VMEM((2, 2, STEPS, 2 * STEPS + 1, shots, depth), jnp.float32),
            pltpu.VMEM((2, 2, STEPS, shots, depth), jnp.float32),
            pltpu.VMEM((2, 5, 2 * STEPS - 1, shots, depth), jnp.float32),
            pltpu.VMEM((features, targets), jnp.bfloat16),
        ],
        compiler_params=compiler_params(40),
        name="finish",
    )(
        lower,
        upper,
        edge,
        prior_edge,
        coef_edge,
        sample,
        depth_hot,
        column,
        list_hot,
        spectra,
        table,
    )


def assemble_kernel(p_inner_ref, q_inner_ref, final_ref, p_out_ref, q_out_ref):
    width = p_out_ref.shape[1] * TILE
    for field, (inner, out) in enumerate(((p_inner_ref, p_out_ref), (q_inner_ref, q_out_ref))):
        rows = ShotRows(out)
        for k in range(STEPS):
            rows[k] = final_ref[0, field, k]
            rows[width - 1 - k] = final_ref[1, field, k]

        @pl.loop(STEPS, width - STEPS, unroll=4)
        def _(x):
            rows[x] = inner[x - STEPS]


def assemble(p_inner, q_inner, final):
    inner, shots, depth = p_inner.shape
    across, along = (inner + 2 * STEPS) // TILE, depth // LANES
    shape = jax.ShapeDtypeStruct((shots, across, along, TILE, LANES), jnp.float32)
    vmem = pl.BlockSpec(memory_space=pltpu.VMEM)
    return pl.pallas_call(
        assemble_kernel,
        in_specs=[vmem] * 3,
        out_specs=[vmem] * 2,
        out_shape=[shape, shape],
        compiler_params=compiler_params(16),
        cost_estimate=pl.CostEstimate(flops=8 * MIB, bytes_accessed=4 * MIB, transcendentals=0),
        name="assemble",
    )(p_inner, q_inner, final)


def tiles_kernel(received_ref, counts_ref, out_ref, *, features):
    groups = received_ref.shape[0]
    slots, patch = out_ref.shape[2], out_ref.shape[3]
    half = patch // 2
    row = lax.broadcasted_iota(jnp.int32, (half, patch), 0)
    lane = lax.broadcasted_iota(jnp.int32, (half, patch), 1)
    live = counts_ref[0, 0]
    total = received_ref[0]
    for g in range(1, groups):
        total = total + received_ref[g]
    for s in range(slots):
        scale = jnp.where(s < live, 1.0 / features, 0.0)
        packed = total[s * half : (s + 1) * half] * scale
        diagonal = total[slots * half + s : slots * half + s + 1] * scale
        turned = jnp.transpose(jnp.concatenate([packed, packed], 0))
        flipped = turned[:half]
        corner = turned[half:]
        out_ref[0, 0, s, pl.ds(0, half), :] = jnp.where(
            (lane < half) & (row > lane), flipped, packed
        )
        last = jnp.where(row > lane, packed, jnp.where(row == lane, diagonal, flipped))
        out_ref[0, 0, s, pl.ds(half, half), :] = jnp.where(
            lane < half, corner, pltpu.roll(last, half, 1)
        )


def tiles(received, patch_counts, slots, features):
    patch = received.shape[2]
    return pl.pallas_call(
        functools.partial(tiles_kernel, features=features),
        in_specs=[
            pl.BlockSpec(memory_space=pltpu.VMEM),
            pl.BlockSpec(memory_space=pltpu.SMEM),
        ],
        out_specs=pl.BlockSpec(memory_space=pltpu.VMEM),
        out_shape=jax.ShapeDtypeStruct((1, 1, slots, patch, patch), jnp.float32),
        compiler_params=compiler_params(16),
        name="tiles",
    )(received, patch_counts)


def shards(
    pressure,
    auxiliary,
    pressure_prior,
    auxiliary_prior,
    courant_sq,
    thomsen_epsilon,
    thomsen_delta,
    tilt_angle,
    frequencies,
    spectra,
    target_cells,
    patch_lists,
    patch_counts,
):
    shots, width, depth = pressure.shape
    _, owners, slots, patch = patch_lists.shape
    fields = [tiled(item) for item in (pressure, auxiliary, pressure_prior, auxiliary_prior)]
    params = (courant_sq, thomsen_epsilon, thomsen_delta, tilt_angle)
    parts, targets = spectra.shape[1:]

    first_rows, last_rows = outer_rows(fields, params)
    bricks = lax.axis_size("brick")
    upward = [(i, i + 1) for i in range(bricks - 1)]
    downward = [(i + 1, i) for i in range(bricks - 1)]
    lower = lax.ppermute(last_rows, "brick", upward)
    upper = lax.ppermute(first_rows, "brick", downward)

    moments = jnp.arange(1, STEPS + 1, dtype=jnp.float32)
    angle = frequencies[None, :] * moments[:, None]
    table = jnp.concatenate([jnp.cos(angle), -jnp.sin(angle)], 1)
    table = jnp.broadcast_to(table[:, :, None], (STEPS, parts, 128))

    edge, prior_edge, coef_edge, p_inner, q_inner, sample, depth_hot, column, list_hot = interior(
        fields, params, target_cells, patch_lists
    )
    spectra_out, packed, final = finish(
        lower,
        upper,
        (edge, prior_edge, coef_edge, sample, depth_hot, column, list_hot),
        spectra.reshape(shots * parts, targets),
        table,
        width,
        owners,
        slots,
        patch,
    )
    received = lax.all_to_all(packed, "shot", split_axis=0, concat_axis=0, tiled=True)
    pressure_out, auxiliary_out = [untiled(item) for item in assemble(p_inner, q_inner, final)]
    gram_tiles = tiles(received, patch_counts, slots, shots * parts * owners)
    return (pressure_out, auxiliary_out, spectra_out.reshape(spectra.shape), gram_tiles)


def solution(mesh):
    return jax.shard_map(
        shards,
        mesh=mesh,
        in_specs=(
            P("shot", "brick", None),
            P("shot", "brick", None),
            P("shot", "brick", None),
            P("shot", "brick", None),
            P("brick", None),
            P("brick", None),
            P("brick", None),
            P("brick", None),
            P(),
            P("shot", None, "brick"),
            P("brick"),
            P("brick", None, None, None),
            P("brick", "shot"),
        ),
        out_specs=(
            P("shot", "brick", None),
            P("shot", "brick", None),
            P("shot", None, "brick"),
            P("brick", "shot", None, None, None),
        ),
        check_vma=False,
    )
```

time: 96.9 us -> 39.4 us (0.41)
  local copies, waits for them, and re-layouts: 45.9 us -> 7.64 us
  other arithmetic: 17.9 us -> 0.19 us
  waiting for transfers between devices: 19.6 us -> 5.28 us
  Pallas kernels: 0 us -> 13.8 us
  matrix products: 1.13 us -> 0 us
    gather x5 -> x0, local copies, waits for them, and re-layouts: 22.5 us -> none  [the longest x4 17.7 us: shards(): jnp.take(interior.reshape(shots_here, width_x * depth), target_cells, axi...]
    slice x9 -> x0, local copies, waits for them, and re-layouts: 16.1 us -> none  [the longest x4 10.3 us: shards(): interior = current[0][:, margin:margin + width_x]]
    pallas_call x0 -> x5, Pallas kernels: none -> 13.8 us  [the longest x1 6.99 us: interior(): pl.pallas_call(interior_kernel, in_specs=[vmem] * 10, out_specs=[vmem] *...]
    add x9 -> x1, other arithmetic: 11.1 us -> 0.01 us  [shards(): moments = jnp.arange(1, STEPS + 1, dtype=jnp.float32)]
    ppermute x2, waiting for transfers between devices: 8.66 us -> 0.01 us  [the longest x1 0.01 us: shards(): lower = lax.ppermute(last_rows, 'brick', upward)]
    unnamed x37 -> x41, local copies, waits for them, and re-layouts: 0.93 us -> 7.57 us
    all_to_all x1, waiting for transfers between devices: 11 us -> 5.28 us  [shards(): lax.all_to_all(packed, 'shot', split_axis=0, concat_axis=0, tiled=True)]
    add x1 -> x0, local copies, waits for them, and re-layouts: 4.68 us -> none  [leapfrog(): 2.0 * pressure - former[0]]
  transfers between devices with their start and end apart: 3 -> 3, of which waited for: 3 -> 1; matrix products, arithmetic and copies ran while one was open for 3% -> 1% of each run, Pallas kernels for 0% -> 22%
where the time goes in v1:
time: 39.4 us; the launch traced here: 38.7 us
  Pallas kernels  13.8 us (35%)
  starting transfers between devices  10.3 us (26%)
  local copies, waits for them, and re-layouts  7.64 us (19%)
  waiting for transfers between devices  5.28 us (13%)
  between operations  1.52 us (4%)
    unnamed x41, local copies, waits for them, and re-layouts  7.57 us
    pallas_call x1, Pallas kernels, interior(): pl.pallas_call(interior_kernel, in_specs=[vmem] * 10, out_specs=[vmem] *...  6.99 us
    all_to_all x1, waiting for transfers between devices, shards(): lax.all_to_all(packed, 'shot', split_axis=0, concat_axis=0, tiled=True)  5.28 us
    pallas_call x1, Pallas kernels, finish(): pl.pallas_call(functools.partial(finish_kernel, width=width), in_specs=[v...  3.87 us
    ppermute x1, starting transfers between devices, shards(): lower = lax.ppermute(last_rows, 'brick', upward)  3.53 us
    all_to_all x1, starting transfers between devices, shards(): lax.all_to_all(packed, 'shot', split_axis=0, concat_axis=0, tiled=True)  3.46 us
    ppermute x1, starting transfers between devices, shards(): upper = lax.ppermute(first_rows, 'brick', downward)  3.34 us
    pallas_call x1, Pallas kernels, assemble(): pl.pallas_call(assemble_kernel, in_specs=[vmem] * 3, out_specs=[vmem] * 2...  1.66 us
  transfers between devices with their start and end apart: 3, of which 1 were waited for; matrix products, arithmetic and copies ran while one was open for 1% of the time, Pallas kernels for 22%

profile of v1, /device:TPU:16, one launch (start us, length us, event | category | flops | bytes accessed | tf_op | source)
XLA Modules:
  0.0 38.7 jit_solution(4967224531113545326)
XLA Ops:
  0.6 0.0 copy-start
  0.6 1.0 %copy-done = f32[8,32,512]{2,1,0:T(8,128)S(1)} copy-done((f32[8,32,512]{2,1,0:T(8,128)S(1)}, f32[8,32,512]{2,1,0:T(8,128)}, u32[]{:S(2)}) %copy-start) | copy-done | bytes 524312
  1.7 1.0 %copy-done.2 = f32[8,32,512]{2,1,0:T(8,128)S(1)} copy-done((f32[8,32,512]{2,1,0:T(8,128)S(1)}, f32[8,32,512]{2,1,0:T(8,128)}, u32[]{:S(2)}) %copy-start.2) | copy-done | bytes 524312
  2.7 0.0 copy-start.4
  2.7 1.0 %copy-done.4 = f32[8,32,512]{2,1,0:T(8,128)S(1)} copy-done((f32[8,32,512]{2,1,0:T(8,128)S(1)}, f32[8,32,512]{2,1,0:T(8,128)}, u32[]{:S(2)}) %copy-start.4) | copy-done | bytes 524312
  3.8 0.0 copy-start.6
  3.8 1.0 %copy-done.6 = f32[8,32,512]{2,1,0:T(8,128)S(1)} copy-done((f32[8,32,512]{2,1,0:T(8,128)S(1)}, f32[8,32,512]{2,1,0:T(8,128)}, u32[]{:S(2)}) %copy-start.6) | copy-done | bytes 524312
  4.8 0.0 copy-start.8
  4.8 0.8 %copy-done.8 = f32[32,512]{1,0:T(8,128)S(1)} copy-done((f32[32,512]{1,0:T(8,128)S(1)}, f32[32,512]{1,0:T(8,128)}, u32[]{:S(2)}) %copy-start.8) | copy-done | bytes 65560
  5.6 0.0 copy-start.10
  5.6 0.8 %copy-done.10 = f32[32,512]{1,0:T(8,128)S(1)} copy-done((f32[32,512]{1,0:T(8,128)S(1)}, f32[32,512]{1,0:T(8,128)}, u32[]{:S(2)}) %copy-start.10) | copy-done | bytes 65560
  6.5 0.0 copy-start.12
  6.5 0.8 %copy-done.12 = f32[32,512]{1,0:T(8,128)S(1)} copy-done((f32[32,512]{1,0:T(8,128)S(1)}, f32[32,512]{1,0:T(8,128)}, u32[]{:S(2)}) %copy-start.12) | copy-done | bytes 65560
  7.3 0.8 %copy-done.14 = f32[32,512]{1,0:T(8,128)S(1)} copy-done((f32[32,512]{1,0:T(8,128)S(1)}, f32[32,512]{1,0:T(8,128)}, u32[]{:S(2)}) %copy-start.14) | copy-done | bytes 65560
  8.2 0.0 copy-start.5
  8.2 0.0 copy-start.7
  8.2 0.0 copy-start.9
  8.2 0.0 copy-start.11
  8.2 0.0 copy-start.13
  8.2 0.0 copy-start.15
  8.2 0.0 copy-start.17
  8.2 0.4 %outer_rows.1 = (bf16[160,512]{1,0:T(8,128)(2,1)S(1)}, bf16[160,512]{1,0:T(8,128)(2,1)S(1)}) custom-call(f32[8,4,4,8,128]{4,3,2,1,0:T(8,128)S(1)} %bitcast.21, f32[8,4,4,8,128]{4,3,2,1,0:T(8,128)S(1)} %bitcast.24, f32[8,4,4,8,128]{4,3,2,1,0:T(8,128)S(1)} %bitcast.27, f32[8,4,4,8,128]{4,3,2,1,0:T(8,128)S(1)} %bitcast.30, f32[8,4,4,8,128]{4,3,2,1,0:T(8,128)S(1)} %bitcast.22, ...), custom_call_target="tpu_custom_call" | custom-call | tf_op jit(solution)/shard_map/outer_rows/pallas_call | solution.py:187
  8.7 0.0 copy-start.16
  8.7 3.5 %collective-permute-start = (bf16[160,512]{1,0:T(8,128)(2,1)S(1)}, bf16[160,512]{1,0:T(8,128)(2,1)S(1)}, u32[]{:S(2)}, u32[]{:S(2)}) collective-permute-start(bf16[160,512]{1,0:T(8,128)(2,1)S(1)} %get-tuple-element.22), channel_id=1, source_target_pairs={{0,1},{1,2},{2,3},{3,4},{4,5},{5,6},{6,7},{8,9},{9,10},{10,11},{11... | collective-permute-start | bytes 491528 | tf_op jit(solution)/shard_map/ppermute | solution.py:639
  12.2 3.3 %collective-permute-start.1 = (bf16[160,512]{1,0:T(8,128)(2,1)S(1)}, bf16[160,512]{1,0:T(8,128)(2,1)S(1)}, u32[]{:S(2)}, u32[]{:S(2)}) collective-permute-start(bf16[160,512]{1,0:T(8,128)(2,1)S(1)} %get-tuple-element.23), channel_id=1, source_target_pairs={{1,0},{2,1},{3,2},{4,3},{5,4},{6,5},{7,6},{9,8},{10,9},{11,10},{12... | collective-permute-start | bytes 491528 | tf_op jit(solution)/shard_map/ppermute | solution.py:640
  15.6 0.0 copy-done.19
  15.6 0.1 multiply_cosine_fusion
  15.7 0.0 copy-done.18
  15.7 0.0 copy-done.1
  15.7 0.0 copy-done.3
  15.7 0.0 copy-done.5
  15.7 0.0 copy-done.7
  15.7 0.0 copy-done.9
  15.8 0.0 copy-done.11
  15.8 0.0 copy-done.13
  15.8 0.0 copy-done.15
  15.8 0.0 copy-done.17
  15.8 7.0 %interior.1 = (f32[2,2,4,2,8,512]{5,4,3,2,1,0:T(8,128)S(1)}, f32[2,2,8,512]{3,2,1,0:T(8,128)S(1)}, f32[2,5,8,512]{3,2,1,0:T(8,128)S(1)}, f32[24,8,512]{2,1,0:T(8...) custom-call(f32[8,4,4,8,128]{4,3,2,1,0:T(8,128)S(1)} %bitcast.23, ...), custom_call_target="tpu_custom_call" | custom-call | flops 104857600 | bytes 8388608 | tf_op jit(solution)/shard_map/interior/pallas_call | solution.py:342
  22.8 0.1 pad_maximum_fusion
  22.9 0.0 collective-permute-done.lower_ref
  22.9 0.0 collective-permute-done.1.upper_ref
  22.9 0.1 broadcast_in_dim.2.table_ref
  22.9 0.0 copy-done.16
  23.0 3.9 %finish.1 = (f32[256,512]{1,0:T(8,128)}, f32[4,200,128]{2,1,0:T(8,128)}, f32[2,2,4,8,512]{4,3,2,1,0:T(8,128)S(1)}) custom-call(bf16[160,512]{1,0:T(8,128)(2,1)S(1)} %collective-permute-done.lower_ref, bf16[160,512]{1,0:T(8,128)(2,1)S(1)} %collective-permute-done.1.upper_ref, f32[2,2,4,2,8,512]{5,4,3,2,1,0:T(8,128)S(1)} %get-tuple-element.24.edge_ref, ...), custom_call_target="tpu_custom_call" | custom-call | tf_op jit(solution)/shard_map/finish/pallas_call | solution.py:516
  26.8 3.5 %all-to-all-start = ((f32[4,200,128]{2,1,0:T(8,128)}), f32[4,200,128]{2,1,0:T(8,128)S(1)}, u32[]{:S(2)}, u32[]{:S(2)}) async-start(f32[4,200,128]{2,1,0:T(8,128)} %get-tuple-element.35), calls=%async_computation | async-start | bytes 819200 | tf_op jit(solution)/shard_map/all_to_all | solution.py:661
  30.9 1.7 %assemble.1 = (f32[8,4,4,8,128]{4,3,2,1,0:T(8,128)}, f32[8,4,4,8,128]{4,3,2,1,0:T(8,128)}) custom-call(f32[24,8,512]{2,1,0:T(8,128)S(1)} %get-tuple-element.20.p_inner_ref, f32[24,8,512]{2,1,0:T(8,128)S(1)} %get-tuple-element.21.q_inner_ref, f32[2,2,4,8,512]{4,3,2,1,0:T(8,128)S(1)} %get-tuple-element.31.final_ref), custom_call_target="tpu_custom_call" | custom-call | flops 8388608 | bytes 4194304 | tf_op jit(solution)/shard_map/assemble/pallas_call | solution.py:562
  32.6 5.3 %all-to-all-done.received_ref = f32[4,200,128]{2,1,0:T(8,128)S(1)} async-done(((f32[4,200,128]{2,1,0:T(8,128)}), f32[4,200,128]{2,1,0:T(8,128)S(1)}, u32[]{:S(2)}, u32[]{:S(2)}) %all-to-all-start) | async-done | bytes 409632 | tf_op jit(solution)/shard_map/all_to_all | solution.py:661
  37.9 0.9 %tiles.1 = f32[1,1,3,128,128]{4,3,2,1,0:T(8,128)} custom-call(f32[4,200,128]{2,1,0:T(8,128)S(1)} %all-to-all-done.received_ref, s32[1,1]{1,0:T(1,128)S(6)} %copy.18.counts_ref), custom_call_target="tpu_custom_call" | custom-call | tf_op jit(solution)/shard_map/tiles/pallas_call | solution.py:601
  (8 shorter events, 0.0 us)
Async XLA Ops:
  0.6 1.0 %copy-start = (f32[8,32,512]{2,1,0:T(8,128)S(1)}, f32[8,32,512]{2,1,0:T(8,128)}, u32[]{:S(2)}) copy-start(f32[8,32,512]{2,1,0:T(8,128)} %param.13) | copy-start | bytes 1572868
  1.7 1.0 %copy-start.2 = (f32[8,32,512]{2,1,0:T(8,128)S(1)}, f32[8,32,512]{2,1,0:T(8,128)}, u32[]{:S(2)}) copy-start(f32[8,32,512]{2,1,0:T(8,128)} %param.14) | copy-start | bytes 1572868
  2.7 1.0 %copy-start.4 = (f32[8,32,512]{2,1,0:T(8,128)S(1)}, f32[8,32,512]{2,1,0:T(8,128)}, u32[]{:S(2)}) copy-start(f32[8,32,512]{2,1,0:T(8,128)} %param.15) | copy-start | bytes 1572868
  3.8 1.0 %copy-start.6 = (f32[8,32,512]{2,1,0:T(8,128)S(1)}, f32[8,32,512]{2,1,0:T(8,128)}, u32[]{:S(2)}) copy-start(f32[8,32,512]{2,1,0:T(8,128)} %param.16) | copy-start | bytes 1572868
  4.8 0.8 %copy-start.8 = (f32[32,512]{1,0:T(8,128)S(1)}, f32[32,512]{1,0:T(8,128)}, u32[]{:S(2)}) copy-start(f32[32,512]{1,0:T(8,128)} %refs_12_.1) | copy-start | bytes 196612
  5.6 0.8 %copy-start.10 = (f32[32,512]{1,0:T(8,128)S(1)}, f32[32,512]{1,0:T(8,128)}, u32[]{:S(2)}) copy-start(f32[32,512]{1,0:T(8,128)} %refs_13_.1) | copy-start | bytes 196612
  6.5 0.8 %copy-start.12 = (f32[32,512]{1,0:T(8,128)S(1)}, f32[32,512]{1,0:T(8,128)}, u32[]{:S(2)}) copy-start(f32[32,512]{1,0:T(8,128)} %refs_14_.1) | copy-start | bytes 196612
  7.3 0.8 %copy-start.14 = (f32[32,512]{1,0:T(8,128)S(1)}, f32[32,512]{1,0:T(8,128)}, u32[]{:S(2)}) copy-start(f32[32,512]{1,0:T(8,128)} %refs_15_.1) | copy-start | bytes 196612
  8.2 7.4 %copy-start.19 = (f32[16]{0:T(128)S(1)}, f32[16]{0:T(128)}, u32[]{:S(2)}) copy-start(f32[16]{0:T(128)} %param.21) | copy-start | bytes 196
  8.2 7.5 %copy-start.18 = (s32[1,4,3,128]{3,1,2,0:T(4,128)S(1)}, s32[1,4,3,128]{3,1,2,0:T(4,128)}, u32[]{:S(2)}) copy-start(s32[1,4,3,128]{3,1,2,0:T(4,128)} %param.24) | copy-start | bytes 18436
  8.2 7.5 %copy-start.1 = (f32[8,32,512]{2,1,0:T(8,128)S(1)}, f32[8,32,512]{2,1,0:T(8,128)}, u32[]{:S(2)}) copy-start(f32[8,32,512]{2,1,0:T(8,128)} %param.13) | copy-start | bytes 1572868
  8.2 7.5 %copy-start.3 = (f32[8,32,512]{2,1,0:T(8,128)S(1)}, f32[8,32,512]{2,1,0:T(8,128)}, u32[]{:S(2)}) copy-start(f32[8,32,512]{2,1,0:T(8,128)} %param.14) | copy-start | bytes 1572868
  8.2 7.6 %copy-start.5 = (f32[8,32,512]{2,1,0:T(8,128)S(1)}, f32[8,32,512]{2,1,0:T(8,128)}, u32[]{:S(2)}) copy-start(f32[8,32,512]{2,1,0:T(8,128)} %param.15) | copy-start | bytes 1572868
  8.2 7.6 %copy-start.7 = (f32[8,32,512]{2,1,0:T(8,128)S(1)}, f32[8,32,512]{2,1,0:T(8,128)}, u32[]{:S(2)}) copy-start(f32[8,32,512]{2,1,0:T(8,128)} %param.16) | copy-start | bytes 1572868
  8.2 7.6 %copy-start.9 = (f32[32,512]{1,0:T(8,128)S(1)}, f32[32,512]{1,0:T(8,128)}, u32[]{:S(2)}) copy-start(f32[32,512]{1,0:T(8,128)} %refs_12_.1) | copy-start | bytes 196612
  8.2 7.6 %copy-start.11 = (f32[32,512]{1,0:T(8,128)S(1)}, f32[32,512]{1,0:T(8,128)}, u32[]{:S(2)}) copy-start(f32[32,512]{1,0:T(8,128)} %refs_13_.1) | copy-start | bytes 196612
  8.2 7.6 %copy-start.13 = (f32[32,512]{1,0:T(8,128)S(1)}, f32[32,512]{1,0:T(8,128)}, u32[]{:S(2)}) copy-start(f32[32,512]{1,0:T(8,128)} %refs_14_.1) | copy-start | bytes 196612
  8.2 7.6 %copy-start.15 = (f32[32,512]{1,0:T(8,128)S(1)}, f32[32,512]{1,0:T(8,128)}, u32[]{:S(2)}) copy-start(f32[32,512]{1,0:T(8,128)} %refs_15_.1) | copy-start | bytes 196612
  8.2 7.6 %copy-start.17 = (s32[512]{0:T(512)S(1)}, s32[512]{0:T(512)}, u32[]{:S(2)}) copy-start(s32[512]{0:T(512)} %param.23) | copy-start | bytes 6148
  8.7 14.3 %copy-start.16 = (f32[8,32,512]{2,1,0:T(8,128)S(1)}, f32[8,32,512]{2,1,0:T(8,128)}, u32[]{:S(2)}) copy-start(f32[8,32,512]{2,1,0:T(8,128)} %param.22) | copy-start | bytes 1572868
  8.7 14.2 %collective-permute-start = (bf16[160,512]{1,0:T(8,128)(2,1)S(1)}, bf16[160,512]{1,0:T(8,128)(2,1)S(1)}, u32[]{:S(2)}, u32[]{:S(2)}) collective-permute-start(bf16[160,512]{1,0:T(8,128)(2,1)S(1)} %get-tuple-element.22), channel_id=1, source_target_pairs={{0,1},{1,2},{2,3},{3,4},{4,5},{5,6},{6,7},{8,9},{9,10},{10,11},{11... | collective-permute-start | bytes 491528 | tf_op jit(solution)/shard_map/ppermute | solution.py:639
  12.2 10.7 %collective-permute-start.1 = (bf16[160,512]{1,0:T(8,128)(2,1)S(1)}, bf16[160,512]{1,0:T(8,128)(2,1)S(1)}, u32[]{:S(2)}, u32[]{:S(2)}) collective-permute-start(bf16[160,512]{1,0:T(8,128)(2,1)S(1)} %get-tuple-element.23), channel_id=1, source_target_pairs={{1,0},{2,1},{3,2},{4,3},{5,4},{6,5},{7,6},{9,8},{10,9},{11,10},{12... | collective-permute-start | bytes 491528 | tf_op jit(solution)/shard_map/ppermute | solution.py:640
  26.8 11.1 %all-to-all-start = ((f32[4,200,128]{2,1,0:T(8,128)}), f32[4,200,128]{2,1,0:T(8,128)S(1)}, u32[]{:S(2)}, u32[]{:S(2)}) async-start(f32[4,200,128]{2,1,0:T(8,128)} %get-tuple-element.35), calls=%async_computation | async-start | bytes 819200 | tf_op jit(solution)/shard_map/all_to_all | solution.py:661

commit v2 on v1

--- a/solution.py
+++ b/solution.py
@@ -127,11 +127,32 @@
 
 
 def outer_kernel(*refs):
-    fields, params, outs = refs[:8], refs[8:16], refs[16:]
-    shots, tile = fields[0].shape[0], fields[0].shape[3]
-    depth = params[0].shape[1]
+    sources, outs, (field_ref, param_ref, field_sem, param_sem) = refs[:8], refs[8:10], refs[10:]
+    shots, across, along, tile, lanes = sources[0].shape
+    depth = along * lanes
+    copies = []
     for side in range(2):
-        views = [ShotRows(ref) for ref in fields[4 * side : 4 * side + 4]]
+        place = side * (across - 1)
+        for i in range(4):
+            copies.append(
+                pltpu.make_async_copy(
+                    sources[i].at[:, pl.ds(place, 1)], field_ref.at[side, i], field_sem.at[side, i]
+                )
+            )
+        for i in range(4):
+            copies.append(
+                pltpu.make_async_copy(
+                    sources[4 + i].at[pl.ds(place * tile, tile)],
+                    param_ref.at[side, i],
+                    param_sem.at[side, i],
+                )
+            )
+    for copy in copies:
+        copy.start()
+    for side in range(2):
+        for copy in copies[8 * side : 8 * side + 8]:
+            copy.wait()
+        views = [ShotRows(field_ref.at[side, i]) for i in range(4)]
         out = outs[side]
 
         def row(field, distance):
@@ -152,7 +173,7 @@
             put(near, near - near.astype(jnp.bfloat16).astype(jnp.float32))
         for first, second in far_items():
             put(row(*first), row(*second))
-        terms = tilt_coefficients(*[ref[...] for ref in params[4 * side : 4 * side + 4]])
+        terms = tilt_coefficients(*[param_ref[side, i] for i in range(4)])
         rows = []
         for term in terms:
             for distance in range(STEPS - 1):
@@ -175,24 +196,22 @@
 def outer_rows(fields, params):
     shots, across, along, tile, lanes = fields[0].shape
     depth = along * lanes
-    last = across - 1
-    field_specs, param_specs = [], []
-    for place in (0, last):
-        field_specs += [
-            pl.BlockSpec((shots, 1, along, tile, lanes), lambda i, place=place: (0, place, 0, 0, 0))
-        ] * 4
-        param_specs += [pl.BlockSpec((tile, depth), lambda i, place=place: (place, 0))] * 4
     rows = 2 * shots * (4 + len(far_items()) + 1)
     shape = jax.ShapeDtypeStruct((rows, depth), jnp.bfloat16)
     return pl.pallas_call(
         outer_kernel,
-        grid=(1,),
-        in_specs=field_specs + param_specs,
-        out_specs=[pl.BlockSpec((rows, depth), lambda i: (0, 0))] * 2,
+        in_specs=[pl.BlockSpec(memory_space=pltpu.HBM)] * 8,
+        out_specs=[pl.BlockSpec(memory_space=pltpu.VMEM)] * 2,
         out_shape=[shape, shape],
-        compiler_params=compiler_params(16),
+        scratch_shapes=[
+            pltpu.VMEM((2, 4, shots, 1, along, tile, lanes), jnp.float32),
+            pltpu.VMEM((2, 4, tile, depth), jnp.float32),
+            pltpu.SemaphoreType.DMA((2, 4)),
+            pltpu.SemaphoreType.DMA((2, 4)),
+        ],
+        compiler_params=compiler_params(60),
         name="outer_rows",
-    )(*fields, *fields, *params, *params)
+    )(*fields, *params)
 
 
 def sample_rows(values, one_hot):

time: 39.4 us -> 33.3 us (0.85)
  local copies, waits for them, and re-layouts: 7.64 us -> 0.13 us
  Pallas kernels: 13.8 us -> 15.6 us
    unnamed x41 -> x25, local copies, waits for them, and re-layouts: 7.57 us -> 0.06 us
    pallas_call x1, Pallas kernels: 0.4 us -> 2.44 us  [outer_rows(): pl.pallas_call(outer_kernel, in_specs=[pl.BlockSpec(memory_space=pltpu.HB...]
  transfers between devices with their start and end apart: 3 -> 3, of which waited for: 1 -> 1; matrix products, arithmetic and copies ran while one was open for 1% -> 1% of each run, Pallas kernels for 22% -> 26%
where the time goes in v2:
time: 33.3 us; the launch traced here: 33 us
  Pallas kernels  15.6 us (47%)
  starting transfers between devices  10.3 us (31%)
  waiting for transfers between devices  5.28 us (16%)
  between operations  1.53 us (5%)
    pallas_call x1, Pallas kernels, interior(): pl.pallas_call(interior_kernel, in_specs=[vmem] * 10, out_specs=[vmem] *...  6.87 us
    all_to_all x1, waiting for transfers between devices, shards(): lax.all_to_all(packed, 'shot', split_axis=0, concat_axis=0, tiled=True)  5.28 us
    pallas_call x1, Pallas kernels, finish(): pl.pallas_call(functools.partial(finish_kernel, width=width), in_specs=[v...  3.72 us
    ppermute x1, starting transfers between devices, shards(): lower = lax.ppermute(last_rows, 'brick', upward)  3.53 us
    all_to_all x1, starting transfers between devices, shards(): lax.all_to_all(packed, 'shot', split_axis=0, concat_axis=0, tiled=True)  3.46 us
    ppermute x1, starting transfers between devices, shards(): upper = lax.ppermute(first_rows, 'brick', downward)  3.34 us
    pallas_call x1, Pallas kernels, outer_rows(): pl.pallas_call(outer_kernel, in_specs=[pl.BlockSpec(memory_space=pltpu.HB...  2.44 us
    pallas_call x1, Pallas kernels, assemble(): pl.pallas_call(assemble_kernel, in_specs=[vmem] * 3, out_specs=[vmem] * 2...  1.66 us
  transfers between devices with their start and end apart: 3, of which 1 were waited for; matrix products, arithmetic and copies ran while one was open for 1% of the time, Pallas kernels for 26%

profile of v2, /device:TPU:16, one launch (start us, length us, event | category | flops | bytes accessed | tf_op | source)
XLA Modules:
  0.0 33.0 jit_solution(4441980514699813702)
XLA Ops:
  0.6 0.0 copy-start
  0.6 0.0 copy-start.1
  0.7 0.0 copy-start.2
  0.7 0.0 copy-start.3
  0.7 0.0 copy-start.5
  0.7 0.0 copy-start.6
  0.7 0.0 copy-start.7
  0.7 0.0 copy-start.8
  0.7 0.0 copy-start.11
  0.7 0.0 copy-start.10
  0.7 0.0 copy-start.9
  0.7 2.4 %outer_rows.1 = (bf16[160,512]{1,0:T(8,128)(2,1)}, bf16[160,512]{1,0:T(8,128)(2,1)}) custom-call(f32[8,4,4,8,128]{4,3,2,1,0:T(8,128)} %bitcast.21, f32[8,4,4,8,128]{4,3,2,1,0:T(8,128)} %bitcast.23, f32[8,4,4,8,128]{4,3,2,1,0:T(8,128)} %bitcast.25, f32[8,4,4,8,128]{4,3,2,1,0:T(8,128)} %bitcast.27, f32[32,512]{1,0:T(8,128)} %refs_4_.1, f32[32,512]{1,0:T(8,128)} %refs_5_.1, ...), custom_call_target="tpu_custom_call" | custom-call | tf_op jit(solution)/shard_map/outer_rows/pallas_call | solution.py:201
  3.2 0.0 copy-start.4
  3.2 3.5 %collective-permute-start = (bf16[160,512]{1,0:T(8,128)(2,1)}, bf16[160,512]{1,0:T(8,128)(2,1)S(1)}, u32[]{:S(2)}, u32[]{:S(2)}) collective-permute-start(bf16[160,512]{1,0:T(8,128)(2,1)} %get-tuple-element.22), channel_id=1, source_target_pairs={{0,1},{1,2},{2,3},{3,4},{4,5},{5,6},{6,7},{8,9},{9,10},{10,11},{11... | collective-permute-start | bytes 491528 | tf_op jit(solution)/shard_map/ppermute | solution.py:658
  6.7 3.3 %collective-permute-start.1 = (bf16[160,512]{1,0:T(8,128)(2,1)}, bf16[160,512]{1,0:T(8,128)(2,1)S(1)}, u32[]{:S(2)}, u32[]{:S(2)}) collective-permute-start(bf16[160,512]{1,0:T(8,128)(2,1)} %get-tuple-element.23), channel_id=1, source_target_pairs={{1,0},{2,1},{3,2},{4,3},{5,4},{6,5},{7,6},{9,8},{10,9},{11,10},{12... | collective-permute-start | bytes 491528 | tf_op jit(solution)/shard_map/ppermute | solution.py:659
  10.1 0.0 copy-done.11
  10.1 0.1 multiply_cosine_fusion
  10.2 0.0 copy-done.10
  10.2 0.0 copy-done
  10.3 0.0 copy-done.1
  10.3 0.0 copy-done.2
  10.3 0.0 copy-done.3
  10.3 0.0 copy-done.5
  10.3 0.0 copy-done.6
  10.3 0.0 copy-done.7
  10.3 0.0 copy-done.8
  10.3 0.0 copy-done.9
  10.3 6.9 %interior.1 = (f32[2,2,4,2,8,512]{5,4,3,2,1,0:T(8,128)S(1)}, f32[2,2,8,512]{3,2,1,0:T(8,128)S(1)}, f32[2,5,8,512]{3,2,1,0:T(8,128)S(1)}, f32[24,8,512]{2,1,0:T(8...) custom-call(f32[8,4,4,8,128]{4,3,2,1,0:T(8,128)S(1)} %bitcast.22, ...), custom_call_target="tpu_custom_call" | custom-call | flops 104857600 | bytes 8388608 | tf_op jit(solution)/shard_map/interior/pallas_call | solution.py:361
  17.2 0.1 pad_maximum_fusion
  17.3 0.0 collective-permute-done.lower_ref
  17.3 0.0 collective-permute-done.1.upper_ref
  17.3 0.1 broadcast_in_dim.2.table_ref
  17.4 0.0 copy-done.4
  17.4 3.7 %finish.1 = (f32[256,512]{1,0:T(8,128)}, f32[4,200,128]{2,1,0:T(8,128)}, f32[2,2,4,8,512]{4,3,2,1,0:T(8,128)S(1)}) custom-call(bf16[160,512]{1,0:T(8,128)(2,1)S(1)} %collective-permute-done.lower_ref, bf16[160,512]{1,0:T(8,128)(2,1)S(1)} %collective-permute-done.1.upper_ref, f32[2,2,4,2,8,512]{5,4,3,2,1,0:T(8,128)S(1)} %get-tuple-element.24.edge_ref, ...), custom_call_target="tpu_custom_call" | custom-call | tf_op jit(solution)/shard_map/finish/pallas_call | solution.py:535
  21.1 3.5 %all-to-all-start = ((f32[4,200,128]{2,1,0:T(8,128)}), f32[4,200,128]{2,1,0:T(8,128)S(1)}, u32[]{:S(2)}, u32[]{:S(2)}) async-start(f32[4,200,128]{2,1,0:T(8,128)} %get-tuple-element.35), calls=%async_computation | async-start | bytes 819200 | tf_op jit(solution)/shard_map/all_to_all | solution.py:680
  25.2 1.7 %assemble.1 = (f32[8,4,4,8,128]{4,3,2,1,0:T(8,128)}, f32[8,4,4,8,128]{4,3,2,1,0:T(8,128)}) custom-call(f32[24,8,512]{2,1,0:T(8,128)S(1)} %get-tuple-element.20.p_inner_ref, f32[24,8,512]{2,1,0:T(8,128)S(1)} %get-tuple-element.21.q_inner_ref, f32[2,2,4,8,512]{4,3,2,1,0:T(8,128)S(1)} %get-tuple-element.31.final_ref), custom_call_target="tpu_custom_call" | custom-call | flops 8388608 | bytes 4194304 | tf_op jit(solution)/shard_map/assemble/pallas_call | solution.py:581
  26.9 5.3 %all-to-all-done.received_ref = f32[4,200,128]{2,1,0:T(8,128)S(1)} async-done(((f32[4,200,128]{2,1,0:T(8,128)}), f32[4,200,128]{2,1,0:T(8,128)S(1)}, u32[]{:S(2)}, u32[]{:S(2)}) %all-to-all-start) | async-done | bytes 409632 | tf_op jit(solution)/shard_map/all_to_all | solution.py:680
  32.2 0.9 %tiles.1 = f32[1,1,3,128,128]{4,3,2,1,0:T(8,128)} custom-call(f32[4,200,128]{2,1,0:T(8,128)S(1)} %all-to-all-done.received_ref, s32[1,1]{1,0:T(1,128)S(6)} %copy.18.counts_ref), custom_call_target="tpu_custom_call" | custom-call | tf_op jit(solution)/shard_map/tiles/pallas_call | solution.py:620
  (2 shorter events, 0.0 us)
Async XLA Ops:
  0.6 9.6 %copy-start = (f32[8,32,512]{2,1,0:T(8,128)S(1)}, f32[8,32,512]{2,1,0:T(8,128)}, u32[]{:S(2)}) copy-start(f32[8,32,512]{2,1,0:T(8,128)} %param.13) | copy-start | bytes 1572868
  0.6 9.6 %copy-start.1 = (f32[8,32,512]{2,1,0:T(8,128)S(1)}, f32[8,32,512]{2,1,0:T(8,128)}, u32[]{:S(2)}) copy-start(f32[8,32,512]{2,1,0:T(8,128)} %param.14) | copy-start | bytes 1572868
  0.7 9.6 %copy-start.2 = (f32[8,32,512]{2,1,0:T(8,128)S(1)}, f32[8,32,512]{2,1,0:T(8,128)}, u32[]{:S(2)}) copy-start(f32[8,32,512]{2,1,0:T(8,128)} %param.15) | copy-start | bytes 1572868
  0.7 9.6 %copy-start.3 = (f32[8,32,512]{2,1,0:T(8,128)S(1)}, f32[8,32,512]{2,1,0:T(8,128)}, u32[]{:S(2)}) copy-start(f32[8,32,512]{2,1,0:T(8,128)} %param.16) | copy-start | bytes 1572868
  0.7 9.6 %copy-start.5 = (f32[32,512]{1,0:T(8,128)S(1)}, f32[32,512]{1,0:T(8,128)}, u32[]{:S(2)}) copy-start(f32[32,512]{1,0:T(8,128)} %refs_4_.1) | copy-start | bytes 196612
  0.7 9.6 %copy-start.6 = (f32[32,512]{1,0:T(8,128)S(1)}, f32[32,512]{1,0:T(8,128)}, u32[]{:S(2)}) copy-start(f32[32,512]{1,0:T(8,128)} %refs_5_.1) | copy-start | bytes 196612
  0.7 9.6 %copy-start.7 = (f32[32,512]{1,0:T(8,128)S(1)}, f32[32,512]{1,0:T(8,128)}, u32[]{:S(2)}) copy-start(f32[32,512]{1,0:T(8,128)} %refs_6_.1) | copy-start | bytes 196612
  0.7 9.6 %copy-start.8 = (f32[32,512]{1,0:T(8,128)S(1)}, f32[32,512]{1,0:T(8,128)}, u32[]{:S(2)}) copy-start(f32[32,512]{1,0:T(8,128)} %refs_7_.1) | copy-start | bytes 196612
  0.7 9.4 %copy-start.11 = (f32[16]{0:T(128)S(1)}, f32[16]{0:T(128)}, u32[]{:S(2)}) copy-start(f32[16]{0:T(128)} %param.21) | copy-start | bytes 196
  0.7 9.5 %copy-start.10 = (s32[1,4,3,128]{3,1,2,0:T(4,128)S(1)}, s32[1,4,3,128]{3,1,2,0:T(4,128)}, u32[]{:S(2)}) copy-start(s32[1,4,3,128]{3,1,2,0:T(4,128)} %param.24) | copy-start | bytes 18436
  0.7 9.6 %copy-start.9 = (s32[512]{0:T(512)S(1)}, s32[512]{0:T(512)}, u32[]{:S(2)}) copy-start(s32[512]{0:T(512)} %param.23) | copy-start | bytes 6148
  3.2 14.2 %copy-start.4 = (f32[8,32,512]{2,1,0:T(8,128)S(1)}, f32[8,32,512]{2,1,0:T(8,128)}, u32[]{:S(2)}) copy-start(f32[8,32,512]{2,1,0:T(8,128)} %param.22) | copy-start | bytes 1572868
  3.2 14.1 %collective-permute-start = (bf16[160,512]{1,0:T(8,128)(2,1)}, bf16[160,512]{1,0:T(8,128)(2,1)S(1)}, u32[]{:S(2)}, u32[]{:S(2)}) collective-permute-start(bf16[160,512]{1,0:T(8,128)(2,1)} %get-tuple-element.22), channel_id=1, source_target_pairs={{0,1},{1,2},{2,3},{3,4},{4,5},{5,6},{6,7},{8,9},{9,10},{10,11},{11... | collective-permute-start | bytes 491528 | tf_op jit(solution)/shard_map/ppermute | solution.py:658
  6.7 10.6 %collective-permute-start.1 = (bf16[160,512]{1,0:T(8,128)(2,1)}, bf16[160,512]{1,0:T(8,128)(2,1)S(1)}, u32[]{:S(2)}, u32[]{:S(2)}) collective-permute-start(bf16[160,512]{1,0:T(8,128)(2,1)} %get-tuple-element.23), channel_id=1, source_target_pairs={{1,0},{2,1},{3,2},{4,3},{5,4},{6,5},{7,6},{9,8},{10,9},{11,10},{12... | collective-permute-start | bytes 491528 | tf_op jit(solution)/shard_map/ppermute | solution.py:659
  21.1 11.1 %all-to-all-start = ((f32[4,200,128]{2,1,0:T(8,128)}), f32[4,200,128]{2,1,0:T(8,128)S(1)}, u32[]{:S(2)}, u32[]{:S(2)}) async-start(f32[4,200,128]{2,1,0:T(8,128)} %get-tuple-element.35), calls=%async_computation | async-start | bytes 819200 | tf_op jit(solution)/shard_map/all_to_all | solution.py:680

commit v3 on v2

--- a/solution.py
+++ b/solution.py
@@ -677,7 +677,7 @@
         slots,
         patch,
     )
-    received = lax.all_to_all(packed, "shot", split_axis=0, concat_axis=0, tiled=True)
+    received = lax.psum_scatter(packed, "shot", scatter_dimension=0, tiled=True)
     pressure_out, auxiliary_out = [untiled(item) for item in assemble(p_inner, q_inner, final)]
     gram_tiles = tiles(received, patch_counts, slots, shots * parts * owners)
     return (pressure_out, auxiliary_out, spectra_out.reshape(spectra.shape), gram_tiles)

time: 33.3 us -> 59.4 us (1.78)
  the two profiles are of different devices: /device:TPU:16 before, /device:TPU:0 now
where the time goes in v3:
time: 59.4 us; the launch traced here: 59.2 us
  waiting for transfers between devices  21.2 us (36%)
  Pallas kernels  15.5 us (26%)
  between operations  14.9 us (25%)
  starting transfers between devices  6.31 us (11%)
  local copies, waits for them, and re-layouts  1.03 us (2%)
    unnamed x2, waiting for transfers between devices  21.2 us
    pallas_call x1, Pallas kernels, interior(): pl.pallas_call(interior_kernel, in_specs=[vmem] * 10, out_specs=[vmem] *...  6.87 us
    ppermute x1, starting transfers between devices, shards(): lower = lax.ppermute(last_rows, 'brick', upward)  4.98 us
    pallas_call x1, Pallas kernels, finish(): pl.pallas_call(functools.partial(finish_kernel, width=width), in_specs=[v...  3.72 us
    pallas_call x1, Pallas kernels, outer_rows(): pl.pallas_call(outer_kernel, in_specs=[pl.BlockSpec(memory_space=pltpu.HB...  2.43 us
    pallas_call x1, Pallas kernels, assemble(): pl.pallas_call(assemble_kernel, in_specs=[vmem] * 3, out_specs=[vmem] * 2...  1.66 us
    ppermute x1, starting transfers between devices, shards(): upper = lax.ppermute(first_rows, 'brick', downward)  1.29 us
  transfers between devices with their start and end apart: 3, of which 1 were waited for; matrix products, arithmetic and copies ran while one was open for 0% of the time, Pallas kernels for 14%

profile of v3, /device:TPU:0, one launch (start us, length us, event | category | flops | bytes accessed | tf_op | source)
XLA Modules:
  0.0 59.2 jit_solution(1884688088481197986)
XLA Ops:
  7.2 0.0 copy-start
  7.2 0.0 copy-start.1
  7.2 0.0 copy-start.2
  7.2 0.0 copy-start.3
  7.2 0.0 copy-start.5
  7.2 0.0 copy-start.6
  7.2 0.0 copy-start.7
  7.2 0.0 copy-start.8
  7.2 0.0 copy-start.12
  7.3 0.0 copy-start.11
  7.3 0.0 copy-start.10
  7.3 0.0 reduce-scatter.4.cloned.1.call-start
  7.3 2.4 %outer_rows.1 = (bf16[160,512]{1,0:T(8,128)(2,1)}, bf16[160,512]{1,0:T(8,128)(2,1)}) custom-call(f32[8,4,4,8,128]{4,3,2,1,0:T(8,128)} %bitcast.22, f32[8,4,4,8,128]{4,3,2,1,0:T(8,128)} %bitcast.24, f32[8,4,4,8,128]{4,3,2,1,0:T(8,128)} %bitcast.26, f32[8,4,4,8,128]{4,3,2,1,0:T(8,128)} %bitcast.28, f32[32,512]{1,0:T(8,128)} %refs_4_.1, f32[32,512]{1,0:T(8,128)} %refs_5_.1, ...), custom_call_target="tpu_custom_call" | custom-call | tf_op jit(solution)/shard_map/outer_rows/pallas_call | solution.py:201
  9.8 0.0 copy-start.4
  9.8 5.0 %collective-permute-start = (bf16[160,512]{1,0:T(8,128)(2,1)}, bf16[160,512]{1,0:T(8,128)(2,1)S(1)}, u32[]{:S(2)}, u32[]{:S(2)}) collective-permute-start(bf16[160,512]{1,0:T(8,128)(2,1)} %get-tuple-element.22), channel_id=1, source_target_pairs={{0,1},{1,2},{2,3},{3,4},{4,5},{5,6},{6,7},{8,9},{9,10},{10,11},{11... | collective-permute-start | bytes 491528 | tf_op jit(solution)/shard_map/ppermute | solution.py:658
  14.8 1.3 %collective-permute-start.1 = (bf16[160,512]{1,0:T(8,128)(2,1)}, bf16[160,512]{1,0:T(8,128)(2,1)S(1)}, u32[]{:S(2)}, u32[]{:S(2)}) collective-permute-start(bf16[160,512]{1,0:T(8,128)(2,1)} %get-tuple-element.23), channel_id=1, source_target_pairs={{1,0},{2,1},{3,2},{4,3},{5,4},{6,5},{7,6},{9,8},{10,9},{11,10},{12... | collective-permute-start | bytes 491528 | tf_op jit(solution)/shard_map/ppermute | solution.py:659
  16.1 0.0 copy-done.12
  16.1 0.1 multiply_cosine_fusion
  16.2 0.0 copy-done.11
  16.2 0.0 copy-done
  16.2 0.0 copy-done.1
  16.2 0.0 copy-done.2
  16.3 0.0 copy-done.3
  16.3 0.0 copy-done.5
  16.3 0.0 copy-done.6
  16.3 0.0 copy-done.7
  16.3 0.0 copy-done.8
  16.3 0.0 copy-done.10
  16.3 6.9 %interior.1 = (f32[2,2,4,2,8,512]{5,4,3,2,1,0:T(8,128)S(1)}, f32[2,2,8,512]{3,2,1,0:T(8,128)S(1)}, f32[2,5,8,512]{3,2,1,0:T(8,128)S(1)}, f32[24,8,512]{2,1,0:T(8...) custom-call(f32[8,4,4,8,128]{4,3,2,1,0:T(8,128)S(1)} %bitcast.23, ...), custom_call_target="tpu_custom_call" | custom-call | flops 104857600 | bytes 8388608 | tf_op jit(solution)/shard_map/interior/pallas_call | solution.py:361
  23.2 0.1 pad_maximum_fusion
  23.3 0.0 collective-permute-done.lower_ref
  23.3 0.0 collective-permute-done.1.upper_ref
  23.3 0.1 broadcast_in_dim.2.table_ref
  23.3 0.0 copy-done.4
  23.4 3.7 %finish.1 = (f32[256,512]{1,0:T(8,128)}, f32[4,200,128]{2,1,0:T(8,128)}, f32[2,2,4,8,512]{4,3,2,1,0:T(8,128)S(1)}) custom-call(bf16[160,512]{1,0:T(8,128)(2,1)S(1)} %collective-permute-done.lower_ref, bf16[160,512]{1,0:T(8,128)(2,1)S(1)} %collective-permute-done.1.upper_ref, f32[2,2,4,2,8,512]{5,4,3,2,1,0:T(8,128)S(1)} %get-tuple-element.24.edge_ref, ...), custom_call_target="tpu_custom_call" | custom-call | tf_op jit(solution)/shard_map/finish/pallas_call | solution.py:535
  27.1 0.0 reduce-scatter.4.cloned.1.call-update
  27.8 1.7 %assemble.1 = (f32[8,4,4,8,128]{4,3,2,1,0:T(8,128)}, f32[8,4,4,8,128]{4,3,2,1,0:T(8,128)}) custom-call(f32[24,8,512]{2,1,0:T(8,128)S(1)} %get-tuple-element.20.p_inner_ref, f32[24,8,512]{2,1,0:T(8,128)S(1)} %get-tuple-element.21.q_inner_ref, f32[2,2,4,8,512]{4,3,2,1,0:T(8,128)S(1)} %get-tuple-element.31.final_ref), custom_call_target="tpu_custom_call" | custom-call | flops 8388608 | bytes 4194304 | tf_op jit(solution)/shard_map/assemble/pallas_call | solution.py:581
  29.4 21.2 %reduce-scatter.4.cloned.1.call-done.received_ref = f32[1,200,128]{2,1,0:T(8,128)} async-done(((f32[4,200,128]{2,1,0:T(8,128)}), f32[1,200,128]{2,1,0:T(8,128)}) %reduce-scatter.4.cloned.1.call-update) | async-done | bytes 102416
  50.6 0.0 copy-start.9
  50.6 0.9 %copy-done.9 = f32[1,200,128]{2,1,0:T(8,128)S(1)} copy-done((f32[1,200,128]{2,1,0:T(8,128)S(1)}, f32[1,200,128]{2,1,0:T(8,128)}, u32[]{:S(2)}) %copy-start.9) | copy-done | bytes 102424
  51.5 0.9 %tiles.1 = f32[1,1,3,128,128]{4,3,2,1,0:T(8,128)} custom-call(f32[1,200,128]{2,1,0:T(8,128)S(1)} %copy-done.9, s32[1,1]{1,0:T(1,128)S(6)} %copy.19.counts_ref), custom_call_target="tpu_custom_call" | custom-call | tf_op jit(solution)/shard_map/tiles/pallas_call | solution.py:620
  (2 shorter events, 0.0 us)
Async XLA Ops:
  7.2 9.1 %copy-start = (f32[8,32,512]{2,1,0:T(8,128)S(1)}, f32[8,32,512]{2,1,0:T(8,128)}, u32[]{:S(2)}) copy-start(f32[8,32,512]{2,1,0:T(8,128)} %param.13) | copy-start | bytes 1572868
  7.2 9.1 %copy-start.1 = (f32[8,32,512]{2,1,0:T(8,128)S(1)}, f32[8,32,512]{2,1,0:T(8,128)}, u32[]{:S(2)}) copy-start(f32[8,32,512]{2,1,0:T(8,128)} %param.14) | copy-start | bytes 1572868
  7.2 9.1 %copy-start.2 = (f32[8,32,512]{2,1,0:T(8,128)S(1)}, f32[8,32,512]{2,1,0:T(8,128)}, u32[]{:S(2)}) copy-start(f32[8,32,512]{2,1,0:T(8,128)} %param.15) | copy-start | bytes 1572868
  7.2 9.1 %copy-start.3 = (f32[8,32,512]{2,1,0:T(8,128)S(1)}, f32[8,32,512]{2,1,0:T(8,128)}, u32[]{:S(2)}) copy-start(f32[8,32,512]{2,1,0:T(8,128)} %param.16) | copy-start | bytes 1572868
  7.2 9.1 %copy-start.5 = (f32[32,512]{1,0:T(8,128)S(1)}, f32[32,512]{1,0:T(8,128)}, u32[]{:S(2)}) copy-start(f32[32,512]{1,0:T(8,128)} %refs_4_.1) | copy-start | bytes 196612
  7.2 9.1 %copy-start.6 = (f32[32,512]{1,0:T(8,128)S(1)}, f32[32,512]{1,0:T(8,128)}, u32[]{:S(2)}) copy-start(f32[32,512]{1,0:T(8,128)} %refs_5_.1) | copy-start | bytes 196612
  7.2 9.1 %copy-start.7 = (f32[32,512]{1,0:T(8,128)S(1)}, f32[32,512]{1,0:T(8,128)}, u32[]{:S(2)}) copy-start(f32[32,512]{1,0:T(8,128)} %refs_6_.1) | copy-start | bytes 196612
  7.2 9.1 %copy-start.8 = (f32[32,512]{1,0:T(8,128)S(1)}, f32[32,512]{1,0:T(8,128)}, u32[]{:S(2)}) copy-start(f32[32,512]{1,0:T(8,128)} %refs_7_.1) | copy-start | bytes 196612
  7.2 8.8 %copy-start.12 = (f32[16]{0:T(128)S(1)}, f32[16]{0:T(128)}, u32[]{:S(2)}) copy-start(f32[16]{0:T(128)} %param.21) | copy-start | bytes 196
  7.3 8.9 %copy-start.11 = (s32[1,4,3,128]{3,1,2,0:T(4,128)S(1)}, s32[1,4,3,128]{3,1,2,0:T(4,128)}, u32[]{:S(2)}) copy-start(s32[1,4,3,128]{3,1,2,0:T(4,128)} %param.24) | copy-start | bytes 18436
  7.3 9.0 %copy-start.10 = (s32[512]{0:T(512)S(1)}, s32[512]{0:T(512)}, u32[]{:S(2)}) copy-start(s32[512]{0:T(512)} %param.23) | copy-start | bytes 6148
  7.3 43.3 %reduce-scatter.4.cloned.1.call-start = ((), (), s32[]{:S(2)}) async-start(), calls=%async_computation.1 | async-start | bytes 512000
  9.8 13.6 %copy-start.4 = (f32[8,32,512]{2,1,0:T(8,128)S(1)}, f32[8,32,512]{2,1,0:T(8,128)}, u32[]{:S(2)}) copy-start(f32[8,32,512]{2,1,0:T(8,128)} %param.22) | copy-start | bytes 1572868
  9.8 13.5 %collective-permute-start = (bf16[160,512]{1,0:T(8,128)(2,1)}, bf16[160,512]{1,0:T(8,128)(2,1)S(1)}, u32[]{:S(2)}, u32[]{:S(2)}) collective-permute-start(bf16[160,512]{1,0:T(8,128)(2,1)} %get-tuple-element.22), channel_id=1, source_target_pairs={{0,1},{1,2},{2,3},{3,4},{4,5},{5,6},{6,7},{8,9},{9,10},{10,11},{11... | collective-permute-start | bytes 491528 | tf_op jit(solution)/shard_map/ppermute | solution.py:658
  14.8 8.5 %collective-permute-start.1 = (bf16[160,512]{1,0:T(8,128)(2,1)}, bf16[160,512]{1,0:T(8,128)(2,1)S(1)}, u32[]{:S(2)}, u32[]{:S(2)}) collective-permute-start(bf16[160,512]{1,0:T(8,128)(2,1)} %get-tuple-element.23), channel_id=1, source_target_pairs={{1,0},{2,1},{3,2},{4,3},{5,4},{6,5},{7,6},{9,8},{10,9},{11,10},{12... | collective-permute-start | bytes 491528 | tf_op jit(solution)/shard_map/ppermute | solution.py:659
  50.6 0.9 %copy-start.9 = (f32[1,200,128]{2,1,0:T(8,128)S(1)}, f32[1,200,128]{2,1,0:T(8,128)}, u32[]{:S(2)}) copy-start(f32[1,200,128]{2,1,0:T(8,128)} %reduce-scatter.4.cloned.1.call-done.received_ref) | copy-start | bytes 307204
Sparse Core Ops, SparseCore 0:
  27.2 23.3 reduce-scatter.3

commit v4 on v3

--- a/solution.py
+++ b/solution.py
@@ -214,6 +214,12 @@
     )(*fields, *params)
 
 
+def partner(me, k, count):
+    if count & (count - 1):
+        return (me + k) % count
+    return me ^ k
+
+
 def sample_rows(values, one_hot):
     high, low = split_bf16(values)
     return jnp.dot(jnp.concatenate([high, low], 1), one_hot, preferred_element_type=jnp.float32)
@@ -272,7 +278,11 @@
             ).astype(jnp.bfloat16)
 
     owners, slots, patch = lists_ref.shape[1:]
-    rows = [lists_ref[0, g, s : s + 1, :] for g in range(owners) for s in range(slots)]
+    me = lax.axis_index("shot")
+    rows = []
+    for k in range(owners):
+        lists = lists_ref[0, partner(me, k, owners)]
+        rows += [lists[s : s + 1, :] for s in range(slots)]
     count = len(rows)
     while len(rows) % 8:
         rows.append(rows[0])
@@ -388,15 +398,11 @@
     spectra_ref,
     table_ref,
     spectra_out_ref,
-    packed_ref,
     final_ref,
-    level_ref,
-    prior_ref,
-    coef_ref,
-    feature_ref,
-    *,
+    *rest,
     width,
 ):
+    packed_refs, (level_ref, prior_ref, coef_ref, feature_ref) = rest[:-4], rest[-4:]
     shots, depth = edge_ref.shape[-2:]
     targets = column_ref.shape[1]
     first = -STEPS
@@ -493,14 +499,14 @@
             spectra_out_ref[pl.ds(s * parts, parts), pl.ds(base, lanes)] = value
             feature_ref[pl.ds(s * parts, parts), pl.ds(base, lanes)] = value.astype(jnp.bfloat16)
 
-    owners = packed_ref.shape[0]
-    patch = packed_ref.shape[2]
+    owners = len(packed_refs)
+    patch = packed_refs[0].shape[1]
     slots = list_hot_ref.shape[0] // (owners * patch)
     half = patch // 2
     row = lax.broadcasted_iota(jnp.int32, (half, patch), 0)
     lane = lax.broadcasted_iota(jnp.int32, (half, patch), 1)
     from_last = (lane < half) & (row > lane)
-    for g in range(owners):
+    for g, packed_ref in enumerate(packed_refs):
         chosen = lax.dot_general(
             list_hot_ref[pl.ds(g * slots * patch, slots * patch), :],
             feature_ref[...],
@@ -512,11 +518,11 @@
             mine = chosen[s * patch : (s + 1) * patch]
             gram = lax.dot_general(mine, mine, NT, preferred_element_type=jnp.float32)
             last = pltpu.roll(gram[half:], half, 1)
-            packed_ref[g, pl.ds(s * half, half), :] = jnp.where(from_last, last, gram[:half])
+            packed_ref[pl.ds(s * half, half), :] = jnp.where(from_last, last, gram[:half])
             diagonals.append(jnp.sum(jnp.where(row == lane, last, 0.0), 0, keepdims=True))
         while len(diagonals) % 8:
             diagonals.append(jnp.zeros((1, patch), jnp.float32))
-        packed_ref[g, pl.ds(slots * half, len(diagonals)), :] = jnp.concatenate(diagonals, 0)
+        packed_ref[pl.ds(slots * half, len(diagonals)), :] = jnp.concatenate(diagonals, 0)
 
 
 def finish(lower, upper, inner, spectra, table, width, owners, slots, patch):
@@ -528,8 +534,8 @@
     rows = slots * (patch // 2) + -(-slots // 8) * 8
     out_shape = [
         f32((features, targets)),
-        f32((owners, rows, patch)),
         f32((2, 2, STEPS, shots, depth)),
+        *[f32((rows, patch))] * owners,
     ]
     vmem = pl.BlockSpec(memory_space=pltpu.VMEM)
     return pl.pallas_call(
@@ -589,16 +595,16 @@
     )(p_inner, q_inner, final)
 
 
-def tiles_kernel(received_ref, counts_ref, out_ref, *, features):
-    groups = received_ref.shape[0]
+def tiles_kernel(counts_ref, *refs, features):
+    received, out_ref = refs[:-1], refs[-1]
     slots, patch = out_ref.shape[2], out_ref.shape[3]
     half = patch // 2
     row = lax.broadcasted_iota(jnp.int32, (half, patch), 0)
     lane = lax.broadcasted_iota(jnp.int32, (half, patch), 1)
     live = counts_ref[0, 0]
-    total = received_ref[0]
-    for g in range(1, groups):
-        total = total + received_ref[g]
+    total = received[0][...]
+    for ref in received[1:]:
+        total = total + ref[...]
     for s in range(slots):
         scale = jnp.where(s < live, 1.0 / features, 0.0)
         packed = total[s * half : (s + 1) * half] * scale
@@ -616,18 +622,16 @@
 
 
 def tiles(received, patch_counts, slots, features):
-    patch = received.shape[2]
+    patch = received[0].shape[1]
     return pl.pallas_call(
         functools.partial(tiles_kernel, features=features),
-        in_specs=[
-            pl.BlockSpec(memory_space=pltpu.VMEM),
-            pl.BlockSpec(memory_space=pltpu.SMEM),
-        ],
+        in_specs=[pl.BlockSpec(memory_space=pltpu.SMEM)]
+        + [pl.BlockSpec(memory_space=pltpu.VMEM)] * len(received),
         out_specs=pl.BlockSpec(memory_space=pltpu.VMEM),
         out_shape=jax.ShapeDtypeStruct((1, 1, slots, patch, patch), jnp.float32),
         compiler_params=compiler_params(16),
         name="tiles",
-    )(received, patch_counts)
+    )(patch_counts, *received)
 
 
 def shards(
@@ -666,7 +670,7 @@
     edge, prior_edge, coef_edge, p_inner, q_inner, sample, depth_hot, column, list_hot = interior(
         fields, params, target_cells, patch_lists
     )
-    spectra_out, packed, final = finish(
+    spectra_out, final, *packed = finish(
         lower,
         upper,
         (edge, prior_edge, coef_edge, sample, depth_hot, column, list_hot),
@@ -677,7 +681,10 @@
         slots,
         patch,
     )
-    received = lax.psum_scatter(packed, "shot", scatter_dimension=0, tiled=True)
+    received = packed[:1]
+    for k in sorted(range(1, owners), key=lambda k: (k < owners // 2, k)):
+        pairs = [(i, int(partner(i, k, owners))) for i in range(owners)]
+        received.append(lax.ppermute(packed[k], "shot", pairs))
     pressure_out, auxiliary_out = [untiled(item) for item in assemble(p_inner, q_inner, final)]
     gram_tiles = tiles(received, patch_counts, slots, shots * parts * owners)
     return (pressure_out, auxiliary_out, spectra_out.reshape(spectra.shape), gram_tiles)

time: 59.4 us -> 28.5 us (0.48)
  the two profiles are of different devices: /device:TPU:0 before, /device:TPU:16 now
where the time goes in v4:
time: 28.5 us; the launch traced here: 28 us
  Pallas kernels  14.8 us (52%)
  starting transfers between devices  9.08 us (32%)
  waiting for transfers between devices  2.24 us (8%)
  between operations  1.53 us (5%)
    pallas_call x1, Pallas kernels, interior(): pl.pallas_call(interior_kernel, in_specs=[vmem] * 10, out_specs=[vmem] *...  6.89 us
    ppermute x1, starting transfers between devices, shards(): lower = lax.ppermute(last_rows, 'brick', upward)  3.53 us
    ppermute x1, starting transfers between devices, shards(): upper = lax.ppermute(first_rows, 'brick', downward)  3.34 us
    pallas_call x1, Pallas kernels, finish(): pl.pallas_call(functools.partial(finish_kernel, width=width), in_specs=[v...  2.97 us
    pallas_call x1, Pallas kernels, outer_rows(): pl.pallas_call(outer_kernel, in_specs=[pl.BlockSpec(memory_space=pltpu.HB...  2.44 us
    ppermute x3, waiting for transfers between devices, shards(): received.append(lax.ppermute(packed[k], 'shot', pairs))  2.24 us
    ppermute x3, starting transfers between devices, shards(): received.append(lax.ppermute(packed[k], 'shot', pairs))  2.21 us
    pallas_call x1, Pallas kernels, assemble(): pl.pallas_call(assemble_kernel, in_specs=[vmem] * 3, out_specs=[vmem] * 2...  1.66 us
  transfers between devices with their start and end apart: 5, of which 2 were waited for; matrix products, arithmetic and copies ran while one was open for 1% of the time, Pallas kernels for 31%

profile of v4, /device:TPU:16, one launch (start us, length us, event | category | flops | bytes accessed | tf_op | source)
XLA Modules:
  0.0 28.0 jit_solution(1713303432336006270)
XLA Ops:
  0.6 0.0 copy-start
  0.6 0.0 copy-start.1
  0.7 0.0 copy-start.2
  0.7 0.0 copy-start.3
  0.7 0.0 copy-start.5
  0.7 0.0 copy-start.6
  0.7 0.0 copy-start.7
  0.7 0.0 copy-start.8
  0.7 0.0 copy-start.11
  0.7 0.0 copy-start.10
  0.7 0.0 copy-start.9
  0.7 2.4 %outer_rows.1 = (bf16[160,512]{1,0:T(8,128)(2,1)}, bf16[160,512]{1,0:T(8,128)(2,1)}) custom-call(f32[8,4,4,8,128]{4,3,2,1,0:T(8,128)} %bitcast.21, f32[8,4,4,8,128]{4,3,2,1,0:T(8,128)} %bitcast.23, f32[8,4,4,8,128]{4,3,2,1,0:T(8,128)} %bitcast.25, f32[8,4,4,8,128]{4,3,2,1,0:T(8,128)} %bitcast.27, f32[32,512]{1,0:T(8,128)} %refs_4_.1, f32[32,512]{1,0:T(8,128)} %refs_5_.1, ...), custom_call_target="tpu_custom_call" | custom-call | tf_op jit(solution)/shard_map/outer_rows/pallas_call | solution.py:201
  3.2 0.0 copy-start.4
  3.2 3.5 %collective-permute-start = (bf16[160,512]{1,0:T(8,128)(2,1)}, bf16[160,512]{1,0:T(8,128)(2,1)S(1)}, u32[]{:S(2)}, u32[]{:S(2)}) collective-permute-start(bf16[160,512]{1,0:T(8,128)(2,1)} %get-tuple-element.25), channel_id=1, source_target_pairs={{0,1},{1,2},{2,3},{3,4},{4,5},{5,6},{6,7},{8,9},{9,10},{10,11},{11... | collective-permute-start | bytes 491528 | tf_op jit(solution)/shard_map/ppermute | solution.py:662
  6.7 3.3 %collective-permute-start.1 = (bf16[160,512]{1,0:T(8,128)(2,1)}, bf16[160,512]{1,0:T(8,128)(2,1)S(1)}, u32[]{:S(2)}, u32[]{:S(2)}) collective-permute-start(bf16[160,512]{1,0:T(8,128)(2,1)} %get-tuple-element.26), channel_id=1, source_target_pairs={{1,0},{2,1},{3,2},{4,3},{5,4},{6,5},{7,6},{9,8},{10,9},{11,10},{12... | collective-permute-start | bytes 491528 | tf_op jit(solution)/shard_map/ppermute | solution.py:663
  10.1 0.0 copy-done.11
  10.1 0.1 multiply_cosine_fusion
  10.2 0.0 copy-done.10
  10.2 0.0 copy-done
  10.3 0.0 copy-done.1
  10.3 0.0 copy-done.2
  10.3 0.0 copy-done.3
  10.3 0.0 copy-done.5
  10.3 0.0 copy-done.6
  10.3 0.0 copy-done.7
  10.3 0.0 copy-done.8
  10.3 0.0 copy-done.9
  10.3 6.9 %interior.1 = (f32[2,2,4,2,8,512]{5,4,3,2,1,0:T(8,128)S(1)}, f32[2,2,8,512]{3,2,1,0:T(8,128)S(1)}, f32[2,5,8,512]{3,2,1,0:T(8,128)S(1)}, f32[24,8,512]{2,1,0:T(8...) custom-call(f32[8,4,4,8,128]{4,3,2,1,0:T(8,128)S(1)} %bitcast.22, ...), custom_call_target="tpu_custom_call" | custom-call | flops 104857600 | bytes 8388608 | tf_op jit(solution)/shard_map/interior/pallas_call | solution.py:371
  17.2 0.1 pad_maximum_fusion
  17.3 0.0 collective-permute-done.lower_ref
  17.3 0.0 collective-permute-done.1.upper_ref
  17.3 0.1 broadcast_in_dim.2.table_ref
  17.4 0.0 copy-done.4
  17.4 3.0 %finish.1 = (f32[256,512]{1,0:T(8,128)}, f32[2,2,4,8,512]{4,3,2,1,0:T(8,128)S(1)}, f32[200,128]{1,0:T(8,128)S(1)}, f32[200,128]{1,0:T(8,128)S(1)}, f32[200,128]{1,0:T(8,128)S(1)}, /*index=5*/f32[200,128]{1,0:T(8,128)S(1)}) custom-call(bf16[160,512]{1,0:T(8,128)(2,1)S(1)} %collective-permute-done.lower_ref, ...), custom_call_target="tpu_custom_call" | custom-call | tf_op jit(solution)/shard_map/finish/pallas_call | solution.py:541
  20.4 1.6 %collective-permute-start.2 = (f32[200,128]{1,0:T(8,128)S(1)}, f32[200,128]{1,0:T(8,128)S(1)}, u32[]{:S(2)}, u32[]{:S(2)}) collective-permute-start(f32[200,128]{1,0:T(8,128)S(1)} %get-tuple-element.39), channel_id=1, source_target_pairs={{0,16},{8,24},{16,0},{24,8},{1,17},{9,25},{17,1},{25,9},{2,18},{10... | collective-permute-start | bytes 307208 | tf_op jit(solution)/shard_map/ppermute | solution.py:687
  22.0 0.0 collective-permute-start.3
  22.0 0.6 %collective-permute-start.4 = (f32[200,128]{1,0:T(8,128)S(1)}, f32[200,128]{1,0:T(8,128)S(1)}, u32[]{:S(2)}, u32[]{:S(2)}) collective-permute-start(f32[200,128]{1,0:T(8,128)S(1)} %get-tuple-element.41), channel_id=1, source_target_pairs={{0,8},{8,0},{16,24},{24,16},{1,9},{9,1},{17,25},{25,17},{2,10},{10... | collective-permute-start | bytes 307208 | tf_op jit(solution)/shard_map/ppermute | solution.py:687
  23.2 1.7 %assemble.1 = (f32[8,4,4,8,128]{4,3,2,1,0:T(8,128)}, f32[8,4,4,8,128]{4,3,2,1,0:T(8,128)}) custom-call(f32[24,8,512]{2,1,0:T(8,128)S(1)} %get-tuple-element.23.p_inner_ref, f32[24,8,512]{2,1,0:T(8,128)S(1)} %get-tuple-element.24.q_inner_ref, f32[2,2,4,8,512]{4,3,2,1,0:T(8,128)S(1)} %get-tuple-element.34.final_ref), custom_call_target="tpu_custom_call" | custom-call | flops 8388608 | bytes 4194304 | tf_op jit(solution)/shard_map/assemble/pallas_call | solution.py:587
  24.9 0.4 %collective-permute-done.2.refs_1_ = f32[200,128]{1,0:T(8,128)S(1)} collective-permute-done((f32[200,128]{1,0:T(8,128)S(1)}, f32[200,128]{1,0:T(8,128)S(1)}, u32[]{:S(2)}, u32[]{:S(2)}) %collective-permute-start.2) | collective-permute-done | bytes 102432 | tf_op jit(solution)/shard_map/ppermute | solution.py:687
  25.3 1.9 %collective-permute-done.3.refs_2_ = f32[200,128]{1,0:T(8,128)S(1)} collective-permute-done((f32[200,128]{1,0:T(8,128)S(1)}, f32[200,128]{1,0:T(8,128)S(1)}, u32[]{:S(2)}, u32[]{:S(2)}) %collective-permute-start.3) | collective-permute-done | bytes 102432 | tf_op jit(solution)/shard_map/ppermute | solution.py:687
  27.1 0.0 collective-permute-done.4.refs_3_
  27.1 0.9 %tiles.1 = f32[1,1,3,128,128]{4,3,2,1,0:T(8,128)} custom-call(s32[1,1]{1,0:T(1,128)S(6)} %copy.18.counts_ref, f32[200,128]{1,0:T(8,128)S(1)} %get-tuple-element.38.refs_0_, f32[200,128]{1,0:T(8,128)S(1)} %collective-permute-done.2.refs_1_, f32[200,128]{1,0:T(8,128)S(1)} %collective-permute-done.3.refs_2_, f32[200,128]{1,0:T(8,128)S(1)} %collective-permute-done.4.refs_3_), custom_call_target="tpu_custom_call" | custom-call | tf_op jit(solution)/shard_map/tiles/pallas_call | solution.py:626
  (2 shorter events, 0.0 us)
Async XLA Ops:
  0.6 9.6 %copy-start = (f32[8,32,512]{2,1,0:T(8,128)S(1)}, f32[8,32,512]{2,1,0:T(8,128)}, u32[]{:S(2)}) copy-start(f32[8,32,512]{2,1,0:T(8,128)} %param.13) | copy-start | bytes 1572868
  0.6 9.6 %copy-start.1 = (f32[8,32,512]{2,1,0:T(8,128)S(1)}, f32[8,32,512]{2,1,0:T(8,128)}, u32[]{:S(2)}) copy-start(f32[8,32,512]{2,1,0:T(8,128)} %param.14) | copy-start | bytes 1572868
  0.7 9.6 %copy-start.2 = (f32[8,32,512]{2,1,0:T(8,128)S(1)}, f32[8,32,512]{2,1,0:T(8,128)}, u32[]{:S(2)}) copy-start(f32[8,32,512]{2,1,0:T(8,128)} %param.15) | copy-start | bytes 1572868
  0.7 9.6 %copy-start.3 = (f32[8,32,512]{2,1,0:T(8,128)S(1)}, f32[8,32,512]{2,1,0:T(8,128)}, u32[]{:S(2)}) copy-start(f32[8,32,512]{2,1,0:T(8,128)} %param.16) | copy-start | bytes 1572868
  0.7 9.6 %copy-start.5 = (f32[32,512]{1,0:T(8,128)S(1)}, f32[32,512]{1,0:T(8,128)}, u32[]{:S(2)}) copy-start(f32[32,512]{1,0:T(8,128)} %refs_4_.1) | copy-start | bytes 196612
  0.7 9.6 %copy-start.6 = (f32[32,512]{1,0:T(8,128)S(1)}, f32[32,512]{1,0:T(8,128)}, u32[]{:S(2)}) copy-start(f32[32,512]{1,0:T(8,128)} %refs_5_.1) | copy-start | bytes 196612
  0.7 9.6 %copy-start.7 = (f32[32,512]{1,0:T(8,128)S(1)}, f32[32,512]{1,0:T(8,128)}, u32[]{:S(2)}) copy-start(f32[32,512]{1,0:T(8,128)} %refs_6_.1) | copy-start | bytes 196612
  0.7 9.6 %copy-start.8 = (f32[32,512]{1,0:T(8,128)S(1)}, f32[32,512]{1,0:T(8,128)}, u32[]{:S(2)}) copy-start(f32[32,512]{1,0:T(8,128)} %refs_7_.1) | copy-start | bytes 196612
  0.7 9.4 %copy-start.11 = (f32[16]{0:T(128)S(1)}, f32[16]{0:T(128)}, u32[]{:S(2)}) copy-start(f32[16]{0:T(128)} %param.21) | copy-start | bytes 196
  0.7 9.5 %copy-start.10 = (s32[1,4,3,128]{3,1,2,0:T(4,128)S(1)}, s32[1,4,3,128]{3,1,2,0:T(4,128)}, u32[]{:S(2)}) copy-start(s32[1,4,3,128]{3,1,2,0:T(4,128)} %param.24) | copy-start | bytes 18436
  0.7 9.6 %copy-start.9 = (s32[512]{0:T(512)S(1)}, s32[512]{0:T(512)}, u32[]{:S(2)}) copy-start(s32[512]{0:T(512)} %param.23) | copy-start | bytes 6148
  3.2 14.2 %copy-start.4 = (f32[8,32,512]{2,1,0:T(8,128)S(1)}, f32[8,32,512]{2,1,0:T(8,128)}, u32[]{:S(2)}) copy-start(f32[8,32,512]{2,1,0:T(8,128)} %param.22) | copy-start | bytes 1572868
  3.2 14.1 %collective-permute-start = (bf16[160,512]{1,0:T(8,128)(2,1)}, bf16[160,512]{1,0:T(8,128)(2,1)S(1)}, u32[]{:S(2)}, u32[]{:S(2)}) collective-permute-start(bf16[160,512]{1,0:T(8,128)(2,1)} %get-tuple-element.25), channel_id=1, source_target_pairs={{0,1},{1,2},{2,3},{3,4},{4,5},{5,6},{6,7},{8,9},{9,10},{10,11},{11... | collective-permute-start | bytes 491528 | tf_op jit(solution)/shard_map/ppermute | solution.py:662
  6.7 10.6 %collective-permute-start.1 = (bf16[160,512]{1,0:T(8,128)(2,1)}, bf16[160,512]{1,0:T(8,128)(2,1)S(1)}, u32[]{:S(2)}, u32[]{:S(2)}) collective-permute-start(bf16[160,512]{1,0:T(8,128)(2,1)} %get-tuple-element.26), channel_id=1, source_target_pairs={{1,0},{2,1},{3,2},{4,3},{5,4},{6,5},{7,6},{9,8},{10,9},{11,10},{12... | collective-permute-start | bytes 491528 | tf_op jit(solution)/shard_map/ppermute | solution.py:663
  20.4 4.9 %collective-permute-start.2 = (f32[200,128]{1,0:T(8,128)S(1)}, f32[200,128]{1,0:T(8,128)S(1)}, u32[]{:S(2)}, u32[]{:S(2)}) collective-permute-start(f32[200,128]{1,0:T(8,128)S(1)} %get-tuple-element.39), channel_id=1, source_target_pairs={{0,16},{8,24},{16,0},{24,8},{1,17},{9,25},{17,1},{25,9},{2,18},{10... | collective-permute-start | bytes 307208 | tf_op jit(solution)/shard_map/ppermute | solution.py:687
  22.0 5.2 %collective-permute-start.3 = (f32[200,128]{1,0:T(8,128)S(1)}, f32[200,128]{1,0:T(8,128)S(1)}, u32[]{:S(2)}, u32[]{:S(2)}) collective-permute-start(f32[200,128]{1,0:T(8,128)S(1)} %get-tuple-element.40), channel_id=1, source_target_pairs={{0,24},{8,16},{16,8},{24,0},{1,25},{9,17},{17,9},{25,1},{2,26},{10... | collective-permute-start | bytes 307208 | tf_op jit(solution)/shard_map/ppermute | solution.py:687
  22.0 5.2 %collective-permute-start.4 = (f32[200,128]{1,0:T(8,128)S(1)}, f32[200,128]{1,0:T(8,128)S(1)}, u32[]{:S(2)}, u32[]{:S(2)}) collective-permute-start(f32[200,128]{1,0:T(8,128)S(1)} %get-tuple-element.41), channel_id=1, source_target_pairs={{0,8},{8,0},{16,24},{24,16},{1,9},{9,1},{17,25},{25,17},{2,10},{10... | collective-permute-start | bytes 307208 | tf_op jit(solution)/shard_map/ppermute | solution.py:687

commit v5 on v4

--- a/solution.py
+++ b/solution.py
@@ -85,39 +85,64 @@
     return sine_sq, quarter_sin, courant, gain_p, gain_q
 
 
+def blocks(row):
+    return [row[:, j : j + LANES] for j in range(0, row.shape[1], LANES)]
+
+
 def depth_terms(row):
-    depth = row.shape[-1]
-    lane = lax.broadcasted_iota(jnp.int32, row.shape, 1)
-    deeper = jnp.where(lane < depth - 1, pltpu.roll(row, depth - 1, 1), 0.0)
-    upper = jnp.where(lane > 0, pltpu.roll(row, 1, 1), 0.0)
-    return deeper + upper, deeper - upper
+    lane = lax.broadcasted_iota(jnp.int32, row[0].shape, 1)
+    shallow = [pltpu.roll(block, 1, 1) for block in row]
+    deep = [pltpu.roll(block, LANES - 1, 1) for block in row]
+    outside = jnp.zeros_like(row[0])
+    sums, differences = [], []
+    for j in range(len(row)):
+        above = jnp.where(lane == 0, shallow[j - 1] if j else outside, shallow[j])
+        below = jnp.where(
+            lane == LANES - 1, deep[j + 1] if j + 1 < len(row) else outside, deep[j]
+        )
+        sums.append(below + above)
+        differences.append(below - above)
+    return sums, differences
 
 
 def advance(count, p_row, q_row, p_prior, q_prior, coefficient, put):
-    p_back, p_here = p_row(-1), p_row(0)
-    q_back, q_here = q_row(-1), q_row(0)
+    p_back, p_here = blocks(p_row(-1)), blocks(p_row(0))
+    q_back, q_here = blocks(q_row(-1)), blocks(q_row(0))
     _, p_back_d = depth_terms(p_back)
     _, q_back_d = depth_terms(q_back)
     p_sum, p_here_d = depth_terms(p_here)
     q_sum, q_here_d = depth_terms(q_here)
     for row in range(count):
-        p_next, q_next = p_row(row + 1), q_row(row + 1)
+        p_next, q_next = blocks(p_row(row + 1)), blocks(q_row(row + 1))
         p_next_sum, p_next_d = depth_terms(p_next)
         q_next_sum, q_next_d = depth_terms(q_next)
-        sine_sq, quarter_sin, courant, gain_p, gain_q = coefficient(row)
-        twice_p, twice_q = p_here + p_here, q_here + q_here
-        side = p_next + p_back
-        across = (side - twice_p) + sine_sq * (p_sum - side) - quarter_sin * (p_next_d - p_back_d)
-        side = q_next + q_back
-        along = (q_sum - twice_q) + sine_sq * (side - q_sum) + quarter_sin * (q_next_d - q_back_d)
-        along = courant * along
-        put(
-            row,
-            (twice_p - p_prior(row)) + (gain_p * across + along),
-            (twice_q - q_prior(row)) + (gain_q * across + along),
-        )
+        p_old, q_old = blocks(p_prior(row)), blocks(q_prior(row))
+        p_new, q_new = [], []
+        for j in range(len(p_here)):
+            sine_sq, quarter_sin, courant, gain_p, gain_q = [coefficient(i, row, j) for i in range(5)]
+            twice_p, twice_q = p_here[j] + p_here[j], q_here[j] + q_here[j]
+            side = p_next[j] + p_back[j]
+            mixed = p_next_d[j] - p_back_d[j]
+            across = (side - twice_p) + sine_sq * (p_sum[j] - side) - quarter_sin * mixed
+            side = q_next[j] + q_back[j]
+            mixed = q_next_d[j] - q_back_d[j]
+            along = (q_sum[j] - twice_q) + sine_sq * (side - q_sum[j]) + quarter_sin * mixed
+            along = courant * along
+            p_new.append((twice_p - p_old[j]) + (gain_p * across + along))
+            q_new.append((twice_q - q_old[j]) + (gain_q * across + along))
+        put(row, jnp.concatenate(p_new, 1), jnp.concatenate(q_new, 1))
         p_back, p_here, p_back_d, p_here_d, p_sum = p_here, p_next, p_here_d, p_next_d, p_next_sum
         q_back, q_here, q_back_d, q_here_d, q_sum = q_here, q_next, q_here_d, q_next_d, q_next_sum
+
+
+class CoefficientRows:
+    def __init__(self, ref, shots):
+        self.shots, (_, self.along, self.rows, lanes) = shots, ref.shape
+        self.flat = ref.reshape(ref.shape[0] * self.along * self.rows, lanes)
+
+    def __call__(self, index, row, j):
+        place = (index * self.along + j) * self.rows + row
+        return self.flat[pl.ds(place, self.shots, stride=0), :]
 
 
 def split_bf16(values):
@@ -136,7 +161,9 @@
         for i in range(4):
             copies.append(
                 pltpu.make_async_copy(
-                    sources[i].at[:, pl.ds(place, 1)], field_ref.at[side, i], field_sem.at[side, i]
+                    sources[i].at[:, pl.ds(place, 1), :, pl.ds(side * STEPS, STEPS)],
+                    field_ref.at[side, i, :, :, :, pl.ds(side * STEPS, STEPS)],
+                    field_sem.at[side, i],
                 )
             )
         for i in range(4):
@@ -175,8 +202,9 @@
             put(row(*first), row(*second))
         terms = tilt_coefficients(*[param_ref[side, i] for i in range(4)])
         rows = []
-        for term in terms:
-            for distance in range(STEPS - 1):
+        for index, term in enumerate(terms):
+            term = -term if index == 1 and side == 0 else term
+            for distance in reversed(range(STEPS - 1)):
                 place = distance if side == 0 else tile - 1 - distance
                 rows.append(term[place : place + 1, :])
         while len(rows) < 2 * shots:
@@ -247,35 +275,42 @@
     list_hot_ref,
     level_ref,
     coef_ref,
+    split_ref,
+    sems,
 ):
-    shots = p_ref.shape[0]
-    width, depth = courant_ref.shape
-    p_rows, q_rows, pp_rows, qq_rows = [ShotRows(ref) for ref in (p_ref, q_ref, pp_ref, qq_ref)]
+    shots, width, depth = p_ref.shape
+    along = depth // LANES
+    copies = []
+    for i, ref in enumerate((p_ref, q_ref, pp_ref, qq_ref)):
+        for s in range(shots):
+            copies.append(
+                pltpu.make_async_copy(
+                    ref.at[s], level_ref.at[1 - i // 2, i % 2, :, s], sems.at[i, s]
+                )
+            )
+    for copy in copies:
+        copy.start()
 
     terms = tilt_coefficients(courant_ref[...], epsilon_ref[...], delta_ref[...], tilt_ref[...])
     for index, term in enumerate(terms):
-        for x in range(width):
-            coef_ref[index, x] = jnp.broadcast_to(term[x : x + 1, :], (shots, depth))
-        flip = -term if index == 1 else term
-        coef_edge_ref[0, index] = term[:8, :]
-        coef_edge_ref[1, index] = flip[width - 8 :, :]
-
-    @pl.loop(0, width)
-    def _(x):
-        level_ref[0, 0, x] = p_rows[x]
-        level_ref[0, 1, x] = q_rows[x]
-
+        for j in range(along):
+            coef_ref[index, j] = term[:, j * LANES : (j + 1) * LANES]
+        for k in range(STEPS):
+            coef_edge_ref[0, index, pl.ds(k, 1), :] = term[k : k + 1, :]
+            row = term[width - 1 - k : width - k, :]
+            coef_edge_ref[1, index, pl.ds(k, 1), :] = -row if index == 1 else row
+
+    one, zero = jnp.bfloat16(1), jnp.bfloat16(0)
     cells = cells_ref[...]
     column = cells // depth
-    z_of = cells - column * depth
     column_ref[...] = column
     targets = cells.shape[1]
-    for half in range(2):
-        for base in range(0, depth, 64):
-            lanes = lax.broadcasted_iota(jnp.int32, (64, targets), 0) + base
-            depth_hot_ref[pl.ds(half * depth + base, 64), :] = jnp.where(
-                lanes == z_of, 1.0, 0.0
-            ).astype(jnp.bfloat16)
+    z_of = jnp.broadcast_to(cells - column * depth, (16, targets)).astype(jnp.int16)
+    places = lax.broadcasted_iota(jnp.int16, (16, targets), 0)
+    for base in range(0, depth, 16):
+        hot = jnp.where(places + jnp.int16(base) == z_of, one, zero)
+        depth_hot_ref[pl.ds(base, 16), :] = hot
+        depth_hot_ref[pl.ds(depth + base, 16), :] = hot
 
     owners, slots, patch = lists_ref.shape[1:]
     me = lax.axis_index("shot")
@@ -286,73 +321,81 @@
     count = len(rows)
     while len(rows) % 8:
         rows.append(rows[0])
-    upright = jnp.transpose(jnp.concatenate(rows, 0).astype(jnp.float32))
-    lanes = lax.broadcasted_iota(jnp.int32, (patch, targets), 1).astype(jnp.float32)
+    upright = jnp.transpose(jnp.concatenate(rows, 0).astype(jnp.float32)).astype(jnp.int32)
+    lanes = lax.broadcasted_iota(jnp.int16, (patch, LANES), 1)
     for k in range(count):
-        list_hot_ref[pl.ds(k * patch, patch), :] = jnp.where(
-            upright[:, k : k + 1] == lanes, 1.0, 0.0
-        ).astype(jnp.bfloat16)
-
+        wanted = jnp.broadcast_to(upright[:, k : k + 1], (patch, LANES)).astype(jnp.int16)
+        for base in range(0, targets, LANES):
+            list_hot_ref[pl.ds(k * patch, patch), pl.ds(base, LANES)] = jnp.where(
+                lanes + jnp.int16(base) == wanted, one, zero
+            )
+
+    for copy in copies:
+        copy.wait()
     for side in range(2):
         x = 0 if side == 0 else width - 1
-        prior_edge_ref[side, 0] = pp_rows[x]
-        prior_edge_ref[side, 1] = qq_rows[x]
-
-    chunk = 8
+        prior_edge_ref[side, 0] = level_ref[0, 0, x]
+        prior_edge_ref[side, 1] = level_ref[0, 1, x]
+
+    coefficients = CoefficientRows(coef_ref, shots)
+    offsets = [0]
     for step in range(1, STEPS + 1):
         low, high = step, width - step
-        chunks = -(-(high - low) // chunk)
-
-        @pl.loop(0, chunks)
+        chunk = 8 if (high - low) % 8 == 0 else 10
+        offset = offsets[-1]
+        offsets.append(offset + high - low)
+
+        @pl.loop(0, -(-(high - low) // chunk))
         def _(index):
-            start = jnp.minimum(low + chunk * index, high - chunk)
-
-            def prior(field):
-                if step == 1:
-                    rows = (pp_rows, qq_rows)[field]
-                    return lambda r: rows[start + r]
-                return lambda r: level_ref[step - 2, field, start + r]
+            at = jnp.minimum(chunk * index, high - low - chunk)
+            start = low + at
+            held = []
 
             def put(r, p_new, q_new):
                 if step < STEPS:
-                    level_ref[step, 0, start + r] = p_new
-                    level_ref[step, 1, start + r] = q_new
+                    level_ref[step + 1, 0, start + r] = p_new
+                    level_ref[step + 1, 1, start + r] = q_new
                 else:
-                    p_inner_ref[start + r - STEPS] = p_new
-                    q_inner_ref[start + r - STEPS] = q_new
+                    p_inner_ref[at + r] = p_new
+                    q_inner_ref[at + r] = q_new
+                held.append(p_new)
+                if len(held) == 2:
+                    first, rest = split_bf16(jnp.concatenate(held, 0))
+                    place = pl.multiple_of((offset + at + r - 1) * shots, 2 * shots)
+                    split_ref[pl.ds(place, 2 * shots), pl.ds(0, depth)] = first
+                    split_ref[pl.ds(place, 2 * shots), pl.ds(depth, depth)] = rest
+                    held.clear()
 
             advance(
                 chunk,
+                lambda r: level_ref[step, 0, start + r],
+                lambda r: level_ref[step, 1, start + r],
                 lambda r: level_ref[step - 1, 0, start + r],
                 lambda r: level_ref[step - 1, 1, start + r],
-                prior(0),
-                prior(1),
-                lambda r: [coef_ref[i, start + r] for i in range(5)],
+                lambda i, r, j: coefficients(i, start + r, j),
                 put,
             )
 
     for step in range(STEPS):
         for field in range(2):
             for near in range(2):
-                edge_ref[0, field, step, near] = level_ref[step, field, step + near]
-                edge_ref[1, field, step, near] = level_ref[step, field, width - 1 - step - near]
-
-    for step in range(1, STEPS + 1):
-        low, high = step, width - step
-        if step < STEPS:
-            values = level_ref[step, 0, low:high]
-        else:
-            values = p_inner_ref[...]
-        found = sample_rows(values.reshape((high - low) * shots, depth), depth_hot_ref[...])
-        total = jnp.zeros((shots, targets), jnp.float32)
-        for r in range(high - low):
-            total = total + jnp.where(column == low + r, found[r * shots : (r + 1) * shots], 0.0)
-        sample_ref[step - 1] = total
+                edge_ref[0, field, step, near] = level_ref[step + 1, field, step + near]
+                edge_ref[1, field, step, near] = level_ref[step + 1, field, width - 1 - step - near]
+
+    found = jnp.dot(split_ref[...], depth_hot_ref[...], preferred_element_type=jnp.float32)
+    totals = [jnp.zeros((shots, targets), jnp.float32) for _ in range(STEPS)]
+    for x in range(1, width - 1):
+        here = column == x
+        for step in range(1, STEPS + 1):
+            if step <= x < width - step:
+                row = (offsets[step - 1] + x - step) * shots
+                totals[step - 1] += jnp.where(here, found[row : row + shots], 0.0)
+    for step in range(STEPS):
+        sample_ref[step] = totals[step]
 
 
 def interior(fields, params, target_cells, patch_lists):
-    shots = fields[0].shape[0]
-    width, depth = params[0].shape
+    shots, width, depth = fields[0].shape
     targets = target_cells.shape[0]
     _, owners, slots, patch = patch_lists.shape
     f32 = functools.partial(jax.ShapeDtypeStruct, dtype=jnp.float32)
@@ -370,12 +413,14 @@
     vmem = pl.BlockSpec(memory_space=pltpu.VMEM)
     return pl.pallas_call(
         interior_kernel,
-        in_specs=[vmem] * 10,
+        in_specs=[pl.BlockSpec(memory_space=pl.ANY)] * 4 + [vmem] * 6,
         out_specs=[vmem] * len(out_shape),
         out_shape=out_shape,
         scratch_shapes=[
-            pltpu.VMEM((STEPS, 2, width, shots, depth), jnp.float32),
-            pltpu.VMEM((5, width, shots, depth), jnp.float32),
+            pltpu.VMEM((STEPS + 1, 2, width, shots, depth), jnp.float32),
+            pltpu.VMEM((5, depth // LANES, width, LANES), jnp.float32),
+            pltpu.VMEM((STEPS * (width - STEPS - 1) * shots, 2 * depth), jnp.bfloat16),
+            pltpu.SemaphoreType.DMA((4, shots)),
         ],
         compiler_params=compiler_params(40),
         cost_estimate=pl.CostEstimate(
@@ -402,7 +447,8 @@
     *rest,
     width,
 ):
-    packed_refs, (level_ref, prior_ref, coef_ref, feature_ref) = rest[:-4], rest[-4:]
+    packed_refs = rest[:-6]
+    level_ref, prior_ref, coef_ref, feature_ref, out_ref, out_sem = rest[-6:]
     shots, depth = edge_ref.shape[-2:]
     targets = column_ref.shape[1]
     first = -STEPS
@@ -425,17 +471,13 @@
                     prior_ref[side, field - 2, -1 - distance - (1 - STEPS)] = value
         params = ref[pl.ds((4 + len(far_items())) * pair, pair), :].astype(jnp.float32)
         for index in range(5):
-            for distance in range(STEPS - 1):
-                line = index * (STEPS - 1) + distance
-                row = params[line : line + 1, :]
-                if index == 1 and side == 1:
-                    row = -row
-                coef_ref[side, index, STEPS - 2 - distance] = jnp.broadcast_to(row, (shots, depth))
-            for k in range(STEPS):
-                coef_ref[side, index, STEPS - 1 + k] = jnp.broadcast_to(
-                    coef_edge_ref[side, index, pl.ds(k if side == 0 else 7 - k, 1), :],
-                    (shots, depth),
-                )
+            far = params[index * (STEPS - 1) : (index + 1) * (STEPS - 1)]
+            near = coef_edge_ref[side, index, pl.ds(0, STEPS), :]
+            for j in range(depth // LANES):
+                coef_ref[side, index, j, pl.ds(0, STEPS - 1), :] = far[:, j * LANES : (j + 1) * LANES]
+                coef_ref[side, index, j, pl.ds(STEPS - 1, STEPS), :] = near[
+                    :, j * LANES : (j + 1) * LANES
+                ]
         for field in range(2):
             prior_ref[side, field, STEPS - 1] = prior_edge_ref[side, field]
             for step in range(STEPS):
@@ -448,6 +490,7 @@
         low = step - STEPS
 
         for side in range(2):
+            coefficients = CoefficientRows(coef_ref.at[side], shots)
 
             def prior(field):
                 if step == 1:
@@ -468,7 +511,7 @@
                 lambda r: level_ref[side, 1, step - 1, low + r - first],
                 prior(0),
                 prior(1),
-                lambda r: [coef_ref[side, i, low + r - (1 - STEPS) + 0] for i in range(5)],
+                lambda i, r, j: coefficients(i, low + r - (1 - STEPS), j),
                 put,
             )
 
@@ -496,8 +539,11 @@
             value = spectra_ref[pl.ds(s * parts, parts), pl.ds(base, lanes)]
             for step in range(STEPS):
                 value = value + table_ref[step] * samples[step][s : s + 1, base : base + lanes]
-            spectra_out_ref[pl.ds(s * parts, parts), pl.ds(base, lanes)] = value
+            out_ref[pl.ds(s * parts, parts), pl.ds(base, lanes)] = value
             feature_ref[pl.ds(s * parts, parts), pl.ds(base, lanes)] = value.astype(jnp.bfloat16)
+
+    out_copy = pltpu.make_async_copy(out_ref, spectra_out_ref, out_sem)
+    out_copy.start()
 
     owners = len(packed_refs)
     patch = packed_refs[0].shape[1]
@@ -523,6 +569,7 @@
         while len(diagonals) % 8:
             diagonals.append(jnp.zeros((1, patch), jnp.float32))
         packed_ref[pl.ds(slots * half, len(diagonals)), :] = jnp.concatenate(diagonals, 0)
+    out_copy.wait()
 
 
 def finish(lower, upper, inner, spectra, table, width, owners, slots, patch):
@@ -541,13 +588,15 @@
     return pl.pallas_call(
         functools.partial(finish_kernel, width=width),
         in_specs=[vmem] * 11,
-        out_specs=[vmem] * len(out_shape),
+        out_specs=[pl.BlockSpec(memory_space=pl.ANY)] + [vmem] * (len(out_shape) - 1),
         out_shape=out_shape,
         scratch_shapes=[
             pltpu.VMEM((2, 2, STEPS, 2 * STEPS + 1, shots, depth), jnp.float32),
             pltpu.VMEM((2, 2, STEPS, shots, depth), jnp.float32),
-            pltpu.VMEM((2, 5, 2 * STEPS - 1, shots, depth), jnp.float32),
+            pltpu.VMEM((2, 5, depth // LANES, 2 * STEPS, LANES), jnp.float32),
             pltpu.VMEM((features, targets), jnp.bfloat16),
+            pltpu.VMEM((features, targets), jnp.float32),
+            pltpu.SemaphoreType.DMA,
         ],
         compiler_params=compiler_params(40),
         name="finish",
@@ -651,11 +700,11 @@
 ):
     shots, width, depth = pressure.shape
     _, owners, slots, patch = patch_lists.shape
-    fields = [tiled(item) for item in (pressure, auxiliary, pressure_prior, auxiliary_prior)]
+    fields = (pressure, auxiliary, pressure_prior, auxiliary_prior)
     params = (courant_sq, thomsen_epsilon, thomsen_delta, tilt_angle)
     parts, targets = spectra.shape[1:]
 
-    first_rows, last_rows = outer_rows(fields, params)
+    first_rows, last_rows = outer_rows([tiled(item) for item in fields], params)
     bricks = lax.axis_size("brick")
     upward = [(i, i + 1) for i in range(bricks - 1)]
     downward = [(i + 1, i) for i in range(bricks - 1)]

time: 28.5 us -> 28.9 us (1.014)
  Pallas kernels: 14.8 us -> 15.3 us
    pallas_call x1, Pallas kernels: 6.89 us -> 7.54 us  [interior(): pl.pallas_call(interior_kernel, in_specs=[pl.BlockSpec(memory_space=pl.AN...]
  transfers between devices with their start and end apart: 5 -> 5, of which waited for: 2 -> 2; matrix products, arithmetic and copies ran while one was open for 1% -> 1% of each run, Pallas kernels for 31% -> 32%
where the time goes in v5:
time: 28.9 us; the launch traced here: 28.4 us
  Pallas kernels  15.3 us (53%)
  starting transfers between devices  9.08 us (31%)
  waiting for transfers between devices  2.24 us (8%)
  between operations  1.53 us (5%)
    pallas_call x1, Pallas kernels, interior(): pl.pallas_call(interior_kernel, in_specs=[pl.BlockSpec(memory_space=pl.AN...  7.54 us
    ppermute x1, starting transfers between devices, shards(): lower = lax.ppermute(last_rows, 'brick', upward)  3.53 us
    ppermute x1, starting transfers between devices, shards(): upper = lax.ppermute(first_rows, 'brick', downward)  3.34 us
    pallas_call x1, Pallas kernels, finish(): pl.pallas_call(functools.partial(finish_kernel, width=width), in_specs=[v...  2.92 us
    pallas_call x1, Pallas kernels, outer_rows(): pl.pallas_call(outer_kernel, in_specs=[pl.BlockSpec(memory_space=pltpu.HB...  2.26 us
    ppermute x3, waiting for transfers between devices, shards(): received.append(lax.ppermute(packed[k], 'shot', pairs))  2.24 us
    ppermute x3, starting transfers between devices, shards(): received.append(lax.ppermute(packed[k], 'shot', pairs))  2.21 us
    pallas_call x1, Pallas kernels, assemble(): pl.pallas_call(assemble_kernel, in_specs=[vmem] * 3, out_specs=[vmem] * 2...  1.66 us
  transfers between devices with their start and end apart: 5, of which 2 were waited for; matrix products, arithmetic and copies ran while one was open for 1% of the time, Pallas kernels for 32%

profile of v5, /device:TPU:16, one launch (start us, length us, event | category | flops | bytes accessed | tf_op | source)
XLA Modules:
  0.0 28.4 jit_solution(4387635176294862493)
XLA Ops:
  0.6 0.0 copy-start.5
  0.6 0.0 copy-start.6
  0.7 0.0 copy-start.7
  0.7 0.0 copy-start.8
  0.7 0.0 copy-start
  0.7 0.0 copy-start.1
  0.7 0.0 copy-start.2
  0.7 0.0 copy-start.3
  0.7 0.0 copy-start.11
  0.7 0.0 copy-start.10
  0.7 0.0 copy-start.9
  0.7 2.3 %outer_rows.1 = (bf16[160,512]{1,0:T(8,128)(2,1)}, bf16[160,512]{1,0:T(8,128)(2,1)}) custom-call(f32[8,4,4,8,128]{4,3,2,1,0:T(8,128)} %bitcast.21, f32[8,4,4,8,128]{4,3,2,1,0:T(8,128)} %bitcast.22, f32[8,4,4,8,128]{4,3,2,1,0:T(8,128)} %bitcast.23, f32[8,4,4,8,128]{4,3,2,1,0:T(8,128)} %bitcast.24, f32[32,512]{1,0:T(8,128)} %refs_4_.1, f32[32,512]{1,0:T(8,128)} %refs_5_.1, ...), custom_call_target="tpu_custom_call" | custom-call | tf_op jit(solution)/shard_map/outer_rows/pallas_call | solution.py:229
  3.0 0.0 copy-start.4
  3.0 3.5 %collective-permute-start = (bf16[160,512]{1,0:T(8,128)(2,1)}, bf16[160,512]{1,0:T(8,128)(2,1)S(1)}, u32[]{:S(2)}, u32[]{:S(2)}) collective-permute-start(bf16[160,512]{1,0:T(8,128)(2,1)} %get-tuple-element.25), channel_id=1, source_target_pairs={{0,1},{1,2},{2,3},{3,4},{4,5},{5,6},{6,7},{8,9},{9,10},{10,11},{11... | collective-permute-start | bytes 491528 | tf_op jit(solution)/shard_map/ppermute | solution.py:711
  6.6 3.3 %collective-permute-start.1 = (bf16[160,512]{1,0:T(8,128)(2,1)}, bf16[160,512]{1,0:T(8,128)(2,1)S(1)}, u32[]{:S(2)}, u32[]{:S(2)}) collective-permute-start(bf16[160,512]{1,0:T(8,128)(2,1)} %get-tuple-element.26), channel_id=1, source_target_pairs={{1,0},{2,1},{3,2},{4,3},{5,4},{6,5},{7,6},{9,8},{10,9},{11,10},{12... | collective-permute-start | bytes 491528 | tf_op jit(solution)/shard_map/ppermute | solution.py:712
  9.9 0.0 copy-done.11
  9.9 0.1 multiply_cosine_fusion
  10.0 0.0 copy-done.10
  10.1 0.0 copy-done.5
  10.1 0.0 copy-done.6
  10.1 0.0 copy-done.7
  10.1 0.0 copy-done.8
  10.1 0.0 copy-done
  10.1 0.0 copy-done.1
  10.1 0.0 copy-done.2
  10.1 0.0 copy-done.3
  10.1 0.0 copy-done.9
  10.2 7.5 %interior.1 = (f32[2,2,4,2,8,512]{5,4,3,2,1,0:T(8,128)S(1)}, f32[2,2,8,512]{3,2,1,0:T(8,128)S(1)}, f32[2,5,8,512]{3,2,1,0:T(8,128)S(1)}, f32[24,8,512]{2,1,0:T(8...) custom-call(f32[8,32,512]{2,1,0:T(8,128)S(1)} %copy-done, ...), custom_call_target="tpu_custom_call" | custom-call | flops 104857600 | bytes 8388608 | tf_op jit(solution)/shard_map/interior/pallas_call | solution.py:414
  17.7 0.1 pad_maximum_fusion
  17.8 0.0 collective-permute-done.lower_ref
  17.8 0.0 collective-permute-done.1.upper_ref
  17.8 0.1 broadcast_in_dim.2.table_ref
  17.9 0.0 copy-done.4
  17.9 2.9 %finish.1 = (f32[256,512]{1,0:T(8,128)}, f32[2,2,4,8,512]{4,3,2,1,0:T(8,128)S(1)}, f32[200,128]{1,0:T(8,128)S(1)}, f32[200,128]{1,0:T(8,128)S(1)}, f32[200,128]{1,0:T(8,128)S(1)}, /*index=5*/f32[200,128]{1,0:T(8,128)S(1)}) custom-call(bf16[160,512]{1,0:T(8,128)(2,1)S(1)} %collective-permute-done.lower_ref, ...), custom_call_target="tpu_custom_call" | custom-call | tf_op jit(solution)/shard_map/finish/pallas_call | solution.py:588
  20.8 1.6 %collective-permute-start.2 = (f32[200,128]{1,0:T(8,128)S(1)}, f32[200,128]{1,0:T(8,128)S(1)}, u32[]{:S(2)}, u32[]{:S(2)}) collective-permute-start(f32[200,128]{1,0:T(8,128)S(1)} %get-tuple-element.39), channel_id=1, source_target_pairs={{0,16},{8,24},{16,0},{24,8},{1,17},{9,25},{17,1},{25,9},{2,18},{10... | collective-permute-start | bytes 307208 | tf_op jit(solution)/shard_map/ppermute | solution.py:736
  22.4 0.0 collective-permute-start.3
  22.4 0.6 %collective-permute-start.4 = (f32[200,128]{1,0:T(8,128)S(1)}, f32[200,128]{1,0:T(8,128)S(1)}, u32[]{:S(2)}, u32[]{:S(2)}) collective-permute-start(f32[200,128]{1,0:T(8,128)S(1)} %get-tuple-element.41), channel_id=1, source_target_pairs={{0,8},{8,0},{16,24},{24,16},{1,9},{9,1},{17,25},{25,17},{2,10},{10... | collective-permute-start | bytes 307208 | tf_op jit(solution)/shard_map/ppermute | solution.py:736
  23.7 1.7 %assemble.1 = (f32[8,4,4,8,128]{4,3,2,1,0:T(8,128)}, f32[8,4,4,8,128]{4,3,2,1,0:T(8,128)}) custom-call(f32[24,8,512]{2,1,0:T(8,128)S(1)} %get-tuple-element.23.p_inner_ref, f32[24,8,512]{2,1,0:T(8,128)S(1)} %get-tuple-element.24.q_inner_ref, f32[2,2,4,8,512]{4,3,2,1,0:T(8,128)S(1)} %get-tuple-element.34.final_ref), custom_call_target="tpu_custom_call" | custom-call | flops 8388608 | bytes 4194304 | tf_op jit(solution)/shard_map/assemble/pallas_call | solution.py:636
  25.3 0.4 %collective-permute-done.2.refs_1_ = f32[200,128]{1,0:T(8,128)S(1)} collective-permute-done((f32[200,128]{1,0:T(8,128)S(1)}, f32[200,128]{1,0:T(8,128)S(1)}, u32[]{:S(2)}, u32[]{:S(2)}) %collective-permute-start.2) | collective-permute-done | bytes 102432 | tf_op jit(solution)/shard_map/ppermute | solution.py:736
  25.7 1.9 %collective-permute-done.3.refs_2_ = f32[200,128]{1,0:T(8,128)S(1)} collective-permute-done((f32[200,128]{1,0:T(8,128)S(1)}, f32[200,128]{1,0:T(8,128)S(1)}, u32[]{:S(2)}, u32[]{:S(2)}) %collective-permute-start.3) | collective-permute-done | bytes 102432 | tf_op jit(solution)/shard_map/ppermute | solution.py:736
  27.6 0.0 collective-permute-done.4.refs_3_
  27.6 0.9 %tiles.1 = f32[1,1,3,128,128]{4,3,2,1,0:T(8,128)} custom-call(s32[1,1]{1,0:T(1,128)S(6)} %copy.18.counts_ref, f32[200,128]{1,0:T(8,128)S(1)} %get-tuple-element.38.refs_0_, f32[200,128]{1,0:T(8,128)S(1)} %collective-permute-done.2.refs_1_, f32[200,128]{1,0:T(8,128)S(1)} %collective-permute-done.3.refs_2_, f32[200,128]{1,0:T(8,128)S(1)} %collective-permute-done.4.refs_3_), custom_call_target="tpu_custom_call" | custom-call | tf_op jit(solution)/shard_map/tiles/pallas_call | solution.py:675
  (2 shorter events, 0.0 us)
Async XLA Ops:
  0.6 9.4 %copy-start.5 = (f32[32,512]{1,0:T(8,128)S(1)}, f32[32,512]{1,0:T(8,128)}, u32[]{:S(2)}) copy-start(f32[32,512]{1,0:T(8,128)} %refs_4_.1) | copy-start | bytes 196612
  0.6 9.4 %copy-start.6 = (f32[32,512]{1,0:T(8,128)S(1)}, f32[32,512]{1,0:T(8,128)}, u32[]{:S(2)}) copy-start(f32[32,512]{1,0:T(8,128)} %refs_5_.1) | copy-start | bytes 196612
  0.7 9.4 %copy-start.7 = (f32[32,512]{1,0:T(8,128)S(1)}, f32[32,512]{1,0:T(8,128)}, u32[]{:S(2)}) copy-start(f32[32,512]{1,0:T(8,128)} %refs_6_.1) | copy-start | bytes 196612
  0.7 9.4 %copy-start.8 = (f32[32,512]{1,0:T(8,128)S(1)}, f32[32,512]{1,0:T(8,128)}, u32[]{:S(2)}) copy-start(f32[32,512]{1,0:T(8,128)} %refs_7_.1) | copy-start | bytes 196612
  0.7 9.4 %copy-start = (f32[8,32,512]{2,1,0:T(8,128)S(1)}, f32[8,32,512]{2,1,0:T(8,128)}, u32[]{:S(2)}) copy-start(f32[8,32,512]{2,1,0:T(8,128)} %p_ref.1) | copy-start | bytes 1572868
  0.7 9.4 %copy-start.1 = (f32[8,32,512]{2,1,0:T(8,128)S(1)}, f32[8,32,512]{2,1,0:T(8,128)}, u32[]{:S(2)}) copy-start(f32[8,32,512]{2,1,0:T(8,128)} %q_ref.1) | copy-start | bytes 1572868
  0.7 9.4 %copy-start.2 = (f32[8,32,512]{2,1,0:T(8,128)S(1)}, f32[8,32,512]{2,1,0:T(8,128)}, u32[]{:S(2)}) copy-start(f32[8,32,512]{2,1,0:T(8,128)} %pp_ref.1) | copy-start | bytes 1572868
  0.7 9.4 %copy-start.3 = (f32[8,32,512]{2,1,0:T(8,128)S(1)}, f32[8,32,512]{2,1,0:T(8,128)}, u32[]{:S(2)}) copy-start(f32[8,32,512]{2,1,0:T(8,128)} %qq_ref.1) | copy-start | bytes 1572868
  0.7 9.2 %copy-start.11 = (f32[16]{0:T(128)S(1)}, f32[16]{0:T(128)}, u32[]{:S(2)}) copy-start(f32[16]{0:T(128)} %param.21) | copy-start | bytes 196
  0.7 9.3 %copy-start.10 = (s32[1,4,3,128]{3,1,2,0:T(4,128)S(1)}, s32[1,4,3,128]{3,1,2,0:T(4,128)}, u32[]{:S(2)}) copy-start(s32[1,4,3,128]{3,1,2,0:T(4,128)} %param.24) | copy-start | bytes 18436
  0.7 9.4 %copy-start.9 = (s32[512]{0:T(512)S(1)}, s32[512]{0:T(512)}, u32[]{:S(2)}) copy-start(s32[512]{0:T(512)} %param.23) | copy-start | bytes 6148
  3.0 14.8 %copy-start.4 = (f32[8,32,512]{2,1,0:T(8,128)S(1)}, f32[8,32,512]{2,1,0:T(8,128)}, u32[]{:S(2)}) copy-start(f32[8,32,512]{2,1,0:T(8,128)} %param.22) | copy-start | bytes 1572868
  3.0 14.8 %collective-permute-start = (bf16[160,512]{1,0:T(8,128)(2,1)}, bf16[160,512]{1,0:T(8,128)(2,1)S(1)}, u32[]{:S(2)}, u32[]{:S(2)}) collective-permute-start(bf16[160,512]{1,0:T(8,128)(2,1)} %get-tuple-element.25), channel_id=1, source_target_pairs={{0,1},{1,2},{2,3},{3,4},{4,5},{5,6},{6,7},{8,9},{9,10},{10,11},{11... | collective-permute-start | bytes 491528 | tf_op jit(solution)/shard_map/ppermute | solution.py:711
  6.6 11.2 %collective-permute-start.1 = (bf16[160,512]{1,0:T(8,128)(2,1)}, bf16[160,512]{1,0:T(8,128)(2,1)S(1)}, u32[]{:S(2)}, u32[]{:S(2)}) collective-permute-start(bf16[160,512]{1,0:T(8,128)(2,1)} %get-tuple-element.26), channel_id=1, source_target_pairs={{1,0},{2,1},{3,2},{4,3},{5,4},{6,5},{7,6},{9,8},{10,9},{11,10},{12... | collective-permute-start | bytes 491528 | tf_op jit(solution)/shard_map/ppermute | solution.py:712
  20.8 4.9 %collective-permute-start.2 = (f32[200,128]{1,0:T(8,128)S(1)}, f32[200,128]{1,0:T(8,128)S(1)}, u32[]{:S(2)}, u32[]{:S(2)}) collective-permute-start(f32[200,128]{1,0:T(8,128)S(1)} %get-tuple-element.39), channel_id=1, source_target_pairs={{0,16},{8,24},{16,0},{24,8},{1,17},{9,25},{17,1},{25,9},{2,18},{10... | collective-permute-start | bytes 307208 | tf_op jit(solution)/shard_map/ppermute | solution.py:736
  22.4 5.2 %collective-permute-start.3 = (f32[200,128]{1,0:T(8,128)S(1)}, f32[200,128]{1,0:T(8,128)S(1)}, u32[]{:S(2)}, u32[]{:S(2)}) collective-permute-start(f32[200,128]{1,0:T(8,128)S(1)} %get-tuple-element.40), channel_id=1, source_target_pairs={{0,24},{8,16},{16,8},{24,0},{1,25},{9,17},{17,9},{25,1},{2,26},{10... | collective-permute-start | bytes 307208 | tf_op jit(solution)/shard_map/ppermute | solution.py:736
  22.4 5.2 %collective-permute-start.4 = (f32[200,128]{1,0:T(8,128)S(1)}, f32[200,128]{1,0:T(8,128)S(1)}, u32[]{:S(2)}, u32[]{:S(2)}) collective-permute-start(f32[200,128]{1,0:T(8,128)S(1)} %get-tuple-element.41), channel_id=1, source_target_pairs={{0,8},{8,0},{16,24},{24,16},{1,9},{9,1},{17,25},{25,17},{2,10},{10... | collective-permute-start | bytes 307208 | tf_op jit(solution)/shard_map/ppermute | solution.py:736

commit v6 on v5

--- a/solution.py
+++ b/solution.py
@@ -276,20 +276,16 @@
     level_ref,
     coef_ref,
     split_ref,
-    sems,
 ):
-    shots, width, depth = p_ref.shape
+    shots = p_ref.shape[0]
+    width, depth = courant_ref.shape
     along = depth // LANES
-    copies = []
-    for i, ref in enumerate((p_ref, q_ref, pp_ref, qq_ref)):
-        for s in range(shots):
-            copies.append(
-                pltpu.make_async_copy(
-                    ref.at[s], level_ref.at[1 - i // 2, i % 2, :, s], sems.at[i, s]
-                )
-            )
-    for copy in copies:
-        copy.start()
+    p_rows, q_rows, pp_rows, qq_rows = [ShotRows(ref) for ref in (p_ref, q_ref, pp_ref, qq_ref)]
+
+    @pl.loop(0, width, unroll=4)
+    def _(x):
+        level_ref[0, 0, x] = p_rows[x]
+        level_ref[0, 1, x] = q_rows[x]
 
     terms = tilt_coefficients(courant_ref[...], epsilon_ref[...], delta_ref[...], tilt_ref[...])
     for index, term in enumerate(terms):
@@ -330,12 +326,10 @@
                 lanes + jnp.int16(base) == wanted, one, zero
             )
 
-    for copy in copies:
-        copy.wait()
     for side in range(2):
         x = 0 if side == 0 else width - 1
-        prior_edge_ref[side, 0] = level_ref[0, 0, x]
-        prior_edge_ref[side, 1] = level_ref[0, 1, x]
+        prior_edge_ref[side, 0] = pp_rows[x]
+        prior_edge_ref[side, 1] = qq_rows[x]
 
     coefficients = CoefficientRows(coef_ref, shots)
     offsets = [0]
@@ -353,8 +347,8 @@
 
             def put(r, p_new, q_new):
                 if step < STEPS:
-                    level_ref[step + 1, 0, start + r] = p_new
-                    level_ref[step + 1, 1, start + r] = q_new
+                    level_ref[step, 0, start + r] = p_new
+                    level_ref[step, 1, start + r] = q_new
                 else:
                     p_inner_ref[at + r] = p_new
                     q_inner_ref[at + r] = q_new
@@ -368,10 +362,10 @@
 
             advance(
                 chunk,
-                lambda r: level_ref[step, 0, start + r],
-                lambda r: level_ref[step, 1, start + r],
                 lambda r: level_ref[step - 1, 0, start + r],
                 lambda r: level_ref[step - 1, 1, start + r],
+                lambda r: pp_rows[start + r] if step == 1 else level_ref[step - 2, 0, start + r],
+                lambda r: qq_rows[start + r] if step == 1 else level_ref[step - 2, 1, start + r],
                 lambda i, r, j: coefficients(i, start + r, j),
                 put,
             )
@@ -379,8 +373,8 @@
     for step in range(STEPS):
         for field in range(2):
             for near in range(2):
-                edge_ref[0, field, step, near] = level_ref[step + 1, field, step + near]
-                edge_ref[1, field, step, near] = level_ref[step + 1, field, width - 1 - step - near]
+                edge_ref[0, field, step, near] = level_ref[step, field, step + near]
+                edge_ref[1, field, step, near] = level_ref[step, field, width - 1 - step - near]
 
     found = jnp.dot(split_ref[...], depth_hot_ref[...], preferred_element_type=jnp.float32)
     totals = [jnp.zeros((shots, targets), jnp.float32) for _ in range(STEPS)]
@@ -395,7 +389,8 @@
 
 
 def interior(fields, params, target_cells, patch_lists):
-    shots, width, depth = fields[0].shape
+    shots = fields[0].shape[0]
+    width, depth = params[0].shape
     targets = target_cells.shape[0]
     _, owners, slots, patch = patch_lists.shape
     f32 = functools.partial(jax.ShapeDtypeStruct, dtype=jnp.float32)
@@ -413,14 +408,13 @@
     vmem = pl.BlockSpec(memory_space=pltpu.VMEM)
     return pl.pallas_call(
         interior_kernel,
-        in_specs=[pl.BlockSpec(memory_space=pl.ANY)] * 4 + [vmem] * 6,
+        in_specs=[vmem] * 10,
         out_specs=[vmem] * len(out_shape),
         out_shape=out_shape,
         scratch_shapes=[
-            pltpu.VMEM((STEPS + 1, 2, width, shots, depth), jnp.float32),
+            pltpu.VMEM((STEPS, 2, width, shots, depth), jnp.float32),
             pltpu.VMEM((5, depth // LANES, width, LANES), jnp.float32),
             pltpu.VMEM((STEPS * (width - STEPS - 1) * shots, 2 * depth), jnp.bfloat16),
-            pltpu.SemaphoreType.DMA((4, shots)),
         ],
         compiler_params=compiler_params(40),
         cost_estimate=pl.CostEstimate(
@@ -700,11 +694,11 @@
 ):
     shots, width, depth = pressure.shape
     _, owners, slots, patch = patch_lists.shape
-    fields = (pressure, auxiliary, pressure_prior, auxiliary_prior)
+    fields = [tiled(item) for item in (pressure, auxiliary, pressure_prior, auxiliary_prior)]
     params = (courant_sq, thomsen_epsilon, thomsen_delta, tilt_angle)
     parts, targets = spectra.shape[1:]
 
-    first_rows, last_rows = outer_rows([tiled(item) for item in fields], params)
+    first_rows, last_rows = outer_rows(fields, params)
     bricks = lax.axis_size("brick")
     upward = [(i, i + 1) for i in range(bricks - 1)]
     downward = [(i + 1, i) for i in range(bricks - 1)]

time: 28.9 us -> 27.9 us (0.965)
  Pallas kernels: 15.3 us -> 14.2 us
    pallas_call x1, Pallas kernels: 7.54 us -> 6.53 us  [interior(): pl.pallas_call(interior_kernel, in_specs=[vmem] * 10, out_specs=[vmem] *...]
  transfers between devices with their start and end apart: 5 -> 5, of which waited for: 2 -> 2; matrix products, arithmetic and copies ran while one was open for 1% -> 1% of each run, Pallas kernels for 32% -> 30%
where the time goes in v6:
time: 27.9 us; the launch traced here: 27.4 us
  Pallas kernels  14.2 us (51%)
  starting transfers between devices  9.08 us (33%)
  waiting for transfers between devices  2.24 us (8%)
  between operations  1.53 us (5%)
    pallas_call x1, Pallas kernels, interior(): pl.pallas_call(interior_kernel, in_specs=[vmem] * 10, out_specs=[vmem] *...  6.53 us
    ppermute x1, starting transfers between devices, shards(): lower = lax.ppermute(last_rows, 'brick', upward)  3.53 us
    ppermute x1, starting transfers between devices, shards(): upper = lax.ppermute(first_rows, 'brick', downward)  3.34 us
    pallas_call x1, Pallas kernels, finish(): pl.pallas_call(functools.partial(finish_kernel, width=width), in_specs=[v...  2.92 us
    pallas_call x1, Pallas kernels, outer_rows(): pl.pallas_call(outer_kernel, in_specs=[pl.BlockSpec(memory_space=pltpu.HB...  2.25 us
    ppermute x3, waiting for transfers between devices, shards(): received.append(lax.ppermute(packed[k], 'shot', pairs))  2.24 us
    ppermute x3, starting transfers between devices, shards(): received.append(lax.ppermute(packed[k], 'shot', pairs))  2.21 us
    pallas_call x1, Pallas kernels, assemble(): pl.pallas_call(assemble_kernel, in_specs=[vmem] * 3, out_specs=[vmem] * 2...  1.66 us
  transfers between devices with their start and end apart: 5, of which 2 were waited for; matrix products, arithmetic and copies ran while one was open for 1% of the time, Pallas kernels for 30%

profile of v6, /device:TPU:16, one launch (start us, length us, event | category | flops | bytes accessed | tf_op | source)
XLA Modules:
  0.0 27.4 jit_solution(974717376022881852)
XLA Ops:
  0.6 0.0 copy-start
  0.6 0.0 copy-start.1
  0.7 0.0 copy-start.2
  0.7 0.0 copy-start.3
  0.7 0.0 copy-start.5
  0.7 0.0 copy-start.6
  0.7 0.0 copy-start.7
  0.7 0.0 copy-start.8
  0.7 0.0 copy-start.11
  0.7 0.0 copy-start.10
  0.7 0.0 copy-start.9
  0.7 2.2 %outer_rows.1 = (bf16[160,512]{1,0:T(8,128)(2,1)}, bf16[160,512]{1,0:T(8,128)(2,1)}) custom-call(f32[8,4,4,8,128]{4,3,2,1,0:T(8,128)} %bitcast.21, f32[8,4,4,8,128]{4,3,2,1,0:T(8,128)} %bitcast.23, f32[8,4,4,8,128]{4,3,2,1,0:T(8,128)} %bitcast.25, f32[8,4,4,8,128]{4,3,2,1,0:T(8,128)} %bitcast.27, f32[32,512]{1,0:T(8,128)} %refs_4_.1, f32[32,512]{1,0:T(8,128)} %refs_5_.1, ...), custom_call_target="tpu_custom_call" | custom-call | tf_op jit(solution)/shard_map/outer_rows/pallas_call | solution.py:229
  3.0 0.0 copy-start.4
  3.0 3.5 %collective-permute-start = (bf16[160,512]{1,0:T(8,128)(2,1)}, bf16[160,512]{1,0:T(8,128)(2,1)S(1)}, u32[]{:S(2)}, u32[]{:S(2)}) collective-permute-start(bf16[160,512]{1,0:T(8,128)(2,1)} %get-tuple-element.25), channel_id=1, source_target_pairs={{0,1},{1,2},{2,3},{3,4},{4,5},{5,6},{6,7},{8,9},{9,10},{10,11},{11... | collective-permute-start | bytes 491528 | tf_op jit(solution)/shard_map/ppermute | solution.py:705
  6.6 3.3 %collective-permute-start.1 = (bf16[160,512]{1,0:T(8,128)(2,1)}, bf16[160,512]{1,0:T(8,128)(2,1)S(1)}, u32[]{:S(2)}, u32[]{:S(2)}) collective-permute-start(bf16[160,512]{1,0:T(8,128)(2,1)} %get-tuple-element.26), channel_id=1, source_target_pairs={{1,0},{2,1},{3,2},{4,3},{5,4},{6,5},{7,6},{9,8},{10,9},{11,10},{12... | collective-permute-start | bytes 491528 | tf_op jit(solution)/shard_map/ppermute | solution.py:706
  9.9 0.0 copy-done.11
  9.9 0.1 multiply_cosine_fusion
  10.0 0.0 copy-done.10
  10.1 0.0 copy-done
  10.1 0.0 copy-done.1
  10.1 0.0 copy-done.2
  10.1 0.0 copy-done.3
  10.1 0.0 copy-done.5
  10.1 0.0 copy-done.6
  10.1 0.0 copy-done.7
  10.1 0.0 copy-done.8
  10.1 0.0 copy-done.9
  10.1 6.5 %interior.1 = (f32[2,2,4,2,8,512]{5,4,3,2,1,0:T(8,128)S(1)}, f32[2,2,8,512]{3,2,1,0:T(8,128)S(1)}, f32[2,5,8,512]{3,2,1,0:T(8,128)S(1)}, f32[24,8,512]{2,1,0:T(8...) custom-call(f32[8,4,4,8,128]{4,3,2,1,0:T(8,128)S(1)} %bitcast.22, ...), custom_call_target="tpu_custom_call" | custom-call | flops 104857600 | bytes 8388608 | tf_op jit(solution)/shard_map/interior/pallas_call | solution.py:409
  16.7 0.1 pad_maximum_fusion
  16.8 0.0 collective-permute-done.lower_ref
  16.8 0.0 collective-permute-done.1.upper_ref
  16.8 0.1 broadcast_in_dim.2.table_ref
  16.8 0.0 copy-done.4
  16.8 2.9 %finish.1 = (f32[256,512]{1,0:T(8,128)}, f32[2,2,4,8,512]{4,3,2,1,0:T(8,128)S(1)}, f32[200,128]{1,0:T(8,128)S(1)}, f32[200,128]{1,0:T(8,128)S(1)}, f32[200,128]{1,0:T(8,128)S(1)}, /*index=5*/f32[200,128]{1,0:T(8,128)S(1)}) custom-call(bf16[160,512]{1,0:T(8,128)(2,1)S(1)} %collective-permute-done.lower_ref, ...), custom_call_target="tpu_custom_call" | custom-call | tf_op jit(solution)/shard_map/finish/pallas_call | solution.py:582
  19.8 1.6 %collective-permute-start.2 = (f32[200,128]{1,0:T(8,128)S(1)}, f32[200,128]{1,0:T(8,128)S(1)}, u32[]{:S(2)}, u32[]{:S(2)}) collective-permute-start(f32[200,128]{1,0:T(8,128)S(1)} %get-tuple-element.39), channel_id=1, source_target_pairs={{0,16},{8,24},{16,0},{24,8},{1,17},{9,25},{17,1},{25,9},{2,18},{10... | collective-permute-start | bytes 307208 | tf_op jit(solution)/shard_map/ppermute | solution.py:730
  21.4 0.0 collective-permute-start.3
  21.4 0.6 %collective-permute-start.4 = (f32[200,128]{1,0:T(8,128)S(1)}, f32[200,128]{1,0:T(8,128)S(1)}, u32[]{:S(2)}, u32[]{:S(2)}) collective-permute-start(f32[200,128]{1,0:T(8,128)S(1)} %get-tuple-element.41), channel_id=1, source_target_pairs={{0,8},{8,0},{16,24},{24,16},{1,9},{9,1},{17,25},{25,17},{2,10},{10... | collective-permute-start | bytes 307208 | tf_op jit(solution)/shard_map/ppermute | solution.py:730
  22.6 1.7 %assemble.1 = (f32[8,4,4,8,128]{4,3,2,1,0:T(8,128)}, f32[8,4,4,8,128]{4,3,2,1,0:T(8,128)}) custom-call(f32[24,8,512]{2,1,0:T(8,128)S(1)} %get-tuple-element.23.p_inner_ref, f32[24,8,512]{2,1,0:T(8,128)S(1)} %get-tuple-element.24.q_inner_ref, f32[2,2,4,8,512]{4,3,2,1,0:T(8,128)S(1)} %get-tuple-element.34.final_ref), custom_call_target="tpu_custom_call" | custom-call | flops 8388608 | bytes 4194304 | tf_op jit(solution)/shard_map/assemble/pallas_call | solution.py:630
  24.3 0.4 %collective-permute-done.2.refs_1_ = f32[200,128]{1,0:T(8,128)S(1)} collective-permute-done((f32[200,128]{1,0:T(8,128)S(1)}, f32[200,128]{1,0:T(8,128)S(1)}, u32[]{:S(2)}, u32[]{:S(2)}) %collective-permute-start.2) | collective-permute-done | bytes 102432 | tf_op jit(solution)/shard_map/ppermute | solution.py:730
  24.7 1.9 %collective-permute-done.3.refs_2_ = f32[200,128]{1,0:T(8,128)S(1)} collective-permute-done((f32[200,128]{1,0:T(8,128)S(1)}, f32[200,128]{1,0:T(8,128)S(1)}, u32[]{:S(2)}, u32[]{:S(2)}) %collective-permute-start.3) | collective-permute-done | bytes 102432 | tf_op jit(solution)/shard_map/ppermute | solution.py:730
  26.5 0.0 collective-permute-done.4.refs_3_
  26.5 0.9 %tiles.1 = f32[1,1,3,128,128]{4,3,2,1,0:T(8,128)} custom-call(s32[1,1]{1,0:T(1,128)S(6)} %copy.18.counts_ref, f32[200,128]{1,0:T(8,128)S(1)} %get-tuple-element.38.refs_0_, f32[200,128]{1,0:T(8,128)S(1)} %collective-permute-done.2.refs_1_, f32[200,128]{1,0:T(8,128)S(1)} %collective-permute-done.3.refs_2_, f32[200,128]{1,0:T(8,128)S(1)} %collective-permute-done.4.refs_3_), custom_call_target="tpu_custom_call" | custom-call | tf_op jit(solution)/shard_map/tiles/pallas_call | solution.py:669
  (2 shorter events, 0.0 us)
Async XLA Ops:
  0.6 9.4 %copy-start = (f32[8,32,512]{2,1,0:T(8,128)S(1)}, f32[8,32,512]{2,1,0:T(8,128)}, u32[]{:S(2)}) copy-start(f32[8,32,512]{2,1,0:T(8,128)} %param.13) | copy-start | bytes 1572868
  0.6 9.4 %copy-start.1 = (f32[8,32,512]{2,1,0:T(8,128)S(1)}, f32[8,32,512]{2,1,0:T(8,128)}, u32[]{:S(2)}) copy-start(f32[8,32,512]{2,1,0:T(8,128)} %param.14) | copy-start | bytes 1572868
  0.7 9.4 %copy-start.2 = (f32[8,32,512]{2,1,0:T(8,128)S(1)}, f32[8,32,512]{2,1,0:T(8,128)}, u32[]{:S(2)}) copy-start(f32[8,32,512]{2,1,0:T(8,128)} %param.15) | copy-start | bytes 1572868
  0.7 9.4 %copy-start.3 = (f32[8,32,512]{2,1,0:T(8,128)S(1)}, f32[8,32,512]{2,1,0:T(8,128)}, u32[]{:S(2)}) copy-start(f32[8,32,512]{2,1,0:T(8,128)} %param.16) | copy-start | bytes 1572868
  0.7 9.4 %copy-start.5 = (f32[32,512]{1,0:T(8,128)S(1)}, f32[32,512]{1,0:T(8,128)}, u32[]{:S(2)}) copy-start(f32[32,512]{1,0:T(8,128)} %refs_4_.1) | copy-start | bytes 196612
  0.7 9.4 %copy-start.6 = (f32[32,512]{1,0:T(8,128)S(1)}, f32[32,512]{1,0:T(8,128)}, u32[]{:S(2)}) copy-start(f32[32,512]{1,0:T(8,128)} %refs_5_.1) | copy-start | bytes 196612
  0.7 9.4 %copy-start.7 = (f32[32,512]{1,0:T(8,128)S(1)}, f32[32,512]{1,0:T(8,128)}, u32[]{:S(2)}) copy-start(f32[32,512]{1,0:T(8,128)} %refs_6_.1) | copy-start | bytes 196612
  0.7 9.4 %copy-start.8 = (f32[32,512]{1,0:T(8,128)S(1)}, f32[32,512]{1,0:T(8,128)}, u32[]{:S(2)}) copy-start(f32[32,512]{1,0:T(8,128)} %refs_7_.1) | copy-start | bytes 196612
  0.7 9.2 %copy-start.11 = (f32[16]{0:T(128)S(1)}, f32[16]{0:T(128)}, u32[]{:S(2)}) copy-start(f32[16]{0:T(128)} %param.21) | copy-start | bytes 196
  0.7 9.3 %copy-start.10 = (s32[1,4,3,128]{3,1,2,0:T(4,128)S(1)}, s32[1,4,3,128]{3,1,2,0:T(4,128)}, u32[]{:S(2)}) copy-start(s32[1,4,3,128]{3,1,2,0:T(4,128)} %param.24) | copy-start | bytes 18436
  0.7 9.4 %copy-start.9 = (s32[512]{0:T(512)S(1)}, s32[512]{0:T(512)}, u32[]{:S(2)}) copy-start(s32[512]{0:T(512)} %param.23) | copy-start | bytes 6148
  3.0 13.8 %copy-start.4 = (f32[8,32,512]{2,1,0:T(8,128)S(1)}, f32[8,32,512]{2,1,0:T(8,128)}, u32[]{:S(2)}) copy-start(f32[8,32,512]{2,1,0:T(8,128)} %param.22) | copy-start | bytes 1572868
  3.0 13.7 %collective-permute-start = (bf16[160,512]{1,0:T(8,128)(2,1)}, bf16[160,512]{1,0:T(8,128)(2,1)S(1)}, u32[]{:S(2)}, u32[]{:S(2)}) collective-permute-start(bf16[160,512]{1,0:T(8,128)(2,1)} %get-tuple-element.25), channel_id=1, source_target_pairs={{0,1},{1,2},{2,3},{3,4},{4,5},{5,6},{6,7},{8,9},{9,10},{10,11},{11... | collective-permute-start | bytes 491528 | tf_op jit(solution)/shard_map/ppermute | solution.py:705
  6.6 10.2 %collective-permute-start.1 = (bf16[160,512]{1,0:T(8,128)(2,1)}, bf16[160,512]{1,0:T(8,128)(2,1)S(1)}, u32[]{:S(2)}, u32[]{:S(2)}) collective-permute-start(bf16[160,512]{1,0:T(8,128)(2,1)} %get-tuple-element.26), channel_id=1, source_target_pairs={{1,0},{2,1},{3,2},{4,3},{5,4},{6,5},{7,6},{9,8},{10,9},{11,10},{12... | collective-permute-start | bytes 491528 | tf_op jit(solution)/shard_map/ppermute | solution.py:706
  19.8 4.9 %collective-permute-start.2 = (f32[200,128]{1,0:T(8,128)S(1)}, f32[200,128]{1,0:T(8,128)S(1)}, u32[]{:S(2)}, u32[]{:S(2)}) collective-permute-start(f32[200,128]{1,0:T(8,128)S(1)} %get-tuple-element.39), channel_id=1, source_target_pairs={{0,16},{8,24},{16,0},{24,8},{1,17},{9,25},{17,1},{25,9},{2,18},{10... | collective-permute-start | bytes 307208 | tf_op jit(solution)/shard_map/ppermute | solution.py:730
  21.4 5.2 %collective-permute-start.3 = (f32[200,128]{1,0:T(8,128)S(1)}, f32[200,128]{1,0:T(8,128)S(1)}, u32[]{:S(2)}, u32[]{:S(2)}) collective-permute-start(f32[200,128]{1,0:T(8,128)S(1)} %get-tuple-element.40), channel_id=1, source_target_pairs={{0,24},{8,16},{16,8},{24,0},{1,25},{9,17},{17,9},{25,1},{2,26},{10... | collective-permute-start | bytes 307208 | tf_op jit(solution)/shard_map/ppermute | solution.py:730
  21.4 5.2 %collective-permute-start.4 = (f32[200,128]{1,0:T(8,128)S(1)}, f32[200,128]{1,0:T(8,128)S(1)}, u32[]{:S(2)}, u32[]{:S(2)}) collective-permute-start(f32[200,128]{1,0:T(8,128)S(1)} %get-tuple-element.41), channel_id=1, source_target_pairs={{0,8},{8,0},{16,24},{24,16},{1,9},{9,1},{17,25},{25,17},{2,10},{10... | collective-permute-start | bytes 307208 | tf_op jit(solution)/shard_map/ppermute | solution.py:730

commit v7 on v6

--- a/solution.py
+++ b/solution.py
@@ -176,30 +176,10 @@
             )
     for copy in copies:
         copy.start()
+    tiles_by_side = []
     for side in range(2):
         for copy in copies[8 * side : 8 * side + 8]:
             copy.wait()
-        views = [ShotRows(field_ref.at[side, i]) for i in range(4)]
-        out = outs[side]
-
-        def row(field, distance):
-            place = distance if side == 0 else tile - 1 - distance
-            return views[field][place]
-
-        position = 0
-
-        def put(first, second):
-            nonlocal position
-            out[pl.ds(position, 2 * shots), :] = jnp.concatenate([first, second], 0).astype(
-                jnp.bfloat16
-            )
-            position += 2 * shots
-
-        for field in range(4):
-            near = row(field, 0)
-            put(near, near - near.astype(jnp.bfloat16).astype(jnp.float32))
-        for first, second in far_items():
-            put(row(*first), row(*second))
         terms = tilt_coefficients(*[param_ref[side, i] for i in range(4)])
         rows = []
         for index, term in enumerate(terms):
@@ -209,7 +189,41 @@
                 rows.append(term[place : place + 1, :])
         while len(rows) < 2 * shots:
             rows.append(jnp.zeros((1, depth), jnp.float32))
-        out[pl.ds(position, 2 * shots), :] = jnp.concatenate(rows, 0).astype(jnp.bfloat16)
+        tiles_by_side.append(jnp.concatenate(rows, 0))
+
+    stride = along * tile
+    flat = field_ref.reshape(2 * 4 * shots * stride, lanes)
+    for turn in range(2):
+        side = outer_side(turn)
+        out = outs[turn]
+
+        def row(field, distance):
+            base = (side * 4 + field) * shots * stride + distance + side * (tile - 1 - 2 * distance)
+            return jnp.concatenate(
+                [flat[pl.ds(base + j * tile, shots, stride=stride), :] for j in range(along)], 1
+            )
+
+        position = 0
+
+        def put(first, second):
+            nonlocal position
+            out[pl.ds(position, 2 * shots), :] = jnp.concatenate([first, second], 0).astype(
+                jnp.bfloat16
+            )
+            position += 2 * shots
+
+        for field in range(4):
+            near = row(field, 0)
+            put(near, near - near.astype(jnp.bfloat16).astype(jnp.float32))
+        for first, second in far_items():
+            put(row(*first), row(*second))
+        out[pl.ds(position, 2 * shots), :] = jnp.where(
+            side == 1, tiles_by_side[1], tiles_by_side[0]
+        ).astype(jnp.bfloat16)
+
+
+def outer_side(turn):
+    return jnp.where(lax.axis_index("brick") % 2 == turn, 1, 0)
 
 
 def far_items():
@@ -425,8 +439,8 @@
 
 
 def finish_kernel(
-    lower_ref,
-    upper_ref,
+    even_ref,
+    odd_ref,
     edge_ref,
     prior_edge_ref,
     coef_edge_ref,
@@ -447,7 +461,8 @@
     targets = column_ref.shape[1]
     first = -STEPS
     pair = 2 * shots
-    for side, ref in enumerate((lower_ref, upper_ref)):
+    for turn, ref in enumerate((even_ref, odd_ref)):
+        side = outer_side(turn)
         for field in range(4):
             both = ref[pl.ds(field * pair, pair), :].astype(jnp.float32)
             value = both[:shots] + both[shots:]
@@ -466,12 +481,13 @@
         params = ref[pl.ds((4 + len(far_items())) * pair, pair), :].astype(jnp.float32)
         for index in range(5):
             far = params[index * (STEPS - 1) : (index + 1) * (STEPS - 1)]
+            for j, block in enumerate(blocks(far)):
+                coef_ref[side, index, j, pl.ds(0, STEPS - 1), :] = block
+    for side in range(2):
+        for index in range(5):
             near = coef_edge_ref[side, index, pl.ds(0, STEPS), :]
-            for j in range(depth // LANES):
-                coef_ref[side, index, j, pl.ds(0, STEPS - 1), :] = far[:, j * LANES : (j + 1) * LANES]
-                coef_ref[side, index, j, pl.ds(STEPS - 1, STEPS), :] = near[
-                    :, j * LANES : (j + 1) * LANES
-                ]
+            for j, block in enumerate(blocks(near)):
+                coef_ref[side, index, j, pl.ds(STEPS - 1, STEPS), :] = block
         for field in range(2):
             prior_ref[side, field, STEPS - 1] = prior_edge_ref[side, field]
             for step in range(STEPS):
@@ -566,7 +582,7 @@
     out_copy.wait()
 
 
-def finish(lower, upper, inner, spectra, table, width, owners, slots, patch):
+def finish(even, odd, inner, spectra, table, width, owners, slots, patch):
     edge, prior_edge, coef_edge, sample, depth_hot, column, list_hot = inner
     shots, depth = edge.shape[-2:]
     targets = column.shape[1]
@@ -595,8 +611,8 @@
         compiler_params=compiler_params(40),
         name="finish",
     )(
-        lower,
-        upper,
+        even,
+        odd,
         edge,
         prior_edge,
         coef_edge,
@@ -698,12 +714,14 @@
     params = (courant_sq, thomsen_epsilon, thomsen_delta, tilt_angle)
     parts, targets = spectra.shape[1:]
 
-    first_rows, last_rows = outer_rows(fields, params)
     bricks = lax.axis_size("brick")
-    upward = [(i, i + 1) for i in range(bricks - 1)]
-    downward = [(i + 1, i) for i in range(bricks - 1)]
-    lower = lax.ppermute(last_rows, "brick", upward)
-    upper = lax.ppermute(first_rows, "brick", downward)
+    swapped = []
+    for turn, rows in enumerate(outer_rows(fields, params)):
+        pairs = []
+        for i in range(turn, bricks - 1, 2):
+            pairs += [(i, i + 1), (i + 1, i)]
+        swapped.append(lax.ppermute(rows, "brick", pairs))
+    even, odd = swapped
 
     moments = jnp.arange(1, STEPS + 1, dtype=jnp.float32)
     angle = frequencies[None, :] * moments[:, None]
@@ -714,8 +732,8 @@
         fields, params, target_cells, patch_lists
     )
     spectra_out, final, *packed = finish(
-        lower,
-        upper,
+        even,
+        odd,
         (edge, prior_edge, coef_edge, sample, depth_hot, column, list_hot),
         spectra.reshape(shots * parts, targets),
         table,

time: 27.9 us -> 26.2 us (0.939)
  the two profiles are of different devices: /device:TPU:16 before, /device:TPU:11 now
where the time goes in v7:
time: 26.2 us; the launch traced here: 26 us
  Pallas kernels  14.4 us (55%)
  starting transfers between devices  7.36 us (28%)
  waiting for transfers between devices  2.36 us (9%)
  between operations  1.52 us (6%)
    pallas_call x1, Pallas kernels, interior(): pl.pallas_call(interior_kernel, in_specs=[vmem] * 10, out_specs=[vmem] *...  6.53 us
    ppermute x2, starting transfers between devices, shards(): swapped.append(lax.ppermute(rows, 'brick', pairs))  4.44 us
    pallas_call x1, Pallas kernels, finish(): pl.pallas_call(functools.partial(finish_kernel, width=width), in_specs=[v...  2.96 us
    ppermute x3, starting transfers between devices, shards(): received.append(lax.ppermute(packed[k], 'shot', pairs))  2.92 us
    pallas_call x1, Pallas kernels, outer_rows(): pl.pallas_call(outer_kernel, in_specs=[pl.BlockSpec(memory_space=pltpu.HB...  2.38 us
    ppermute x3, waiting for transfers between devices, shards(): received.append(lax.ppermute(packed[k], 'shot', pairs))  2.36 us
    pallas_call x1, Pallas kernels, assemble(): pl.pallas_call(assemble_kernel, in_specs=[vmem] * 3, out_specs=[vmem] * 2...  1.66 us
    pallas_call x1, Pallas kernels, tiles(): pl.pallas_call(functools.partial(tiles_kernel, features=features), in_spe...  0.88 us
  transfers between devices with their start and end apart: 5, of which 1 were waited for; matrix products, arithmetic and copies ran while one was open for 1% of the time, Pallas kernels for 31%

profile of v7, /device:TPU:11, one launch (start us, length us, event | category | flops | bytes accessed | tf_op | source)
XLA Modules:
  0.0 26.0 jit_solution(6526907311692291535)
XLA Ops:
  0.6 0.0 copy-start
  0.6 0.0 copy-start.1
  0.7 0.0 copy-start.2
  0.7 0.0 copy-start.3
  0.7 0.0 copy-start.5
  0.7 0.0 copy-start.6
  0.7 0.0 copy-start.7
  0.7 0.0 copy-start.8
  0.7 0.0 copy-start.11
  0.7 0.0 copy-start.10
  0.7 0.0 copy-start.9
  0.7 2.4 %outer_rows.1 = (bf16[160,512]{1,0:T(8,128)(2,1)}, bf16[160,512]{1,0:T(8,128)(2,1)}) custom-call(f32[8,4,4,8,128]{4,3,2,1,0:T(8,128)} %bitcast.21, f32[8,4,4,8,128]{4,3,2,1,0:T(8,128)} %bitcast.23, f32[8,4,4,8,128]{4,3,2,1,0:T(8,128)} %bitcast.25, f32[8,4,4,8,128]{4,3,2,1,0:T(8,128)} %bitcast.27, f32[32,512]{1,0:T(8,128)} %refs_4_.1, f32[32,512]{1,0:T(8,128)} %refs_5_.1, ...), custom_call_target="tpu_custom_call" | custom-call | tf_op jit(solution)/shard_map/outer_rows/pallas_call | solution.py:243
  3.1 0.0 copy-start.4
  3.1 0.3 %collective-permute-start = (bf16[160,512]{1,0:T(8,128)(2,1)}, bf16[160,512]{1,0:T(8,128)(2,1)S(1)}, u32[]{:S(2)}, u32[]{:S(2)}) collective-permute-start(bf16[160,512]{1,0:T(8,128)(2,1)} %get-tuple-element.25), channel_id=1, source_target_pairs={{0,1},{1,0},{2,3},{3,2},{4,5},{5,4},{6,7},{7,6},{8,9},{9,8},{10,11... | collective-permute-start | bytes 491528 | tf_op jit(solution)/shard_map/ppermute | solution.py:723
  3.5 4.1 %collective-permute-start.1 = (bf16[160,512]{1,0:T(8,128)(2,1)}, bf16[160,512]{1,0:T(8,128)(2,1)S(1)}, u32[]{:S(2)}, u32[]{:S(2)}) collective-permute-start(bf16[160,512]{1,0:T(8,128)(2,1)} %get-tuple-element.26), channel_id=1, source_target_pairs={{1,2},{2,1},{3,4},{4,3},{5,6},{6,5},{9,10},{10,9},{11,12},{12,11},... | collective-permute-start | bytes 491528 | tf_op jit(solution)/shard_map/ppermute | solution.py:723
  7.6 0.0 copy-done.11
  7.6 0.1 multiply_cosine_fusion
  7.7 0.0 copy-done.10
  7.7 0.0 copy-done
  7.8 0.0 copy-done.1
  7.8 0.0 copy-done.2
  7.8 0.0 copy-done.3
  7.8 0.0 copy-done.5
  7.8 0.0 copy-done.6
  7.8 0.0 copy-done.7
  7.8 0.0 copy-done.8
  7.8 0.0 copy-done.9
  7.8 6.5 %interior.1 = (f32[2,2,4,2,8,512]{5,4,3,2,1,0:T(8,128)S(1)}, f32[2,2,8,512]{3,2,1,0:T(8,128)S(1)}, f32[2,5,8,512]{3,2,1,0:T(8,128)S(1)}, f32[24,8,512]{2,1,0:T(8...) custom-call(f32[8,4,4,8,128]{4,3,2,1,0:T(8,128)S(1)} %bitcast.22, ...), custom_call_target="tpu_custom_call" | custom-call | flops 104857600 | bytes 8388608 | tf_op jit(solution)/shard_map/interior/pallas_call | solution.py:423
  14.4 0.1 pad_maximum_fusion
  14.4 0.0 collective-permute-done.even_ref
  14.5 0.0 collective-permute-done.1.odd_ref
  14.5 0.1 broadcast_in_dim.2.table_ref
  14.5 0.0 copy-done.4
  14.5 3.0 %finish.1 = (f32[256,512]{1,0:T(8,128)}, f32[2,2,4,8,512]{4,3,2,1,0:T(8,128)S(1)}, f32[200,128]{1,0:T(8,128)S(1)}, f32[200,128]{1,0:T(8,128)S(1)}, f32[200,128]{1,0:T(8,128)S(1)}, /*index=5*/f32[200,128]{1,0:T(8,128)S(1)}) custom-call(bf16[160,512]{1,0:T(8,128)(2,1)S(1)} %collective-permute-done.even_ref, ...), custom_call_target="tpu_custom_call" | custom-call | tf_op jit(solution)/shard_map/finish/pallas_call | solution.py:598
  17.5 1.3 %collective-permute-start.2 = (f32[200,128]{1,0:T(8,128)S(1)}, f32[200,128]{1,0:T(8,128)S(1)}, u32[]{:S(2)}, u32[]{:S(2)}) collective-permute-start(f32[200,128]{1,0:T(8,128)S(1)} %get-tuple-element.39), channel_id=1, source_target_pairs={{0,16},{8,24},{16,0},{24,8},{1,17},{9,25},{17,1},{25,9},{2,18},{10... | collective-permute-start | bytes 307208 | tf_op jit(solution)/shard_map/ppermute | solution.py:748
  18.8 1.6 %collective-permute-start.3 = (f32[200,128]{1,0:T(8,128)S(1)}, f32[200,128]{1,0:T(8,128)S(1)}, u32[]{:S(2)}, u32[]{:S(2)}) collective-permute-start(f32[200,128]{1,0:T(8,128)S(1)} %get-tuple-element.40), channel_id=1, source_target_pairs={{0,24},{8,16},{16,8},{24,0},{1,25},{9,17},{17,9},{25,1},{2,26},{10... | collective-permute-start | bytes 307208 | tf_op jit(solution)/shard_map/ppermute | solution.py:748
  20.4 0.0 collective-permute-start.4
  21.1 1.7 %assemble.1 = (f32[8,4,4,8,128]{4,3,2,1,0:T(8,128)}, f32[8,4,4,8,128]{4,3,2,1,0:T(8,128)}) custom-call(f32[24,8,512]{2,1,0:T(8,128)S(1)} %get-tuple-element.23.p_inner_ref, f32[24,8,512]{2,1,0:T(8,128)S(1)} %get-tuple-element.24.q_inner_ref, f32[2,2,4,8,512]{4,3,2,1,0:T(8,128)S(1)} %get-tuple-element.34.final_ref), custom_call_target="tpu_custom_call" | custom-call | flops 8388608 | bytes 4194304 | tf_op jit(solution)/shard_map/assemble/pallas_call | solution.py:646
  22.7 0.0 collective-permute-done.2.refs_1_
  22.7 2.4 %collective-permute-done.3.refs_2_ = f32[200,128]{1,0:T(8,128)S(1)} collective-permute-done((f32[200,128]{1,0:T(8,128)S(1)}, f32[200,128]{1,0:T(8,128)S(1)}, u32[]{:S(2)}, u32[]{:S(2)}) %collective-permute-start.3) | collective-permute-done | bytes 102432 | tf_op jit(solution)/shard_map/ppermute | solution.py:748
  25.1 0.0 collective-permute-done.4.refs_3_
  25.1 0.9 %tiles.1 = f32[1,1,3,128,128]{4,3,2,1,0:T(8,128)} custom-call(s32[1,1]{1,0:T(1,128)S(6)} %copy.18.counts_ref, f32[200,128]{1,0:T(8,128)S(1)} %get-tuple-element.38.refs_0_, f32[200,128]{1,0:T(8,128)S(1)} %collective-permute-done.2.refs_1_, f32[200,128]{1,0:T(8,128)S(1)} %collective-permute-done.3.refs_2_, f32[200,128]{1,0:T(8,128)S(1)} %collective-permute-done.4.refs_3_), custom_call_target="tpu_custom_call" | custom-call | tf_op jit(solution)/shard_map/tiles/pallas_call | solution.py:685
  (2 shorter events, 0.0 us)
Async XLA Ops:
  0.6 7.1 %copy-start = (f32[8,32,512]{2,1,0:T(8,128)S(1)}, f32[8,32,512]{2,1,0:T(8,128)}, u32[]{:S(2)}) copy-start(f32[8,32,512]{2,1,0:T(8,128)} %param.13) | copy-start | bytes 1572868
  0.6 7.1 %copy-start.1 = (f32[8,32,512]{2,1,0:T(8,128)S(1)}, f32[8,32,512]{2,1,0:T(8,128)}, u32[]{:S(2)}) copy-start(f32[8,32,512]{2,1,0:T(8,128)} %param.14) | copy-start | bytes 1572868
  0.7 7.1 %copy-start.2 = (f32[8,32,512]{2,1,0:T(8,128)S(1)}, f32[8,32,512]{2,1,0:T(8,128)}, u32[]{:S(2)}) copy-start(f32[8,32,512]{2,1,0:T(8,128)} %param.15) | copy-start | bytes 1572868
  0.7 7.1 %copy-start.3 = (f32[8,32,512]{2,1,0:T(8,128)S(1)}, f32[8,32,512]{2,1,0:T(8,128)}, u32[]{:S(2)}) copy-start(f32[8,32,512]{2,1,0:T(8,128)} %param.16) | copy-start | bytes 1572868
  0.7 7.1 %copy-start.5 = (f32[32,512]{1,0:T(8,128)S(1)}, f32[32,512]{1,0:T(8,128)}, u32[]{:S(2)}) copy-start(f32[32,512]{1,0:T(8,128)} %refs_4_.1) | copy-start | bytes 196612
  0.7 7.1 %copy-start.6 = (f32[32,512]{1,0:T(8,128)S(1)}, f32[32,512]{1,0:T(8,128)}, u32[]{:S(2)}) copy-start(f32[32,512]{1,0:T(8,128)} %refs_5_.1) | copy-start | bytes 196612
  0.7 7.1 %copy-start.7 = (f32[32,512]{1,0:T(8,128)S(1)}, f32[32,512]{1,0:T(8,128)}, u32[]{:S(2)}) copy-start(f32[32,512]{1,0:T(8,128)} %refs_6_.1) | copy-start | bytes 196612
  0.7 7.1 %copy-start.8 = (f32[32,512]{1,0:T(8,128)S(1)}, f32[32,512]{1,0:T(8,128)}, u32[]{:S(2)}) copy-start(f32[32,512]{1,0:T(8,128)} %refs_7_.1) | copy-start | bytes 196612
  0.7 6.9 %copy-start.11 = (f32[16]{0:T(128)S(1)}, f32[16]{0:T(128)}, u32[]{:S(2)}) copy-start(f32[16]{0:T(128)} %param.21) | copy-start | bytes 196
  0.7 7.0 %copy-start.10 = (s32[1,4,3,128]{3,1,2,0:T(4,128)S(1)}, s32[1,4,3,128]{3,1,2,0:T(4,128)}, u32[]{:S(2)}) copy-start(s32[1,4,3,128]{3,1,2,0:T(4,128)} %param.24) | copy-start | bytes 18436
  0.7 7.1 %copy-start.9 = (s32[512]{0:T(512)S(1)}, s32[512]{0:T(512)}, u32[]{:S(2)}) copy-start(s32[512]{0:T(512)} %param.23) | copy-start | bytes 6148
  3.1 11.4 %copy-start.4 = (f32[8,32,512]{2,1,0:T(8,128)S(1)}, f32[8,32,512]{2,1,0:T(8,128)}, u32[]{:S(2)}) copy-start(f32[8,32,512]{2,1,0:T(8,128)} %param.22) | copy-start | bytes 1572868
  3.1 11.3 %collective-permute-start = (bf16[160,512]{1,0:T(8,128)(2,1)}, bf16[160,512]{1,0:T(8,128)(2,1)S(1)}, u32[]{:S(2)}, u32[]{:S(2)}) collective-permute-start(bf16[160,512]{1,0:T(8,128)(2,1)} %get-tuple-element.25), channel_id=1, source_target_pairs={{0,1},{1,0},{2,3},{3,2},{4,5},{5,4},{6,7},{7,6},{8,9},{9,8},{10,11... | collective-permute-start | bytes 491528 | tf_op jit(solution)/shard_map/ppermute | solution.py:723
  3.5 11.0 %collective-permute-start.1 = (bf16[160,512]{1,0:T(8,128)(2,1)}, bf16[160,512]{1,0:T(8,128)(2,1)S(1)}, u32[]{:S(2)}, u32[]{:S(2)}) collective-permute-start(bf16[160,512]{1,0:T(8,128)(2,1)} %get-tuple-element.26), channel_id=1, source_target_pairs={{1,2},{2,1},{3,4},{4,3},{5,6},{6,5},{9,10},{10,9},{11,12},{12,11},... | collective-permute-start | bytes 491528 | tf_op jit(solution)/shard_map/ppermute | solution.py:723
  17.5 5.2 %collective-permute-start.2 = (f32[200,128]{1,0:T(8,128)S(1)}, f32[200,128]{1,0:T(8,128)S(1)}, u32[]{:S(2)}, u32[]{:S(2)}) collective-permute-start(f32[200,128]{1,0:T(8,128)S(1)} %get-tuple-element.39), channel_id=1, source_target_pairs={{0,16},{8,24},{16,0},{24,8},{1,17},{9,25},{17,1},{25,9},{2,18},{10... | collective-permute-start | bytes 307208 | tf_op jit(solution)/shard_map/ppermute | solution.py:748
  18.8 6.3 %collective-permute-start.3 = (f32[200,128]{1,0:T(8,128)S(1)}, f32[200,128]{1,0:T(8,128)S(1)}, u32[]{:S(2)}, u32[]{:S(2)}) collective-permute-start(f32[200,128]{1,0:T(8,128)S(1)} %get-tuple-element.40), channel_id=1, source_target_pairs={{0,24},{8,16},{16,8},{24,0},{1,25},{9,17},{17,9},{25,1},{2,26},{10... | collective-permute-start | bytes 307208 | tf_op jit(solution)/shard_map/ppermute | solution.py:748
  20.4 4.7 %collective-permute-start.4 = (f32[200,128]{1,0:T(8,128)S(1)}, f32[200,128]{1,0:T(8,128)S(1)}, u32[]{:S(2)}, u32[]{:S(2)}) collective-permute-start(f32[200,128]{1,0:T(8,128)S(1)} %get-tuple-element.41), channel_id=1, source_target_pairs={{0,8},{8,0},{16,24},{24,16},{1,9},{9,1},{17,25},{25,17},{2,10},{10... | collective-permute-start | bytes 307208 | tf_op jit(solution)/shard_map/ppermute | solution.py:748

commit v8 on v7

--- a/solution.py
+++ b/solution.py
@@ -151,75 +151,67 @@
     return high, low
 
 
+def pack_message(out, side, row, terms):
+    size, depth = out.shape
+    pair = size // (len(far_items()) + 5)
+    items = []
+    for field in range(4):
+        near = row(field, 0)
+        items.append((near, near - near.astype(jnp.bfloat16).astype(jnp.float32)))
+    for first, second in far_items():
+        items.append((row(*first), row(*second)))
+    for position, both in enumerate(items):
+        out[pl.ds(position * pair, pair), :] = jnp.concatenate(both, 0).astype(jnp.bfloat16)
+    lines = []
+    for index, term in enumerate(terms):
+        last = term.shape[0] - 1
+        for distance in reversed(range(STEPS - 1)):
+            low = term[distance : distance + 1, :]
+            high = term[last - distance : last - distance + 1, :]
+            lines.append(jnp.where(side == 1, high, -low if index == 1 else low))
+    while len(lines) < pair:
+        lines.append(jnp.zeros((1, depth), jnp.float32))
+    out[pl.ds(len(items) * pair, pair), :] = jnp.concatenate(lines, 0).astype(jnp.bfloat16)
+
+
+def message_shape(shots, depth):
+    return jax.ShapeDtypeStruct((2 * shots * (len(far_items()) + 5), depth), jnp.bfloat16)
+
+
 def outer_kernel(*refs):
-    sources, outs, (field_ref, param_ref, field_sem, param_sem) = refs[:8], refs[8:10], refs[10:]
+    sources, out, (field_ref, param_ref, field_sem, param_sem) = refs[:8], refs[8], refs[9:]
     shots, across, along, tile, lanes = sources[0].shape
-    depth = along * lanes
+    side = outer_side(0)
+    place = side * (across - 1)
     copies = []
-    for side in range(2):
-        place = side * (across - 1)
-        for i in range(4):
-            copies.append(
-                pltpu.make_async_copy(
-                    sources[i].at[:, pl.ds(place, 1), :, pl.ds(side * STEPS, STEPS)],
-                    field_ref.at[side, i, :, :, :, pl.ds(side * STEPS, STEPS)],
-                    field_sem.at[side, i],
-                )
+    for i in range(4):
+        copies.append(
+            pltpu.make_async_copy(
+                sources[4 + i].at[pl.ds(pl.multiple_of(place * tile, tile), tile)],
+                param_ref.at[i],
+                param_sem.at[i],
             )
-        for i in range(4):
-            copies.append(
-                pltpu.make_async_copy(
-                    sources[4 + i].at[pl.ds(place * tile, tile)],
-                    param_ref.at[side, i],
-                    param_sem.at[side, i],
-                )
+        )
+    for i in range(4):
+        copies.append(
+            pltpu.make_async_copy(
+                sources[i].at[:, pl.ds(place, 1)], field_ref.at[i], field_sem.at[i]
             )
+        )
     for copy in copies:
         copy.start()
-    tiles_by_side = []
-    for side in range(2):
-        for copy in copies[8 * side : 8 * side + 8]:
-            copy.wait()
-        terms = tilt_coefficients(*[param_ref[side, i] for i in range(4)])
-        rows = []
-        for index, term in enumerate(terms):
-            term = -term if index == 1 and side == 0 else term
-            for distance in reversed(range(STEPS - 1)):
-                place = distance if side == 0 else tile - 1 - distance
-                rows.append(term[place : place + 1, :])
-        while len(rows) < 2 * shots:
-            rows.append(jnp.zeros((1, depth), jnp.float32))
-        tiles_by_side.append(jnp.concatenate(rows, 0))
-
-    stride = along * tile
-    flat = field_ref.reshape(2 * 4 * shots * stride, lanes)
-    for turn in range(2):
-        side = outer_side(turn)
-        out = outs[turn]
-
-        def row(field, distance):
-            base = (side * 4 + field) * shots * stride + distance + side * (tile - 1 - 2 * distance)
-            return jnp.concatenate(
-                [flat[pl.ds(base + j * tile, shots, stride=stride), :] for j in range(along)], 1
-            )
-
-        position = 0
-
-        def put(first, second):
-            nonlocal position
-            out[pl.ds(position, 2 * shots), :] = jnp.concatenate([first, second], 0).astype(
-                jnp.bfloat16
-            )
-            position += 2 * shots
-
-        for field in range(4):
-            near = row(field, 0)
-            put(near, near - near.astype(jnp.bfloat16).astype(jnp.float32))
-        for first, second in far_items():
-            put(row(*first), row(*second))
-        out[pl.ds(position, 2 * shots), :] = jnp.where(
-            side == 1, tiles_by_side[1], tiles_by_side[0]
-        ).astype(jnp.bfloat16)
+    for copy in copies[:4]:
+        copy.wait()
+    terms = tilt_coefficients(*[param_ref[i] for i in range(4)])
+    for copy in copies[4:]:
+        copy.wait()
+    views = [ShotRows(field_ref.at[i]) for i in range(4)]
+    pack_message(
+        out,
+        side,
+        lambda field, distance: views[field][distance + side * (tile - 1 - 2 * distance)],
+        terms,
+    )
 
 
 def outer_side(turn):
@@ -238,18 +230,16 @@
 def outer_rows(fields, params):
     shots, across, along, tile, lanes = fields[0].shape
     depth = along * lanes
-    rows = 2 * shots * (4 + len(far_items()) + 1)
-    shape = jax.ShapeDtypeStruct((rows, depth), jnp.bfloat16)
     return pl.pallas_call(
         outer_kernel,
         in_specs=[pl.BlockSpec(memory_space=pltpu.HBM)] * 8,
-        out_specs=[pl.BlockSpec(memory_space=pltpu.VMEM)] * 2,
-        out_shape=[shape, shape],
+        out_specs=pl.BlockSpec(memory_space=pltpu.VMEM),
+        out_shape=message_shape(shots, depth),
         scratch_shapes=[
-            pltpu.VMEM((2, 4, shots, 1, along, tile, lanes), jnp.float32),
-            pltpu.VMEM((2, 4, tile, depth), jnp.float32),
-            pltpu.SemaphoreType.DMA((2, 4)),
-            pltpu.SemaphoreType.DMA((2, 4)),
+            pltpu.VMEM((4, shots, 1, along, tile, lanes), jnp.float32),
+            pltpu.VMEM((4, tile, depth), jnp.float32),
+            pltpu.SemaphoreType.DMA((4,)),
+            pltpu.SemaphoreType.DMA((4,)),
         ],
         compiler_params=compiler_params(60),
         name="outer_rows",
@@ -267,7 +257,40 @@
     return jnp.dot(jnp.concatenate([high, low], 1), one_hot, preferred_element_type=jnp.float32)
 
 
-def interior_kernel(
+def run_step(step, width, level, prior, coefficients, put_row, split_ref, offset):
+    low, high = step, width - step
+    chunk = 8 if (high - low) % 8 == 0 else 10
+    here = level(step - 1)
+    shots, depth = here.shape[-2:]
+
+    @pl.loop(0, -(-(high - low) // chunk))
+    def _(index):
+        at = jnp.minimum(chunk * index, high - low - chunk)
+        start = low + at
+        held = []
+
+        def put(r, p_new, q_new):
+            put_row(start + r, p_new, q_new)
+            held.append(p_new)
+            if len(held) == 2:
+                first, rest = split_bf16(jnp.concatenate(held, 0))
+                place = pl.multiple_of((offset + at + r - 1) * shots, 2 * shots)
+                split_ref[pl.ds(place, 2 * shots), pl.ds(0, depth)] = first
+                split_ref[pl.ds(place, 2 * shots), pl.ds(depth, depth)] = rest
+                held.clear()
+
+        advance(
+            chunk,
+            lambda r: here[0, start + r],
+            lambda r: here[1, start + r],
+            lambda r: prior(0, start + r),
+            lambda r: prior(1, start + r),
+            lambda i, r, j: coefficients(i, start + r, j),
+            put,
+        )
+
+
+def begin_kernel(
     p_ref,
     q_ref,
     pp_ref,
@@ -278,12 +301,10 @@
     tilt_ref,
     cells_ref,
     lists_ref,
-    edge_ref,
+    sent_ref,
+    message_ref,
     prior_edge_ref,
     coef_edge_ref,
-    p_inner_ref,
-    q_inner_ref,
-    sample_ref,
     depth_hot_ref,
     column_ref,
     list_hot_ref,
@@ -345,97 +366,156 @@
         prior_edge_ref[side, 0] = pp_rows[x]
         prior_edge_ref[side, 1] = qq_rows[x]
 
+    views = (p_rows, q_rows, pp_rows, qq_rows)
+    side = outer_side(1)
+    pack_message(
+        message_ref,
+        side,
+        lambda field, distance: views[field][distance + side * (width - 1 - 2 * distance)],
+        terms,
+    )
+
+    def put_row(x, p_new, q_new):
+        level_ref[1, 0, x] = p_new
+        level_ref[1, 1, x] = q_new
+
+    run_step(
+        1,
+        width,
+        lambda m: level_ref.at[m],
+        lambda field, x: views[2 + field][x],
+        CoefficientRows(coef_ref, shots),
+        put_row,
+        split_ref,
+        0,
+    )
+
+
+def begin(fields, params, target_cells, patch_lists, sent):
+    shots = fields[0].shape[0]
+    width, depth = params[0].shape
+    targets = target_cells.shape[0]
+    _, owners, slots, patch = patch_lists.shape
+    f32 = functools.partial(jax.ShapeDtypeStruct, dtype=jnp.float32)
+    bf16 = functools.partial(jax.ShapeDtypeStruct, dtype=jnp.bfloat16)
+    out_shape = [
+        message_shape(shots, depth),
+        f32((2, 2, shots, depth)),
+        f32((2, 5, 8, depth)),
+        bf16((2 * depth, targets)),
+        jax.ShapeDtypeStruct((1, targets), jnp.int32),
+        bf16((owners * slots * patch, targets)),
+        f32((2, 2, width, shots, depth)),
+        f32((5, depth // LANES, width, LANES)),
+        bf16(((width - 2) * shots, 2 * depth)),
+    ]
+    vmem = pl.BlockSpec(memory_space=pltpu.VMEM)
+    return pl.pallas_call(
+        begin_kernel,
+        in_specs=[vmem] * 10 + [pl.BlockSpec(memory_space=pl.ANY)],
+        out_specs=[vmem] * len(out_shape),
+        out_shape=out_shape,
+        compiler_params=compiler_params(32),
+        cost_estimate=pl.CostEstimate(
+            flops=4000 * STEPS * shots * width * depth, bytes_accessed=32 * MIB, transcendentals=0
+        ),
+        name="begin",
+    )(*fields, *params, target_cells.reshape(1, targets), patch_lists, sent)
+
+
+def interior_kernel(
+    begun_ref,
+    coef_ref,
+    begun_split_ref,
+    depth_hot_ref,
+    column_ref,
+    received_ref,
+    edge_ref,
+    p_inner_ref,
+    q_inner_ref,
+    sample_ref,
+    level_ref,
+    split_ref,
+):
+    width, shots, depth = begun_ref.shape[2:]
+    targets = column_ref.shape[1]
+
+    def level(m):
+        return begun_ref.at[m] if m < 2 else level_ref.at[m - 2]
+
     coefficients = CoefficientRows(coef_ref, shots)
-    offsets = [0]
-    for step in range(1, STEPS + 1):
-        low, high = step, width - step
-        chunk = 8 if (high - low) % 8 == 0 else 10
-        offset = offsets[-1]
-        offsets.append(offset + high - low)
-
-        @pl.loop(0, -(-(high - low) // chunk))
-        def _(index):
-            at = jnp.minimum(chunk * index, high - low - chunk)
-            start = low + at
-            held = []
-
-            def put(r, p_new, q_new):
-                if step < STEPS:
-                    level_ref[step, 0, start + r] = p_new
-                    level_ref[step, 1, start + r] = q_new
-                else:
-                    p_inner_ref[at + r] = p_new
-                    q_inner_ref[at + r] = q_new
-                held.append(p_new)
-                if len(held) == 2:
-                    first, rest = split_bf16(jnp.concatenate(held, 0))
-                    place = pl.multiple_of((offset + at + r - 1) * shots, 2 * shots)
-                    split_ref[pl.ds(place, 2 * shots), pl.ds(0, depth)] = first
-                    split_ref[pl.ds(place, 2 * shots), pl.ds(depth, depth)] = rest
-                    held.clear()
-
-            advance(
-                chunk,
-                lambda r: level_ref[step - 1, 0, start + r],
-                lambda r: level_ref[step - 1, 1, start + r],
-                lambda r: pp_rows[start + r] if step == 1 else level_ref[step - 2, 0, start + r],
-                lambda r: qq_rows[start + r] if step == 1 else level_ref[step - 2, 1, start + r],
-                lambda i, r, j: coefficients(i, start + r, j),
-                put,
-            )
+    offsets = [0, 0]
+    for step in range(2, STEPS + 1):
+
+        def put_row(x, p_new, q_new):
+            if step < STEPS:
+                level(step)[0, x] = p_new
+                level(step)[1, x] = q_new
+            else:
+                p_inner_ref[x - STEPS] = p_new
+                q_inner_ref[x - STEPS] = q_new
+
+        run_step(
+            step,
+            width,
+            level,
+            lambda field, x: level(step - 2)[field, x],
+            coefficients,
+            put_row,
+            split_ref,
+            offsets[-1],
+        )
+        offsets.append(offsets[-1] + width - 2 * step)
 
     for step in range(STEPS):
         for field in range(2):
             for near in range(2):
-                edge_ref[0, field, step, near] = level_ref[step, field, step + near]
-                edge_ref[1, field, step, near] = level_ref[step, field, width - 1 - step - near]
-
-    found = jnp.dot(split_ref[...], depth_hot_ref[...], preferred_element_type=jnp.float32)
+                edge_ref[0, field, step, near] = level(step)[field, step + near]
+                edge_ref[1, field, step, near] = level(step)[field, width - 1 - step - near]
+
+    hot = depth_hot_ref[...]
+    first = jnp.dot(begun_split_ref[...], hot, preferred_element_type=jnp.float32)
+    found = jnp.dot(split_ref[...], hot, preferred_element_type=jnp.float32)
+    column = column_ref[...]
     totals = [jnp.zeros((shots, targets), jnp.float32) for _ in range(STEPS)]
     for x in range(1, width - 1):
         here = column == x
         for step in range(1, STEPS + 1):
             if step <= x < width - step:
                 row = (offsets[step - 1] + x - step) * shots
-                totals[step - 1] += jnp.where(here, found[row : row + shots], 0.0)
+                value = (first if step == 1 else found)[row : row + shots]
+                totals[step - 1] += jnp.where(here, value, 0.0)
     for step in range(STEPS):
         sample_ref[step] = totals[step]
 
 
-def interior(fields, params, target_cells, patch_lists):
-    shots = fields[0].shape[0]
-    width, depth = params[0].shape
-    targets = target_cells.shape[0]
-    _, owners, slots, patch = patch_lists.shape
+def interior(begun, coef, begun_split, depth_hot, column, received):
+    width, shots, depth = begun.shape[2:]
+    targets = column.shape[1]
     f32 = functools.partial(jax.ShapeDtypeStruct, dtype=jnp.float32)
     out_shape = [
         f32((2, 2, STEPS, 2, shots, depth)),
-        f32((2, 2, shots, depth)),
-        f32((2, 5, 8, depth)),
         f32((width - 2 * STEPS, shots, depth)),
         f32((width - 2 * STEPS, shots, depth)),
         f32((STEPS, shots, targets)),
-        jax.ShapeDtypeStruct((2 * depth, targets), jnp.bfloat16),
-        jax.ShapeDtypeStruct((1, targets), jnp.int32),
-        jax.ShapeDtypeStruct((owners * slots * patch, targets), jnp.bfloat16),
     ]
+    rows = sum(width - 2 * step for step in range(2, STEPS + 1))
     vmem = pl.BlockSpec(memory_space=pltpu.VMEM)
     return pl.pallas_call(
         interior_kernel,
-        in_specs=[vmem] * 10,
+        in_specs=[vmem] * 5 + [pl.BlockSpec(memory_space=pl.ANY)],
         out_specs=[vmem] * len(out_shape),
         out_shape=out_shape,
         scratch_shapes=[
-            pltpu.VMEM((STEPS, 2, width, shots, depth), jnp.float32),
-            pltpu.VMEM((5, depth // LANES, width, LANES), jnp.float32),
-            pltpu.VMEM((STEPS * (width - STEPS - 1) * shots, 2 * depth), jnp.bfloat16),
+            pltpu.VMEM((STEPS - 2, 2, width, shots, depth), jnp.float32),
+            pltpu.VMEM((rows * shots, 2 * depth), jnp.bfloat16),
         ],
-        compiler_params=compiler_params(40),
+        compiler_params=compiler_params(32),
         cost_estimate=pl.CostEstimate(
-            flops=200 * STEPS * shots * width * depth, bytes_accessed=8 * MIB, transcendentals=0
+            flops=MIB, bytes_accessed=MIB, transcendentals=0
         ),
         name="interior",
-    )(*fields, *params, target_cells.reshape(1, targets), patch_lists)
+    )(begun, coef, begun_split, depth_hot, column, received)
 
 
 def finish_kernel(
@@ -715,22 +795,26 @@
     parts, targets = spectra.shape[1:]
 
     bricks = lax.axis_size("brick")
-    swapped = []
-    for turn, rows in enumerate(outer_rows(fields, params)):
+
+    def swap(rows, turn):
         pairs = []
         for i in range(turn, bricks - 1, 2):
             pairs += [(i, i + 1), (i + 1, i)]
-        swapped.append(lax.ppermute(rows, "brick", pairs))
-    even, odd = swapped
+        return lax.ppermute(rows, "brick", pairs)
+
+    rows = outer_rows(fields, params)
+    even = swap(rows, 0)
+    message, prior_edge, coef_edge, depth_hot, column, list_hot, *begun = begin(
+        fields, params, target_cells, patch_lists, rows
+    )
+    odd = swap(message, 1)
+    edge, p_inner, q_inner, sample = interior(*begun, depth_hot, column, even)
 
     moments = jnp.arange(1, STEPS + 1, dtype=jnp.float32)
     angle = frequencies[None, :] * moments[:, None]
     table = jnp.concatenate([jnp.cos(angle), -jnp.sin(angle)], 1)
     table = jnp.broadcast_to(table[:, :, None], (STEPS, parts, 128))
 
-    edge, prior_edge, coef_edge, p_inner, q_inner, sample, depth_hot, column, list_hot = interior(
-        fields, params, target_cells, patch_lists
-    )
     spectra_out, final, *packed = finish(
         even,
         odd,

time: 26.2 us -> 27.6 us (1.053)
  the two profiles are of different devices: /device:TPU:11 before, /device:TPU:16 now
where the time goes in v8:
time: 27.6 us; the launch traced here: 27.1 us
  Pallas kernels  14.2 us (51%)
  starting transfers between devices  6.09 us (22%)
  waiting for transfers between devices  4.11 us (15%)
  between operations  1.51 us (5%)
  local copies, waits for them, and re-layouts  1.04 us (4%)
    pallas_call x1, Pallas kernels, interior(): pl.pallas_call(interior_kernel, in_specs=[vmem] * 5 + [pl.BlockSpec(memor...  4.02 us
    ppermute x2, starting transfers between devices, swap(): return lax.ppermute(rows, 'brick', pairs)  3.89 us
    pallas_call x1, Pallas kernels, finish(): pl.pallas_call(functools.partial(finish_kernel, width=width), in_specs=[v...  2.93 us
    pallas_call x1, Pallas kernels, begin(): pl.pallas_call(begin_kernel, in_specs=[vmem] * 10 + [pl.BlockSpec(memory_...  2.49 us
    ppermute x3, waiting for transfers between devices, shards(): received.append(lax.ppermute(packed[k], 'shot', pairs))  2.24 us
    ppermute x3, starting transfers between devices, shards(): received.append(lax.ppermute(packed[k], 'shot', pairs))  2.21 us
    pallas_call x1, Pallas kernels, outer_rows(): pl.pallas_call(outer_kernel, in_specs=[pl.BlockSpec(memory_space=pltpu.HB...  2.17 us
    ppermute x2, waiting for transfers between devices, swap(): return lax.ppermute(rows, 'brick', pairs)  1.87 us
  transfers between devices with their start and end apart: 5, of which 3 were waited for; matrix products, arithmetic and copies ran while one was open for 1% of the time, Pallas kernels for 30%

profile of v8, /device:TPU:16, one launch (start us, length us, event | category | flops | bytes accessed | tf_op | source)
XLA Modules:
  0.0 27.1 jit_solution(16141234577746224111)
XLA Ops:
  0.6 0.0 copy-start
  0.6 0.0 copy-start.1
  0.7 0.0 copy-start.2
  0.7 0.0 copy-start.3
  0.7 0.0 copy-start.6
  0.7 0.0 copy-start.7
  0.7 0.0 copy-start.8
  0.7 0.0 copy-start.9
  0.7 0.0 copy-start.11
  0.7 0.0 copy-start.10
  0.7 2.2 %outer_rows.1.sent_ref = bf16[160,512]{1,0:T(8,128)(2,1)} custom-call(f32[8,4,4,8,128]{4,3,2,1,0:T(8,128)} %bitcast.21, f32[8,4,4,8,128]{4,3,2,1,0:T(8,128)} %bitcast.23, f32[8,4,4,8,128]{4,3,2,1,0:T(8,128)} %bitcast.25, f32[8,4,4,8,128]{4,3,2,1,0:T(8,128)} %bitcast.27, f32[32,512]{1,0:T(8,128)} %courant_ref.1, f32[32,512]{1,0:T(8,128)} %epsilon_ref.1, ...), custom_call_target="tpu_custom_call" | custom-call | tf_op jit(solution)/shard_map/outer_rows/pallas_call | solution.py:233
  2.9 1.6 %collective-permute-start = (bf16[160,512]{1,0:T(8,128)(2,1)}, bf16[160,512]{1,0:T(8,128)(2,1)S(1)}, u32[]{:S(2)}, u32[]{:S(2)}) collective-permute-start(bf16[160,512]{1,0:T(8,128)(2,1)} %outer_rows.1.sent_ref), channel_id=1, source_target_pairs={{0,1},{1,0},{2,3},{3,2},{4,5},{5,4},{6,7},{7,6},{8,9},{9,8},{10,11... | collective-permute-start | bytes 491528 | tf_op jit(solution)/shard_map/ppermute | solution.py:803
  4.5 0.0 copy-done.11
  4.5 0.0 copy-done
  4.5 0.0 copy-done.1
  4.5 0.0 copy-done.2
  4.5 0.0 copy-done.3
  4.5 0.0 copy-done.6
  4.5 0.0 copy-done.7
  4.5 0.0 copy-done.8
  4.5 0.0 copy-done.9
  4.6 0.0 copy-done.10
  4.6 0.0 copy-start.5
  4.6 0.9 %copy-done.5 = bf16[160,512]{1,0:T(8,128)(2,1)S(1)} copy-done((bf16[160,512]{1,0:T(8,128)(2,1)S(1)}, bf16[160,512]{1,0:T(8,128)(2,1)}, u32[]{:S(2)}) %copy-start.5) | copy-done | bytes 163864
  5.5 0.0 copy-start.12
  5.5 2.5 %begin.1 = (bf16[160,512]{1,0:T(8,128)(2,1)S(1)}, f32[2,2,8,512]{3,2,1,0:T(8,128)S(1)}, f32[2,5,8,512]{3,2,1,0:T(8,128)S(1)}, bf16[1024,512]{1,0:T(8,128)(2,1)S(...) custom-call(f32[8,4,4,8,128]{4,3,2,1,0:T(8,128)S(1)} %bitcast.22, ...), custom_call_target="tpu_custom_call" | custom-call | flops 2097152000 | bytes 33554432 | tf_op jit(solution)/shard_map/begin/pallas_call | solution.py:413
  8.0 2.3 %collective-permute-start.1 = (bf16[160,512]{1,0:T(8,128)(2,1)S(1)}, bf16[160,512]{1,0:T(8,128)(2,1)S(1)}, u32[]{:S(2)}, u32[]{:S(2)}) collective-permute-start(bf16[160,512]{1,0:T(8,128)(2,1)S(1)} %get-tuple-element.32), channel_id=1, source_target_pairs={{1,2},{2,1},{3,4},{4,3},{5,6},{6,5},{9,10},{10,9},{11,12},{12,11},... | collective-permute-start | bytes 491528 | tf_op jit(solution)/shard_map/ppermute | solution.py:803
  10.3 0.0 copy-done.12
  10.3 0.1 multiply_cosine_fusion
  10.5 0.1 pad_maximum_fusion
  10.5 0.0 collective-permute-done.received_ref.even_ref
  10.5 0.0 copy-start.4
  10.5 4.0 %interior.1 = (f32[2,2,4,2,8,512]{5,4,3,2,1,0:T(8,128)S(1)}, f32[24,8,512]{2,1,0:T(8,128)S(1)}, f32[24,8,512]{2,1,0:T(8,128)S(1)}, f32[4,8,512]{2,1,0:T(8,128)S(1)}) custom-call(f32[2,2,32,8,512]{4,3,2,1,0:T(8,128)S(1)} %get-tuple-element.25.begun_ref, f32[5,4,32,128]{3,2,1,0:T(8,128)S(1)} %get-tuple-element.26.coef_ref, ...), custom_call_target="tpu_custom_call" | custom-call | flops 1048576 | bytes 1048576 | tf_op jit(solution)/shard_map/interior/pallas_call | solution.py:504
  14.6 1.9 %collective-permute-done.1.odd_ref = bf16[160,512]{1,0:T(8,128)(2,1)S(1)} collective-permute-done((bf16[160,512]{1,0:T(8,128)(2,1)S(1)}, bf16[160,512]{1,0:T(8,128)(2,1)S(1)}, u32[]{:S(2)}, u32[]{:S(2)}) %collective-permute-start.1) | collective-permute-done | bytes 163872 | tf_op jit(solution)/shard_map/ppermute | solution.py:803
  16.4 0.1 broadcast_in_dim.2.table_ref
  16.5 0.0 copy-done.4
  16.5 2.9 %finish.1 = (f32[256,512]{1,0:T(8,128)}, f32[2,2,4,8,512]{4,3,2,1,0:T(8,128)S(1)}, f32[200,128]{1,0:T(8,128)S(1)}, f32[200,128]{1,0:T(8,128)S(1)}, f32[200,128]{1,0:T(8,128)S(1)}, /*index=5*/f32[200,128]{1,0:T(8,128)S(1)}) custom-call(bf16[160,512]{1,0:T(8,128)(2,1)S(1)} %collective-permute-done.received_ref.even_ref, ...), custom_call_target="tpu_custom_call" | custom-call | tf_op jit(solution)/shard_map/finish/pallas_call | solution.py:678
  19.5 1.6 %collective-permute-start.2 = (f32[200,128]{1,0:T(8,128)S(1)}, f32[200,128]{1,0:T(8,128)S(1)}, u32[]{:S(2)}, u32[]{:S(2)}) collective-permute-start(f32[200,128]{1,0:T(8,128)S(1)} %get-tuple-element.43), channel_id=1, source_target_pairs={{0,16},{8,24},{16,0},{24,8},{1,17},{9,25},{17,1},{25,9},{2,18},{10... | collective-permute-start | bytes 307208 | tf_op jit(solution)/shard_map/ppermute | solution.py:832
  21.0 0.0 collective-permute-start.3
  21.0 0.6 %collective-permute-start.4 = (f32[200,128]{1,0:T(8,128)S(1)}, f32[200,128]{1,0:T(8,128)S(1)}, u32[]{:S(2)}, u32[]{:S(2)}) collective-permute-start(f32[200,128]{1,0:T(8,128)S(1)} %get-tuple-element.45), channel_id=1, source_target_pairs={{0,8},{8,0},{16,24},{24,16},{1,9},{9,1},{17,25},{25,17},{2,10},{10... | collective-permute-start | bytes 307208 | tf_op jit(solution)/shard_map/ppermute | solution.py:832
  22.3 1.7 %assemble.1 = (f32[8,4,4,8,128]{4,3,2,1,0:T(8,128)}, f32[8,4,4,8,128]{4,3,2,1,0:T(8,128)}) custom-call(f32[24,8,512]{2,1,0:T(8,128)S(1)} %get-tuple-element.30.p_inner_ref, f32[24,8,512]{2,1,0:T(8,128)S(1)} %get-tuple-element.31.q_inner_ref, f32[2,2,4,8,512]{4,3,2,1,0:T(8,128)S(1)} %get-tuple-element.38.final_ref), custom_call_target="tpu_custom_call" | custom-call | flops 8388608 | bytes 4194304 | tf_op jit(solution)/shard_map/assemble/pallas_call | solution.py:726
  24.0 0.4 %collective-permute-done.2.refs_1_ = f32[200,128]{1,0:T(8,128)S(1)} collective-permute-done((f32[200,128]{1,0:T(8,128)S(1)}, f32[200,128]{1,0:T(8,128)S(1)}, u32[]{:S(2)}, u32[]{:S(2)}) %collective-permute-start.2) | collective-permute-done | bytes 102432 | tf_op jit(solution)/shard_map/ppermute | solution.py:832
  24.3 1.9 %collective-permute-done.3.refs_2_ = f32[200,128]{1,0:T(8,128)S(1)} collective-permute-done((f32[200,128]{1,0:T(8,128)S(1)}, f32[200,128]{1,0:T(8,128)S(1)}, u32[]{:S(2)}, u32[]{:S(2)}) %collective-permute-start.3) | collective-permute-done | bytes 102432 | tf_op jit(solution)/shard_map/ppermute | solution.py:832
  26.2 0.0 collective-permute-done.4.refs_3_
  26.2 0.9 %tiles.1 = f32[1,1,3,128,128]{4,3,2,1,0:T(8,128)} custom-call(s32[1,1]{1,0:T(1,128)S(6)} %copy.18.counts_ref, f32[200,128]{1,0:T(8,128)S(1)} %get-tuple-element.42.refs_0_, f32[200,128]{1,0:T(8,128)S(1)} %collective-permute-done.2.refs_1_, f32[200,128]{1,0:T(8,128)S(1)} %collective-permute-done.3.refs_2_, f32[200,128]{1,0:T(8,128)S(1)} %collective-permute-done.4.refs_3_), custom_call_target="tpu_custom_call" | custom-call | tf_op jit(solution)/shard_map/tiles/pallas_call | solution.py:765
  (2 shorter events, 0.0 us)
Async XLA Ops:
  0.6 3.8 %copy-start = (f32[8,32,512]{2,1,0:T(8,128)S(1)}, f32[8,32,512]{2,1,0:T(8,128)}, u32[]{:S(2)}) copy-start(f32[8,32,512]{2,1,0:T(8,128)} %param.13) | copy-start | bytes 1572868
  0.6 3.8 %copy-start.1 = (f32[8,32,512]{2,1,0:T(8,128)S(1)}, f32[8,32,512]{2,1,0:T(8,128)}, u32[]{:S(2)}) copy-start(f32[8,32,512]{2,1,0:T(8,128)} %param.14) | copy-start | bytes 1572868
  0.7 3.8 %copy-start.2 = (f32[8,32,512]{2,1,0:T(8,128)S(1)}, f32[8,32,512]{2,1,0:T(8,128)}, u32[]{:S(2)}) copy-start(f32[8,32,512]{2,1,0:T(8,128)} %param.15) | copy-start | bytes 1572868
  0.7 3.8 %copy-start.3 = (f32[8,32,512]{2,1,0:T(8,128)S(1)}, f32[8,32,512]{2,1,0:T(8,128)}, u32[]{:S(2)}) copy-start(f32[8,32,512]{2,1,0:T(8,128)} %param.16) | copy-start | bytes 1572868
  0.7 3.8 %copy-start.6 = (f32[32,512]{1,0:T(8,128)S(1)}, f32[32,512]{1,0:T(8,128)}, u32[]{:S(2)}) copy-start(f32[32,512]{1,0:T(8,128)} %courant_ref.1) | copy-start | bytes 196612
  0.7 3.8 %copy-start.7 = (f32[32,512]{1,0:T(8,128)S(1)}, f32[32,512]{1,0:T(8,128)}, u32[]{:S(2)}) copy-start(f32[32,512]{1,0:T(8,128)} %epsilon_ref.1) | copy-start | bytes 196612
  0.7 3.8 %copy-start.8 = (f32[32,512]{1,0:T(8,128)S(1)}, f32[32,512]{1,0:T(8,128)}, u32[]{:S(2)}) copy-start(f32[32,512]{1,0:T(8,128)} %delta_ref.1) | copy-start | bytes 196612
  0.7 3.8 %copy-start.9 = (f32[32,512]{1,0:T(8,128)S(1)}, f32[32,512]{1,0:T(8,128)}, u32[]{:S(2)}) copy-start(f32[32,512]{1,0:T(8,128)} %tilt_ref.1) | copy-start | bytes 196612
  0.7 3.8 %copy-start.11 = (s32[1,4,3,128]{3,1,2,0:T(4,128)S(1)}, s32[1,4,3,128]{3,1,2,0:T(4,128)}, u32[]{:S(2)}) copy-start(s32[1,4,3,128]{3,1,2,0:T(4,128)} %param.24) | copy-start | bytes 18436
  0.7 3.8 %copy-start.10 = (s32[512]{0:T(512)S(1)}, s32[512]{0:T(512)}, u32[]{:S(2)}) copy-start(s32[512]{0:T(512)} %param.23) | copy-start | bytes 6148
  2.9 7.6 %collective-permute-start = (bf16[160,512]{1,0:T(8,128)(2,1)}, bf16[160,512]{1,0:T(8,128)(2,1)S(1)}, u32[]{:S(2)}, u32[]{:S(2)}) collective-permute-start(bf16[160,512]{1,0:T(8,128)(2,1)} %outer_rows.1.sent_ref), channel_id=1, source_target_pairs={{0,1},{1,0},{2,3},{3,2},{4,5},{5,4},{6,7},{7,6},{8,9},{9,8},{10,11... | collective-permute-start | bytes 491528 | tf_op jit(solution)/shard_map/ppermute | solution.py:803
  4.6 0.9 %copy-start.5 = (bf16[160,512]{1,0:T(8,128)(2,1)S(1)}, bf16[160,512]{1,0:T(8,128)(2,1)}, u32[]{:S(2)}) copy-start(bf16[160,512]{1,0:T(8,128)(2,1)} %outer_rows.1.sent_ref) | copy-start | bytes 491524
  5.5 4.9 %copy-start.12 = (f32[16]{0:T(128)S(1)}, f32[16]{0:T(128)}, u32[]{:S(2)}) copy-start(f32[16]{0:T(128)} %param.21) | copy-start | bytes 196
  8.0 8.5 %collective-permute-start.1 = (bf16[160,512]{1,0:T(8,128)(2,1)S(1)}, bf16[160,512]{1,0:T(8,128)(2,1)S(1)}, u32[]{:S(2)}, u32[]{:S(2)}) collective-permute-start(bf16[160,512]{1,0:T(8,128)(2,1)S(1)} %get-tuple-element.32), channel_id=1, source_target_pairs={{1,2},{2,1},{3,4},{4,3},{5,6},{6,5},{9,10},{10,9},{11,12},{12,11},... | collective-permute-start | bytes 491528 | tf_op jit(solution)/shard_map/ppermute | solution.py:803
  10.5 6.0 %copy-start.4 = (f32[8,32,512]{2,1,0:T(8,128)S(1)}, f32[8,32,512]{2,1,0:T(8,128)}, u32[]{:S(2)}) copy-start(f32[8,32,512]{2,1,0:T(8,128)} %param.22) | copy-start | bytes 1572868
  19.5 4.9 %collective-permute-start.2 = (f32[200,128]{1,0:T(8,128)S(1)}, f32[200,128]{1,0:T(8,128)S(1)}, u32[]{:S(2)}, u32[]{:S(2)}) collective-permute-start(f32[200,128]{1,0:T(8,128)S(1)} %get-tuple-element.43), channel_id=1, source_target_pairs={{0,16},{8,24},{16,0},{24,8},{1,17},{9,25},{17,1},{25,9},{2,18},{10... | collective-permute-start | bytes 307208 | tf_op jit(solution)/shard_map/ppermute | solution.py:832
  21.0 5.2 %collective-permute-start.3 = (f32[200,128]{1,0:T(8,128)S(1)}, f32[200,128]{1,0:T(8,128)S(1)}, u32[]{:S(2)}, u32[]{:S(2)}) collective-permute-start(f32[200,128]{1,0:T(8,128)S(1)} %get-tuple-element.44), channel_id=1, source_target_pairs={{0,24},{8,16},{16,8},{24,0},{1,25},{9,17},{17,9},{25,1},{2,26},{10... | collective-permute-start | bytes 307208 | tf_op jit(solution)/shard_map/ppermute | solution.py:832
  21.0 5.2 %collective-permute-start.4 = (f32[200,128]{1,0:T(8,128)S(1)}, f32[200,128]{1,0:T(8,128)S(1)}, u32[]{:S(2)}, u32[]{:S(2)}) collective-permute-start(f32[200,128]{1,0:T(8,128)S(1)} %get-tuple-element.45), channel_id=1, source_target_pairs={{0,8},{8,0},{16,24},{24,16},{1,9},{9,1},{17,25},{25,17},{2,10},{10... | collective-permute-start | bytes 307208 | tf_op jit(solution)/shard_map/ppermute | solution.py:832

commit v9 on v7

--- a/solution.py
+++ b/solution.py
@@ -262,6 +262,12 @@
     return me ^ k
 
 
+def owner_of(me, k, owners):
+    chips = owners // 2
+    chip, core = me // 2, me % 2
+    return partner(chip, k % chips, chips) * 2 + (core ^ (k // chips))
+
+
 def sample_rows(values, one_hot):
     high, low = split_bf16(values)
     return jnp.dot(jnp.concatenate([high, low], 1), one_hot, preferred_element_type=jnp.float32)
@@ -326,7 +332,7 @@
     me = lax.axis_index("shot")
     rows = []
     for k in range(owners):
-        lists = lists_ref[0, partner(me, k, owners)]
+        lists = lists_ref[0, owner_of(me, k, owners)]
         rows += [lists[s : s + 1, :] for s in range(slots)]
     count = len(rows)
     while len(rows) % 8:
@@ -555,14 +561,17 @@
     out_copy = pltpu.make_async_copy(out_ref, spectra_out_ref, out_sem)
     out_copy.start()
 
-    owners = len(packed_refs)
-    patch = packed_refs[0].shape[1]
+    chips = len(packed_refs) - 1
+    owners = 2 * chips
+    size, patch = packed_refs[0].shape
     slots = list_hot_ref.shape[0] // (owners * patch)
     half = patch // 2
     row = lax.broadcasted_iota(jnp.int32, (half, patch), 0)
     lane = lax.broadcasted_iota(jnp.int32, (half, patch), 1)
     from_last = (lane < half) & (row > lane)
-    for g, packed_ref in enumerate(packed_refs):
+    for g in range(owners):
+        packed_ref = packed_refs[min(g, chips)]
+        base = max(g - chips, 0) * size
         chosen = lax.dot_general(
             list_hot_ref[pl.ds(g * slots * patch, slots * patch), :],
             feature_ref[...],
@@ -574,11 +583,11 @@
             mine = chosen[s * patch : (s + 1) * patch]
             gram = lax.dot_general(mine, mine, NT, preferred_element_type=jnp.float32)
             last = pltpu.roll(gram[half:], half, 1)
-            packed_ref[pl.ds(s * half, half), :] = jnp.where(from_last, last, gram[:half])
+            packed_ref[pl.ds(base + s * half, half), :] = jnp.where(from_last, last, gram[:half])
             diagonals.append(jnp.sum(jnp.where(row == lane, last, 0.0), 0, keepdims=True))
         while len(diagonals) % 8:
             diagonals.append(jnp.zeros((1, patch), jnp.float32))
-        packed_ref[pl.ds(slots * half, len(diagonals)), :] = jnp.concatenate(diagonals, 0)
+        packed_ref[pl.ds(base + slots * half, len(diagonals)), :] = jnp.concatenate(diagonals, 0)
     out_copy.wait()
 
 
@@ -592,7 +601,8 @@
     out_shape = [
         f32((features, targets)),
         f32((2, 2, STEPS, shots, depth)),
-        *[f32((rows, patch))] * owners,
+        *[f32((rows, patch))] * (owners // 2),
+        f32((owners // 2 * rows, patch)),
     ]
     vmem = pl.BlockSpec(memory_space=pltpu.VMEM)
     return pl.pallas_call(
@@ -663,7 +673,7 @@
     live = counts_ref[0, 0]
     total = received[0][...]
     for ref in received[1:]:
-        total = total + ref[...]
+        total = total + ref[pl.ds(0, total.shape[0]), :]
     for s in range(slots):
         scale = jnp.where(s < live, 1.0 / features, 0.0)
         packed = total[s * half : (s + 1) * half] * scale
@@ -742,10 +752,14 @@
         slots,
         patch,
     )
-    received = packed[:1]
-    for k in sorted(range(1, owners), key=lambda k: (k < owners // 2, k)):
-        pairs = [(i, int(partner(i, k, owners))) for i in range(owners)]
-        received.append(lax.ppermute(packed[k], "shot", pairs))
+    chips = owners // 2
+    beside = lax.ppermute(packed[chips], "shot", [(i, i ^ 1) for i in range(owners)])
+    received = [packed[0], beside]
+    size = packed[0].shape[0]
+    for k in range(1, chips):
+        both = packed[k] + beside[k * size : (k + 1) * size]
+        pairs = [(i, partner(i // 2, k, chips) * 2 + i % 2) for i in range(owners)]
+        received.append(lax.ppermute(both, "shot", pairs))
     pressure_out, auxiliary_out = [untiled(item) for item in assemble(p_inner, q_inner, final)]
     gram_tiles = tiles(received, patch_counts, slots, shots * parts * owners)
     return (pressure_out, auxiliary_out, spectra_out.reshape(spectra.shape), gram_tiles)

time: 26.2 us -> 25.7 us (0.981)
  the two profiles are of different devices: /device:TPU:11 before, /device:TPU:18 now
where the time goes in v9:
time: 25.7 us; the launch traced here: 25.5 us
  Pallas kernels  14.4 us (56%)
  starting transfers between devices  6.65 us (26%)
  waiting for transfers between devices  2.54 us (10%)
  between operations  1.53 us (6%)
    pallas_call x1, Pallas kernels, interior(): pl.pallas_call(interior_kernel, in_specs=[vmem] * 10, out_specs=[vmem] *...  6.54 us
    ppermute x2, starting transfers between devices, shards(): swapped.append(lax.ppermute(rows, 'brick', pairs))  5 us
    pallas_call x1, Pallas kernels, finish(): pl.pallas_call(functools.partial(finish_kernel, width=width), in_specs=[v...  2.95 us
    pallas_call x1, Pallas kernels, outer_rows(): pl.pallas_call(outer_kernel, in_specs=[pl.BlockSpec(memory_space=pltpu.HB...  2.38 us
    pallas_call x1, Pallas kernels, assemble(): pl.pallas_call(assemble_kernel, in_specs=[vmem] * 3, out_specs=[vmem] * 2...  1.66 us
    ppermute x1, starting transfers between devices, shards(): received.append(lax.ppermute(both, 'shot', pairs))  1.58 us
    ppermute x1, waiting for transfers between devices, shards(): lax.ppermute(packed[chips], 'shot', [(i, i ^ 1) for i in range(owners)])  1.44 us
    ppermute x1, waiting for transfers between devices, shards(): received.append(lax.ppermute(both, 'shot', pairs))  1.1 us
  transfers between devices with their start and end apart: 4, of which 2 were waited for; matrix products, arithmetic and copies ran while one was open for 1% of the time, Pallas kernels for 32%

profile of v9, /device:TPU:18, one launch (start us, length us, event | category | flops | bytes accessed | tf_op | source)
XLA Modules:
  0.0 25.5 jit_solution(14781011024916389016)
XLA Ops:
  0.6 0.0 copy-start
  0.6 0.0 copy-start.1
  0.7 0.0 copy-start.2
  0.7 0.0 copy-start.3
  0.7 0.0 copy-start.5
  0.7 0.0 copy-start.6
  0.7 0.0 copy-start.7
  0.7 0.0 copy-start.8
  0.7 0.0 copy-start.11
  0.7 0.0 copy-start.10
  0.7 0.0 copy-start.9
  0.7 2.4 %outer_rows.1 = (bf16[160,512]{1,0:T(8,128)(2,1)}, bf16[160,512]{1,0:T(8,128)(2,1)}) custom-call(f32[8,4,4,8,128]{4,3,2,1,0:T(8,128)} %bitcast.21, f32[8,4,4,8,128]{4,3,2,1,0:T(8,128)} %bitcast.23, f32[8,4,4,8,128]{4,3,2,1,0:T(8,128)} %bitcast.25, f32[8,4,4,8,128]{4,3,2,1,0:T(8,128)} %bitcast.27, f32[32,512]{1,0:T(8,128)} %refs_4_.1, f32[32,512]{1,0:T(8,128)} %refs_5_.1, ...), custom_call_target="tpu_custom_call" | custom-call | tf_op jit(solution)/shard_map/outer_rows/pallas_call | solution.py:243
  3.1 0.0 copy-start.4
  3.1 0.6 %collective-permute-start = (bf16[160,512]{1,0:T(8,128)(2,1)}, bf16[160,512]{1,0:T(8,128)(2,1)S(1)}, u32[]{:S(2)}, u32[]{:S(2)}) collective-permute-start(bf16[160,512]{1,0:T(8,128)(2,1)} %get-tuple-element.24), channel_id=1, source_target_pairs={{0,1},{1,0},{2,3},{3,2},{4,5},{5,4},{6,7},{7,6},{8,9},{9,8},{10,11... | collective-permute-start | bytes 491528 | tf_op jit(solution)/shard_map/ppermute | solution.py:733
  3.7 4.4 %collective-permute-start.1 = (bf16[160,512]{1,0:T(8,128)(2,1)}, bf16[160,512]{1,0:T(8,128)(2,1)S(1)}, u32[]{:S(2)}, u32[]{:S(2)}) collective-permute-start(bf16[160,512]{1,0:T(8,128)(2,1)} %get-tuple-element.25), channel_id=1, source_target_pairs={{1,2},{2,1},{3,4},{4,3},{5,6},{6,5},{9,10},{10,9},{11,12},{12,11},... | collective-permute-start | bytes 491528 | tf_op jit(solution)/shard_map/ppermute | solution.py:733
  8.2 0.0 copy-done.11
  8.2 0.1 multiply_cosine_fusion
  8.3 0.0 copy-done.10
  8.3 0.0 copy-done
  8.3 0.0 copy-done.1
  8.3 0.0 copy-done.2
  8.3 0.0 copy-done.3
  8.3 0.0 copy-done.5
  8.4 0.0 copy-done.6
  8.4 0.0 copy-done.7
  8.4 0.0 copy-done.8
  8.4 0.0 copy-done.9
  8.4 6.5 %interior.1 = (f32[2,2,4,2,8,512]{5,4,3,2,1,0:T(8,128)S(1)}, f32[2,2,8,512]{3,2,1,0:T(8,128)S(1)}, f32[2,5,8,512]{3,2,1,0:T(8,128)S(1)}, f32[24,8,512]{2,1,0:T(8...) custom-call(f32[8,4,4,8,128]{4,3,2,1,0:T(8,128)S(1)} %bitcast.22, ...), custom_call_target="tpu_custom_call" | custom-call | flops 104857600 | bytes 8388608 | tf_op jit(solution)/shard_map/interior/pallas_call | solution.py:429
  14.9 0.1 pad_maximum_fusion
  15.0 0.0 collective-permute-done.even_ref
  15.0 0.0 collective-permute-done.1.odd_ref
  15.0 0.1 broadcast_in_dim.2.table_ref
  15.1 0.0 copy-done.4
  15.1 2.9 %finish.1 = (f32[256,512]{1,0:T(8,128)}, f32[2,2,4,8,512]{4,3,2,1,0:T(8,128)S(1)}, f32[200,128]{1,0:T(8,128)S(1)}, f32[200,128]{1,0:T(8,128)S(1)}, f32[400,128]{1,0:T(8,128)S(1)}) custom-call(bf16[160,512]{1,0:T(8,128)(2,1)S(1)} %collective-permute-done.even_ref, bf16[160,512]{1,0:T(8,128)(2,1)S(1)} %collective-permute-done.1.odd_ref, ...), custom_call_target="tpu_custom_call" | custom-call | tf_op jit(solution)/shard_map/finish/pallas_call | solution.py:608
  18.1 0.1 collective-permute-start.2
  18.1 1.4 %collective-permute-done.2.refs_1_ = f32[400,128]{1,0:T(8,128)S(1)} collective-permute-done((f32[400,128]{1,0:T(8,128)S(1)}, f32[400,128]{1,0:T(8,128)S(1)}, u32[]{:S(2)}, u32[]{:S(2)}) %collective-permute-start.2) | collective-permute-done | bytes 204832 | tf_op jit(solution)/shard_map/ppermute | solution.py:756
  19.6 1.6 %collective-permute-start.3 = (f32[200,128]{1,0:T(8,128)S(1)}, f32[200,128]{1,0:T(8,128)S(1)}, u32[]{:S(2)}, u32[]{:S(2)}) collective-permute-start(f32[200,128]{1,0:T(8,128)S(1)} %slice_add_fusion), channel_id=1, source_target_pairs={{0,16},{8,24},{16,0},{24,8},{1,17},{9,25},{17,1},{25,9},{2,18},{10... | collective-permute-start | bytes 307208 | tf_op jit(solution)/shard_map/ppermute | solution.py:762
  21.8 1.7 %assemble.1 = (f32[8,4,4,8,128]{4,3,2,1,0:T(8,128)}, f32[8,4,4,8,128]{4,3,2,1,0:T(8,128)}) custom-call(f32[24,8,512]{2,1,0:T(8,128)S(1)} %get-tuple-element.22.p_inner_ref, f32[24,8,512]{2,1,0:T(8,128)S(1)} %get-tuple-element.23.q_inner_ref, f32[2,2,4,8,512]{4,3,2,1,0:T(8,128)S(1)} %get-tuple-element.33.final_ref), custom_call_target="tpu_custom_call" | custom-call | flops 8388608 | bytes 4194304 | tf_op jit(solution)/shard_map/assemble/pallas_call | solution.py:656
  23.5 1.1 %collective-permute-done.3.refs_2_ = f32[200,128]{1,0:T(8,128)S(1)} collective-permute-done((f32[200,128]{1,0:T(8,128)S(1)}, f32[200,128]{1,0:T(8,128)S(1)}, u32[]{:S(2)}, u32[]{:S(2)}) %collective-permute-start.3) | collective-permute-done | bytes 102432 | tf_op jit(solution)/shard_map/ppermute | solution.py:762
  24.6 0.9 %tiles.1 = f32[1,1,3,128,128]{4,3,2,1,0:T(8,128)} custom-call(s32[1,1]{1,0:T(1,128)S(6)} %copy.18.counts_ref, f32[200,128]{1,0:T(8,128)S(1)} %get-tuple-element.37.refs_0_, f32[400,128]{1,0:T(8,128)S(1)} %collective-permute-done.2.refs_1_, f32[200,128]{1,0:T(8,128)S(1)} %collective-permute-done.3.refs_2_), custom_call_target="tpu_custom_call" | custom-call | tf_op jit(solution)/shard_map/tiles/pallas_call | solution.py:695
  (3 shorter events, 0.0 us)
Async XLA Ops:
  0.6 7.7 %copy-start = (f32[8,32,512]{2,1,0:T(8,128)S(1)}, f32[8,32,512]{2,1,0:T(8,128)}, u32[]{:S(2)}) copy-start(f32[8,32,512]{2,1,0:T(8,128)} %param.13) | copy-start | bytes 1572868
  0.6 7.7 %copy-start.1 = (f32[8,32,512]{2,1,0:T(8,128)S(1)}, f32[8,32,512]{2,1,0:T(8,128)}, u32[]{:S(2)}) copy-start(f32[8,32,512]{2,1,0:T(8,128)} %param.14) | copy-start | bytes 1572868
  0.7 7.7 %copy-start.2 = (f32[8,32,512]{2,1,0:T(8,128)S(1)}, f32[8,32,512]{2,1,0:T(8,128)}, u32[]{:S(2)}) copy-start(f32[8,32,512]{2,1,0:T(8,128)} %param.15) | copy-start | bytes 1572868
  0.7 7.7 %copy-start.3 = (f32[8,32,512]{2,1,0:T(8,128)S(1)}, f32[8,32,512]{2,1,0:T(8,128)}, u32[]{:S(2)}) copy-start(f32[8,32,512]{2,1,0:T(8,128)} %param.16) | copy-start | bytes 1572868
  0.7 7.7 %copy-start.5 = (f32[32,512]{1,0:T(8,128)S(1)}, f32[32,512]{1,0:T(8,128)}, u32[]{:S(2)}) copy-start(f32[32,512]{1,0:T(8,128)} %refs_4_.1) | copy-start | bytes 196612
  0.7 7.7 %copy-start.6 = (f32[32,512]{1,0:T(8,128)S(1)}, f32[32,512]{1,0:T(8,128)}, u32[]{:S(2)}) copy-start(f32[32,512]{1,0:T(8,128)} %refs_5_.1) | copy-start | bytes 196612
  0.7 7.7 %copy-start.7 = (f32[32,512]{1,0:T(8,128)S(1)}, f32[32,512]{1,0:T(8,128)}, u32[]{:S(2)}) copy-start(f32[32,512]{1,0:T(8,128)} %refs_6_.1) | copy-start | bytes 196612
  0.7 7.7 %copy-start.8 = (f32[32,512]{1,0:T(8,128)S(1)}, f32[32,512]{1,0:T(8,128)}, u32[]{:S(2)}) copy-start(f32[32,512]{1,0:T(8,128)} %refs_7_.1) | copy-start | bytes 196612
  0.7 7.5 %copy-start.11 = (f32[16]{0:T(128)S(1)}, f32[16]{0:T(128)}, u32[]{:S(2)}) copy-start(f32[16]{0:T(128)} %param.21) | copy-start | bytes 196
  0.7 7.6 %copy-start.10 = (s32[1,4,3,128]{3,1,2,0:T(4,128)S(1)}, s32[1,4,3,128]{3,1,2,0:T(4,128)}, u32[]{:S(2)}) copy-start(s32[1,4,3,128]{3,1,2,0:T(4,128)} %param.24) | copy-start | bytes 18436
  0.7 7.7 %copy-start.9 = (s32[512]{0:T(512)S(1)}, s32[512]{0:T(512)}, u32[]{:S(2)}) copy-start(s32[512]{0:T(512)} %param.23) | copy-start | bytes 6148
  3.1 12.0 %copy-start.4 = (f32[8,32,512]{2,1,0:T(8,128)S(1)}, f32[8,32,512]{2,1,0:T(8,128)}, u32[]{:S(2)}) copy-start(f32[8,32,512]{2,1,0:T(8,128)} %param.22) | copy-start | bytes 1572868
  3.1 11.9 %collective-permute-start = (bf16[160,512]{1,0:T(8,128)(2,1)}, bf16[160,512]{1,0:T(8,128)(2,1)S(1)}, u32[]{:S(2)}, u32[]{:S(2)}) collective-permute-start(bf16[160,512]{1,0:T(8,128)(2,1)} %get-tuple-element.24), channel_id=1, source_target_pairs={{0,1},{1,0},{2,3},{3,2},{4,5},{5,4},{6,7},{7,6},{8,9},{9,8},{10,11... | collective-permute-start | bytes 491528 | tf_op jit(solution)/shard_map/ppermute | solution.py:733
  3.7 11.3 %collective-permute-start.1 = (bf16[160,512]{1,0:T(8,128)(2,1)}, bf16[160,512]{1,0:T(8,128)(2,1)S(1)}, u32[]{:S(2)}, u32[]{:S(2)}) collective-permute-start(bf16[160,512]{1,0:T(8,128)(2,1)} %get-tuple-element.25), channel_id=1, source_target_pairs={{1,2},{2,1},{3,4},{4,3},{5,6},{6,5},{9,10},{10,9},{11,12},{12,11},... | collective-permute-start | bytes 491528 | tf_op jit(solution)/shard_map/ppermute | solution.py:733
  18.1 1.5 %collective-permute-start.2 = (f32[400,128]{1,0:T(8,128)S(1)}, f32[400,128]{1,0:T(8,128)S(1)}, u32[]{:S(2)}, u32[]{:S(2)}) collective-permute-start(f32[400,128]{1,0:T(8,128)S(1)} %get-tuple-element.38), channel_id=1, source_target_pairs={{0,8},{8,0},{16,24},{24,16},{1,9},{9,1},{17,25},{25,17},{2,10},{10... | collective-permute-start | bytes 614408 | tf_op jit(solution)/shard_map/ppermute | solution.py:756
  19.6 5.0 %collective-permute-start.3 = (f32[200,128]{1,0:T(8,128)S(1)}, f32[200,128]{1,0:T(8,128)S(1)}, u32[]{:S(2)}, u32[]{:S(2)}) collective-permute-start(f32[200,128]{1,0:T(8,128)S(1)} %slice_add_fusion), channel_id=1, source_target_pairs={{0,16},{8,24},{16,0},{24,8},{1,17},{9,25},{17,1},{25,9},{2,18},{10... | collective-permute-start | bytes 307208 | tf_op jit(solution)/shard_map/ppermute | solution.py:762

commit v10 on v9

--- a/solution.py
+++ b/solution.py
@@ -40,6 +40,9 @@
         else:
             start = (lax.div(x, TILE) * self.along + j) * TILE + lax.rem(x, TILE)
         return pl.ds(start, self.shots, stride=self.stride)
+
+    def block(self, x, j):
+        return self.flat[self.place(x, j), :]
 
     def __getitem__(self, x):
         return jnp.concatenate([self.flat[self.place(x, j), :] for j in range(self.along)], 1)
@@ -89,50 +92,51 @@
     return [row[:, j : j + LANES] for j in range(0, row.shape[1], LANES)]
 
 
-def depth_terms(row):
-    lane = lax.broadcasted_iota(jnp.int32, row[0].shape, 1)
-    shallow = [pltpu.roll(block, 1, 1) for block in row]
-    deep = [pltpu.roll(block, LANES - 1, 1) for block in row]
-    outside = jnp.zeros_like(row[0])
-    sums, differences = [], []
-    for j in range(len(row)):
-        above = jnp.where(lane == 0, shallow[j - 1] if j else outside, shallow[j])
-        below = jnp.where(
-            lane == LANES - 1, deep[j + 1] if j + 1 < len(row) else outside, deep[j]
-        )
-        sums.append(below + above)
-        differences.append(below - above)
-    return sums, differences
-
-
-def advance(count, p_row, q_row, p_prior, q_prior, coefficient, put):
-    p_back, p_here = blocks(p_row(-1)), blocks(p_row(0))
-    q_back, q_here = blocks(q_row(-1)), blocks(q_row(0))
-    _, p_back_d = depth_terms(p_back)
-    _, q_back_d = depth_terms(q_back)
-    p_sum, p_here_d = depth_terms(p_here)
-    q_sum, q_here_d = depth_terms(q_here)
-    for row in range(count):
-        p_next, q_next = blocks(p_row(row + 1)), blocks(q_row(row + 1))
-        p_next_sum, p_next_d = depth_terms(p_next)
-        q_next_sum, q_next_d = depth_terms(q_next)
-        p_old, q_old = blocks(p_prior(row)), blocks(q_prior(row))
-        p_new, q_new = [], []
-        for j in range(len(p_here)):
+def depth_terms(read, row, j, last):
+    block = read(row, j)
+    lane = lax.broadcasted_iota(jnp.int32, block.shape, 1)
+    outside = jnp.zeros_like(block)
+    above = pltpu.roll(read(row, j - 1), 1, 1) if j else outside
+    below = pltpu.roll(read(row, j + 1), LANES - 1, 1) if j < last else outside
+    shallow = jnp.where(lane == 0, above, pltpu.roll(block, 1, 1))
+    deep = jnp.where(lane == LANES - 1, below, pltpu.roll(block, LANES - 1, 1))
+    return block, deep + shallow, deep - shallow
+
+
+def advance(count, along, p_row, q_row, p_prior, q_prior, coefficient, put):
+    for j in range(along):
+        p_terms = functools.partial(depth_terms, p_row, j=j, last=along - 1)
+        q_terms = functools.partial(depth_terms, q_row, j=j, last=along - 1)
+        p_back, _, p_back_d = p_terms(-1)
+        q_back, _, q_back_d = q_terms(-1)
+        p_here, p_sum, p_here_d = p_terms(0)
+        q_here, q_sum, q_here_d = q_terms(0)
+        for row in range(count):
+            p_next, p_next_sum, p_next_d = p_terms(row + 1)
+            q_next, q_next_sum, q_next_d = q_terms(row + 1)
             sine_sq, quarter_sin, courant, gain_p, gain_q = [coefficient(i, row, j) for i in range(5)]
-            twice_p, twice_q = p_here[j] + p_here[j], q_here[j] + q_here[j]
-            side = p_next[j] + p_back[j]
-            mixed = p_next_d[j] - p_back_d[j]
-            across = (side - twice_p) + sine_sq * (p_sum[j] - side) - quarter_sin * mixed
-            side = q_next[j] + q_back[j]
-            mixed = q_next_d[j] - q_back_d[j]
-            along = (q_sum[j] - twice_q) + sine_sq * (side - q_sum[j]) + quarter_sin * mixed
-            along = courant * along
-            p_new.append((twice_p - p_old[j]) + (gain_p * across + along))
-            q_new.append((twice_q - q_old[j]) + (gain_q * across + along))
-        put(row, jnp.concatenate(p_new, 1), jnp.concatenate(q_new, 1))
-        p_back, p_here, p_back_d, p_here_d, p_sum = p_here, p_next, p_here_d, p_next_d, p_next_sum
-        q_back, q_here, q_back_d, q_here_d, q_sum = q_here, q_next, q_here_d, q_next_d, q_next_sum
+            twice_p, twice_q = p_here + p_here, q_here + q_here
+            side = p_next + p_back
+            mixed = p_next_d - p_back_d
+            across = (side - twice_p) + sine_sq * (p_sum - side) - quarter_sin * mixed
+            side = q_next + q_back
+            mixed = q_next_d - q_back_d
+            along_q = (q_sum - twice_q) + sine_sq * (side - q_sum) + quarter_sin * mixed
+            along_q = courant * along_q
+            put(
+                row,
+                j,
+                (twice_p - p_prior(row, j)) + (gain_p * across + along_q),
+                (twice_q - q_prior(row, j)) + (gain_q * across + along_q),
+            )
+            p_back, p_here, p_sum = p_here, p_next, p_next_sum
+            p_back_d, p_here_d = p_here_d, p_next_d
+            q_back, q_here, q_sum = q_here, q_next, q_next_sum
+            q_back_d, q_here_d = q_here_d, q_next_d
+
+
+def lanes_of(j):
+    return pl.ds(j * LANES, LANES)
 
 
 class CoefficientRows:
@@ -365,27 +369,37 @@
             start = low + at
             held = []
 
-            def put(r, p_new, q_new):
+            def put(r, j, p_new, q_new):
                 if step < STEPS:
-                    level_ref[step, 0, start + r] = p_new
-                    level_ref[step, 1, start + r] = q_new
+                    level_ref[step, 0, start + r, :, lanes_of(j)] = p_new
+                    level_ref[step, 1, start + r, :, lanes_of(j)] = q_new
                 else:
-                    p_inner_ref[at + r] = p_new
-                    q_inner_ref[at + r] = q_new
+                    p_inner_ref[at + r, :, lanes_of(j)] = p_new
+                    q_inner_ref[at + r, :, lanes_of(j)] = q_new
                 held.append(p_new)
                 if len(held) == 2:
                     first, rest = split_bf16(jnp.concatenate(held, 0))
                     place = pl.multiple_of((offset + at + r - 1) * shots, 2 * shots)
-                    split_ref[pl.ds(place, 2 * shots), pl.ds(0, depth)] = first
-                    split_ref[pl.ds(place, 2 * shots), pl.ds(depth, depth)] = rest
+                    split_ref[pl.ds(place, 2 * shots), lanes_of(j)] = first
+                    split_ref[pl.ds(place, 2 * shots), lanes_of(along + j)] = rest
                     held.clear()
+
+            def current(field):
+                return lambda r, j: level_ref[step - 1, field, start + r, :, lanes_of(j)]
+
+            def prior(field):
+                if step == 1:
+                    rows = (pp_rows, qq_rows)[field]
+                    return lambda r, j: rows.block(start + r, j)
+                return lambda r, j: level_ref[step - 2, field, start + r, :, lanes_of(j)]
 
             advance(
                 chunk,
-                lambda r: level_ref[step - 1, 0, start + r],
-                lambda r: level_ref[step - 1, 1, start + r],
-                lambda r: pp_rows[start + r] if step == 1 else level_ref[step - 2, 0, start + r],
-                lambda r: qq_rows[start + r] if step == 1 else level_ref[step - 2, 1, start + r],
+                along,
+                current(0),
+                current(1),
+                prior(0),
+                prior(1),
                 lambda i, r, j: coefficients(i, start + r, j),
                 put,
             )
@@ -508,23 +522,28 @@
         for side in range(2):
             coefficients = CoefficientRows(coef_ref.at[side], shots)
 
+            def current(field):
+                return lambda r, j: level_ref[side, field, step - 1, low + r - first, :, lanes_of(j)]
+
             def prior(field):
                 if step == 1:
-                    return lambda r: prior_ref[side, field, low + r - (1 - STEPS)]
-                return lambda r: level_ref[side, field, step - 2, low + r - first]
-
-            def put(r, p_new, q_new):
+                    place = low - (1 - STEPS)
+                    return lambda r, j: prior_ref[side, field, place + r, :, lanes_of(j)]
+                return lambda r, j: level_ref[side, field, step - 2, low + r - first, :, lanes_of(j)]
+
+            def put(r, j, p_new, q_new):
                 if step < STEPS:
-                    level_ref[side, 0, step, low + r - first] = p_new
-                    level_ref[side, 1, step, low + r - first] = q_new
+                    level_ref[side, 0, step, low + r - first, :, lanes_of(j)] = p_new
+                    level_ref[side, 1, step, low + r - first, :, lanes_of(j)] = q_new
                 else:
-                    final_ref[side, 0, r] = p_new
-                    final_ref[side, 1, r] = q_new
+                    final_ref[side, 0, r, :, lanes_of(j)] = p_new
+                    final_ref[side, 1, r, :, lanes_of(j)] = q_new
 
             advance(
                 STEPS,
-                lambda r: level_ref[side, 0, step - 1, low + r - first],
-                lambda r: level_ref[side, 1, step - 1, low + r - first],
+                depth // LANES,
+                current(0),
+                current(1),
                 prior(0),
                 prior(1),
                 lambda i, r, j: coefficients(i, low + r - (1 - STEPS), j),

time: 25.7 us -> 27.4 us (1.066)
  Pallas kernels: 14.4 us -> 16.2 us
    pallas_call x1, Pallas kernels: 6.54 us -> 7.76 us  [interior(): pl.pallas_call(interior_kernel, in_specs=[vmem] * 10, out_specs=[vmem] *...]
    pallas_call x1, Pallas kernels: 2.95 us -> 3.51 us  [finish(): pl.pallas_call(functools.partial(finish_kernel, width=width), in_specs=[v...]
  transfers between devices with their start and end apart: 4 -> 4, of which waited for: 2 -> 2; matrix products, arithmetic and copies ran while one was open for 1% -> 1% of each run, Pallas kernels for 32% -> 35%
where the time goes in v10:
time: 27.4 us; the launch traced here: 27.2 us
  Pallas kernels  16.2 us (59%)
  starting transfers between devices  6.65 us (24%)
  waiting for transfers between devices  2.54 us (9%)
  between operations  1.53 us (6%)
    pallas_call x1, Pallas kernels, interior(): pl.pallas_call(interior_kernel, in_specs=[vmem] * 10, out_specs=[vmem] *...  7.76 us
    ppermute x2, starting transfers between devices, shards(): swapped.append(lax.ppermute(rows, 'brick', pairs))  5 us
    pallas_call x1, Pallas kernels, finish(): pl.pallas_call(functools.partial(finish_kernel, width=width), in_specs=[v...  3.51 us
    pallas_call x1, Pallas kernels, outer_rows(): pl.pallas_call(outer_kernel, in_specs=[pl.BlockSpec(memory_space=pltpu.HB...  2.38 us
    pallas_call x1, Pallas kernels, assemble(): pl.pallas_call(assemble_kernel, in_specs=[vmem] * 3, out_specs=[vmem] * 2...  1.66 us
    ppermute x1, starting transfers between devices, shards(): received.append(lax.ppermute(both, 'shot', pairs))  1.58 us
    ppermute x1, waiting for transfers between devices, shards(): lax.ppermute(packed[chips], 'shot', [(i, i ^ 1) for i in range(owners)])  1.44 us
    ppermute x1, waiting for transfers between devices, shards(): received.append(lax.ppermute(both, 'shot', pairs))  1.1 us
  transfers between devices with their start and end apart: 4, of which 2 were waited for; matrix products, arithmetic and copies ran while one was open for 1% of the time, Pallas kernels for 35%

profile of v10, /device:TPU:18, one launch (start us, length us, event | category | flops | bytes accessed | tf_op | source)
XLA Modules:
  0.0 27.2 jit_solution(13147777194080680041)
XLA Ops:
  0.6 0.0 copy-start
  0.6 0.0 copy-start.1
  0.7 0.0 copy-start.2
  0.7 0.0 copy-start.3
  0.7 0.0 copy-start.5
  0.7 0.0 copy-start.6
  0.7 0.0 copy-start.7
  0.7 0.0 copy-start.8
  0.7 0.0 copy-start.11
  0.7 0.0 copy-start.10
  0.7 0.0 copy-start.9
  0.7 2.4 %outer_rows.1 = (bf16[160,512]{1,0:T(8,128)(2,1)}, bf16[160,512]{1,0:T(8,128)(2,1)}) custom-call(f32[8,4,4,8,128]{4,3,2,1,0:T(8,128)} %bitcast.21, f32[8,4,4,8,128]{4,3,2,1,0:T(8,128)} %bitcast.23, f32[8,4,4,8,128]{4,3,2,1,0:T(8,128)} %bitcast.25, f32[8,4,4,8,128]{4,3,2,1,0:T(8,128)} %bitcast.27, f32[32,512]{1,0:T(8,128)} %refs_4_.1, f32[32,512]{1,0:T(8,128)} %refs_5_.1, ...), custom_call_target="tpu_custom_call" | custom-call | tf_op jit(solution)/shard_map/outer_rows/pallas_call | solution.py:247
  3.1 0.0 copy-start.4
  3.1 0.6 %collective-permute-start = (bf16[160,512]{1,0:T(8,128)(2,1)}, bf16[160,512]{1,0:T(8,128)(2,1)S(1)}, u32[]{:S(2)}, u32[]{:S(2)}) collective-permute-start(bf16[160,512]{1,0:T(8,128)(2,1)} %get-tuple-element.24), channel_id=1, source_target_pairs={{0,1},{1,0},{2,3},{3,2},{4,5},{5,4},{6,7},{7,6},{8,9},{9,8},{10,11... | collective-permute-start | bytes 491528 | tf_op jit(solution)/shard_map/ppermute | solution.py:752
  3.7 4.4 %collective-permute-start.1 = (bf16[160,512]{1,0:T(8,128)(2,1)}, bf16[160,512]{1,0:T(8,128)(2,1)S(1)}, u32[]{:S(2)}, u32[]{:S(2)}) collective-permute-start(bf16[160,512]{1,0:T(8,128)(2,1)} %get-tuple-element.25), channel_id=1, source_target_pairs={{1,2},{2,1},{3,4},{4,3},{5,6},{6,5},{9,10},{10,9},{11,12},{12,11},... | collective-permute-start | bytes 491528 | tf_op jit(solution)/shard_map/ppermute | solution.py:752
  8.2 0.0 copy-done.11
  8.2 0.1 multiply_cosine_fusion
  8.3 0.0 copy-done.10
  8.3 0.0 copy-done
  8.3 0.0 copy-done.1
  8.3 0.0 copy-done.2
  8.3 0.0 copy-done.3
  8.3 0.0 copy-done.5
  8.4 0.0 copy-done.6
  8.4 0.0 copy-done.7
  8.4 0.0 copy-done.8
  8.4 0.0 copy-done.9
  8.4 7.8 %interior.1 = (f32[2,2,4,2,8,512]{5,4,3,2,1,0:T(8,128)S(1)}, f32[2,2,8,512]{3,2,1,0:T(8,128)S(1)}, f32[2,5,8,512]{3,2,1,0:T(8,128)S(1)}, f32[24,8,512]{2,1,0:T(8...) custom-call(f32[8,4,4,8,128]{4,3,2,1,0:T(8,128)S(1)} %bitcast.22, ...), custom_call_target="tpu_custom_call" | custom-call | flops 104857600 | bytes 8388608 | tf_op jit(solution)/shard_map/interior/pallas_call | solution.py:443
  16.2 0.1 pad_maximum_fusion
  16.2 0.0 collective-permute-done.even_ref
  16.2 0.0 collective-permute-done.1.odd_ref
  16.2 0.1 broadcast_in_dim.2.table_ref
  16.3 0.0 copy-done.4
  16.3 3.5 %finish.1 = (f32[256,512]{1,0:T(8,128)}, f32[2,2,4,8,512]{4,3,2,1,0:T(8,128)S(1)}, f32[200,128]{1,0:T(8,128)S(1)}, f32[200,128]{1,0:T(8,128)S(1)}, f32[400,128]{1,0:T(8,128)S(1)}) custom-call(bf16[160,512]{1,0:T(8,128)(2,1)S(1)} %collective-permute-done.even_ref, bf16[160,512]{1,0:T(8,128)(2,1)S(1)} %collective-permute-done.1.odd_ref, ...), custom_call_target="tpu_custom_call" | custom-call | tf_op jit(solution)/shard_map/finish/pallas_call | solution.py:627
  19.8 0.1 collective-permute-start.2
  19.9 1.4 %collective-permute-done.2.refs_1_ = f32[400,128]{1,0:T(8,128)S(1)} collective-permute-done((f32[400,128]{1,0:T(8,128)S(1)}, f32[400,128]{1,0:T(8,128)S(1)}, u32[]{:S(2)}, u32[]{:S(2)}) %collective-permute-start.2) | collective-permute-done | bytes 204832 | tf_op jit(solution)/shard_map/ppermute | solution.py:775
  21.4 1.6 %collective-permute-start.3 = (f32[200,128]{1,0:T(8,128)S(1)}, f32[200,128]{1,0:T(8,128)S(1)}, u32[]{:S(2)}, u32[]{:S(2)}) collective-permute-start(f32[200,128]{1,0:T(8,128)S(1)} %slice_add_fusion), channel_id=1, source_target_pairs={{0,16},{8,24},{16,0},{24,8},{1,17},{9,25},{17,1},{25,9},{2,18},{10... | collective-permute-start | bytes 307208 | tf_op jit(solution)/shard_map/ppermute | solution.py:781
  23.6 1.7 %assemble.1 = (f32[8,4,4,8,128]{4,3,2,1,0:T(8,128)}, f32[8,4,4,8,128]{4,3,2,1,0:T(8,128)}) custom-call(f32[24,8,512]{2,1,0:T(8,128)S(1)} %get-tuple-element.22.p_inner_ref, f32[24,8,512]{2,1,0:T(8,128)S(1)} %get-tuple-element.23.q_inner_ref, f32[2,2,4,8,512]{4,3,2,1,0:T(8,128)S(1)} %get-tuple-element.33.final_ref), custom_call_target="tpu_custom_call" | custom-call | flops 8388608 | bytes 4194304 | tf_op jit(solution)/shard_map/assemble/pallas_call | solution.py:675
  25.3 1.1 %collective-permute-done.3.refs_2_ = f32[200,128]{1,0:T(8,128)S(1)} collective-permute-done((f32[200,128]{1,0:T(8,128)S(1)}, f32[200,128]{1,0:T(8,128)S(1)}, u32[]{:S(2)}, u32[]{:S(2)}) %collective-permute-start.3) | collective-permute-done | bytes 102432 | tf_op jit(solution)/shard_map/ppermute | solution.py:781
  26.4 0.9 %tiles.1 = f32[1,1,3,128,128]{4,3,2,1,0:T(8,128)} custom-call(s32[1,1]{1,0:T(1,128)S(6)} %copy.18.counts_ref, f32[200,128]{1,0:T(8,128)S(1)} %get-tuple-element.37.refs_0_, f32[400,128]{1,0:T(8,128)S(1)} %collective-permute-done.2.refs_1_, f32[200,128]{1,0:T(8,128)S(1)} %collective-permute-done.3.refs_2_), custom_call_target="tpu_custom_call" | custom-call | tf_op jit(solution)/shard_map/tiles/pallas_call | solution.py:714
  (3 shorter events, 0.0 us)
Async XLA Ops:
  0.6 7.7 %copy-start = (f32[8,32,512]{2,1,0:T(8,128)S(1)}, f32[8,32,512]{2,1,0:T(8,128)}, u32[]{:S(2)}) copy-start(f32[8,32,512]{2,1,0:T(8,128)} %param.13) | copy-start | bytes 1572868
  0.6 7.7 %copy-start.1 = (f32[8,32,512]{2,1,0:T(8,128)S(1)}, f32[8,32,512]{2,1,0:T(8,128)}, u32[]{:S(2)}) copy-start(f32[8,32,512]{2,1,0:T(8,128)} %param.14) | copy-start | bytes 1572868
  0.7 7.7 %copy-start.2 = (f32[8,32,512]{2,1,0:T(8,128)S(1)}, f32[8,32,512]{2,1,0:T(8,128)}, u32[]{:S(2)}) copy-start(f32[8,32,512]{2,1,0:T(8,128)} %param.15) | copy-start | bytes 1572868
  0.7 7.7 %copy-start.3 = (f32[8,32,512]{2,1,0:T(8,128)S(1)}, f32[8,32,512]{2,1,0:T(8,128)}, u32[]{:S(2)}) copy-start(f32[8,32,512]{2,1,0:T(8,128)} %param.16) | copy-start | bytes 1572868
  0.7 7.7 %copy-start.5 = (f32[32,512]{1,0:T(8,128)S(1)}, f32[32,512]{1,0:T(8,128)}, u32[]{:S(2)}) copy-start(f32[32,512]{1,0:T(8,128)} %refs_4_.1) | copy-start | bytes 196612
  0.7 7.7 %copy-start.6 = (f32[32,512]{1,0:T(8,128)S(1)}, f32[32,512]{1,0:T(8,128)}, u32[]{:S(2)}) copy-start(f32[32,512]{1,0:T(8,128)} %refs_5_.1) | copy-start | bytes 196612
  0.7 7.7 %copy-start.7 = (f32[32,512]{1,0:T(8,128)S(1)}, f32[32,512]{1,0:T(8,128)}, u32[]{:S(2)}) copy-start(f32[32,512]{1,0:T(8,128)} %refs_6_.1) | copy-start | bytes 196612
  0.7 7.7 %copy-start.8 = (f32[32,512]{1,0:T(8,128)S(1)}, f32[32,512]{1,0:T(8,128)}, u32[]{:S(2)}) copy-start(f32[32,512]{1,0:T(8,128)} %refs_7_.1) | copy-start | bytes 196612
  0.7 7.5 %copy-start.11 = (f32[16]{0:T(128)S(1)}, f32[16]{0:T(128)}, u32[]{:S(2)}) copy-start(f32[16]{0:T(128)} %param.21) | copy-start | bytes 196
  0.7 7.6 %copy-start.10 = (s32[1,4,3,128]{3,1,2,0:T(4,128)S(1)}, s32[1,4,3,128]{3,1,2,0:T(4,128)}, u32[]{:S(2)}) copy-start(s32[1,4,3,128]{3,1,2,0:T(4,128)} %param.24) | copy-start | bytes 18436
  0.7 7.7 %copy-start.9 = (s32[512]{0:T(512)S(1)}, s32[512]{0:T(512)}, u32[]{:S(2)}) copy-start(s32[512]{0:T(512)} %param.23) | copy-start | bytes 6148
  3.1 13.2 %copy-start.4 = (f32[8,32,512]{2,1,0:T(8,128)S(1)}, f32[8,32,512]{2,1,0:T(8,128)}, u32[]{:S(2)}) copy-start(f32[8,32,512]{2,1,0:T(8,128)} %param.22) | copy-start | bytes 1572868
  3.1 13.1 %collective-permute-start = (bf16[160,512]{1,0:T(8,128)(2,1)}, bf16[160,512]{1,0:T(8,128)(2,1)S(1)}, u32[]{:S(2)}, u32[]{:S(2)}) collective-permute-start(bf16[160,512]{1,0:T(8,128)(2,1)} %get-tuple-element.24), channel_id=1, source_target_pairs={{0,1},{1,0},{2,3},{3,2},{4,5},{5,4},{6,7},{7,6},{8,9},{9,8},{10,11... | collective-permute-start | bytes 491528 | tf_op jit(solution)/shard_map/ppermute | solution.py:752
  3.7 12.5 %collective-permute-start.1 = (bf16[160,512]{1,0:T(8,128)(2,1)}, bf16[160,512]{1,0:T(8,128)(2,1)S(1)}, u32[]{:S(2)}, u32[]{:S(2)}) collective-permute-start(bf16[160,512]{1,0:T(8,128)(2,1)} %get-tuple-element.25), channel_id=1, source_target_pairs={{1,2},{2,1},{3,4},{4,3},{5,6},{6,5},{9,10},{10,9},{11,12},{12,11},... | collective-permute-start | bytes 491528 | tf_op jit(solution)/shard_map/ppermute | solution.py:752
  19.8 1.5 %collective-permute-start.2 = (f32[400,128]{1,0:T(8,128)S(1)}, f32[400,128]{1,0:T(8,128)S(1)}, u32[]{:S(2)}, u32[]{:S(2)}) collective-permute-start(f32[400,128]{1,0:T(8,128)S(1)} %get-tuple-element.38), channel_id=1, source_target_pairs={{0,8},{8,0},{16,24},{24,16},{1,9},{9,1},{17,25},{25,17},{2,10},{10... | collective-permute-start | bytes 614408 | tf_op jit(solution)/shard_map/ppermute | solution.py:775
  21.4 5.0 %collective-permute-start.3 = (f32[200,128]{1,0:T(8,128)S(1)}, f32[200,128]{1,0:T(8,128)S(1)}, u32[]{:S(2)}, u32[]{:S(2)}) collective-permute-start(f32[200,128]{1,0:T(8,128)S(1)} %slice_add_fusion), channel_id=1, source_target_pairs={{0,16},{8,24},{16,0},{24,8},{1,17},{9,25},{17,1},{25,9},{2,18},{10... | collective-permute-start | bytes 307208 | tf_op jit(solution)/shard_map/ppermute | solution.py:781

commit v11 on v9

--- a/solution.py
+++ b/solution.py
@@ -262,6 +262,11 @@
     return me ^ k
 
 
+def loop_rows(count):
+    sizes = range(10, 16, 2)
+    return min(sizes, key=lambda size: (-(-count // size) * (size + 1), size))
+
+
 def owner_of(me, k, owners):
     chips = owners // 2
     chip, core = me // 2, me % 2
@@ -355,7 +360,7 @@
     offsets = [0]
     for step in range(1, STEPS + 1):
         low, high = step, width - step
-        chunk = 8 if (high - low) % 8 == 0 else 10
+        chunk = loop_rows(high - low)
         offset = offsets[-1]
         offsets.append(offset + high - low)
 
@@ -444,6 +449,54 @@
     )(*fields, *params, target_cells.reshape(1, targets), patch_lists)
 
 
+def packed_rows(slots, patch):
+    return slots * (patch // 2) + -(-slots // 8) * 8
+
+
+def pack_products(list_hot_ref, owner, feature_ref, out_ref, place, slots):
+    patch = out_ref.shape[1]
+    half = patch // 2
+    base = place * packed_rows(slots, patch)
+    row = lax.broadcasted_iota(jnp.int32, (half, patch), 0)
+    lane = lax.broadcasted_iota(jnp.int32, (half, patch), 1)
+    from_last = (lane < half) & (row > lane)
+    chosen = lax.dot_general(
+        list_hot_ref[pl.ds(owner * slots * patch, slots * patch), :],
+        feature_ref[...],
+        NT,
+        preferred_element_type=jnp.float32,
+    ).astype(jnp.bfloat16)
+    diagonals = []
+    for s in range(slots):
+        mine = chosen[s * patch : (s + 1) * patch]
+        gram = lax.dot_general(mine, mine, NT, preferred_element_type=jnp.float32)
+        last = pltpu.roll(gram[half:], half, 1)
+        out_ref[pl.ds(base + s * half, half), :] = jnp.where(from_last, last, gram[:half])
+        diagonals.append(jnp.sum(jnp.where(row == lane, last, 0.0), 0, keepdims=True))
+    while len(diagonals) % 8:
+        diagonals.append(jnp.zeros((1, patch), jnp.float32))
+    out_ref[pl.ds(base + slots * half, len(diagonals)), :] = jnp.concatenate(diagonals, 0)
+
+
+def own_kernel(list_hot_ref, feature_ref, *out_refs, slots):
+    for k, out_ref in enumerate(out_refs):
+        pack_products(list_hot_ref, k, feature_ref, out_ref, 0, slots)
+
+
+def own_products(list_hot, features, chips, slots, patch):
+    vmem = pl.BlockSpec(memory_space=pltpu.VMEM)
+    shape = jax.ShapeDtypeStruct((packed_rows(slots, patch), patch), jnp.float32)
+    return pl.pallas_call(
+        functools.partial(own_kernel, slots=slots),
+        in_specs=[vmem] * 2,
+        out_specs=[vmem] * chips,
+        out_shape=[shape] * chips,
+        compiler_params=compiler_params(24),
+        cost_estimate=pl.CostEstimate(flops=512 * MIB, bytes_accessed=2 * MIB, transcendentals=0),
+        name="own_products",
+    )(list_hot, features)
+
+
 def finish_kernel(
     even_ref,
     odd_ref,
@@ -460,9 +513,9 @@
     final_ref,
     *rest,
     width,
+    slots,
 ):
-    packed_refs = rest[:-6]
-    level_ref, prior_ref, coef_ref, feature_ref, out_ref, out_sem = rest[-6:]
+    feature_ref, beside_ref, level_ref, prior_ref, coef_ref, out_ref, out_sem = rest
     shots, depth = edge_ref.shape[-2:]
     targets = column_ref.shape[1]
     first = -STEPS
@@ -561,33 +614,9 @@
     out_copy = pltpu.make_async_copy(out_ref, spectra_out_ref, out_sem)
     out_copy.start()
 
-    chips = len(packed_refs) - 1
-    owners = 2 * chips
-    size, patch = packed_refs[0].shape
-    slots = list_hot_ref.shape[0] // (owners * patch)
-    half = patch // 2
-    row = lax.broadcasted_iota(jnp.int32, (half, patch), 0)
-    lane = lax.broadcasted_iota(jnp.int32, (half, patch), 1)
-    from_last = (lane < half) & (row > lane)
-    for g in range(owners):
-        packed_ref = packed_refs[min(g, chips)]
-        base = max(g - chips, 0) * size
-        chosen = lax.dot_general(
-            list_hot_ref[pl.ds(g * slots * patch, slots * patch), :],
-            feature_ref[...],
-            NT,
-            preferred_element_type=jnp.float32,
-        ).astype(jnp.bfloat16)
-        diagonals = []
-        for s in range(slots):
-            mine = chosen[s * patch : (s + 1) * patch]
-            gram = lax.dot_general(mine, mine, NT, preferred_element_type=jnp.float32)
-            last = pltpu.roll(gram[half:], half, 1)
-            packed_ref[pl.ds(base + s * half, half), :] = jnp.where(from_last, last, gram[:half])
-            diagonals.append(jnp.sum(jnp.where(row == lane, last, 0.0), 0, keepdims=True))
-        while len(diagonals) % 8:
-            diagonals.append(jnp.zeros((1, patch), jnp.float32))
-        packed_ref[pl.ds(base + slots * half, len(diagonals)), :] = jnp.concatenate(diagonals, 0)
+    chips = beside_ref.shape[0] // packed_rows(slots, beside_ref.shape[1])
+    for k in range(chips):
+        pack_products(list_hot_ref, chips + k, feature_ref, beside_ref, k, slots)
     out_copy.wait()
 
 
@@ -597,16 +626,16 @@
     targets = column.shape[1]
     features = spectra.shape[0]
     f32 = functools.partial(jax.ShapeDtypeStruct, dtype=jnp.float32)
-    rows = slots * (patch // 2) + -(-slots // 8) * 8
+    rows = packed_rows(slots, patch)
     out_shape = [
         f32((features, targets)),
         f32((2, 2, STEPS, shots, depth)),
-        *[f32((rows, patch))] * (owners // 2),
+        jax.ShapeDtypeStruct((features, targets), jnp.bfloat16),
         f32((owners // 2 * rows, patch)),
     ]
     vmem = pl.BlockSpec(memory_space=pltpu.VMEM)
     return pl.pallas_call(
-        functools.partial(finish_kernel, width=width),
+        functools.partial(finish_kernel, width=width, slots=slots),
         in_specs=[vmem] * 11,
         out_specs=[pl.BlockSpec(memory_space=pl.ANY)] + [vmem] * (len(out_shape) - 1),
         out_shape=out_shape,
@@ -614,7 +643,6 @@
             pltpu.VMEM((2, 2, STEPS, 2 * STEPS + 1, shots, depth), jnp.float32),
             pltpu.VMEM((2, 2, STEPS, shots, depth), jnp.float32),
             pltpu.VMEM((2, 5, depth // LANES, 2 * STEPS, LANES), jnp.float32),
-            pltpu.VMEM((features, targets), jnp.bfloat16),
             pltpu.VMEM((features, targets), jnp.float32),
             pltpu.SemaphoreType.DMA,
         ],
@@ -741,7 +769,7 @@
     edge, prior_edge, coef_edge, p_inner, q_inner, sample, depth_hot, column, list_hot = interior(
         fields, params, target_cells, patch_lists
     )
-    spectra_out, final, *packed = finish(
+    spectra_out, final, features, for_beside = finish(
         even,
         odd,
         (edge, prior_edge, coef_edge, sample, depth_hot, column, list_hot),
@@ -753,7 +781,8 @@
         patch,
     )
     chips = owners // 2
-    beside = lax.ppermute(packed[chips], "shot", [(i, i ^ 1) for i in range(owners)])
+    beside = lax.ppermute(for_beside, "shot", [(i, i ^ 1) for i in range(owners)])
+    packed = own_products(list_hot, features, chips, slots, patch)
     received = [packed[0], beside]
     size = packed[0].shape[0]
     for k in range(1, chips):

time: 25.7 us -> 24.8 us (0.965)
  the two profiles are of different devices: /device:TPU:18 before, /device:TPU:6 now
where the time goes in v11:
time: 24.8 us; the launch traced here: 24.6 us
  Pallas kernels  14.5 us (58%)
  starting transfers between devices  5.64 us (23%)
  waiting for transfers between devices  2.54 us (10%)
  between operations  1.54 us (6%)
    pallas_call x1, Pallas kernels, interior(): pl.pallas_call(interior_kernel, in_specs=[vmem] * 10, out_specs=[vmem] *...  6.19 us
    ppermute x2, starting transfers between devices, shards(): swapped.append(lax.ppermute(rows, 'brick', pairs))  5 us
    pallas_call x1, Pallas kernels, finish(): pl.pallas_call(functools.partial(finish_kernel, width=width, slots=slots)...  2.42 us
    pallas_call x1, Pallas kernels, outer_rows(): pl.pallas_call(outer_kernel, in_specs=[pl.BlockSpec(memory_space=pltpu.HB...  2.38 us
    ppermute x1, waiting for transfers between devices, shards(): received.append(lax.ppermute(both, 'shot', pairs))  2.11 us
    pallas_call x1, Pallas kernels, assemble(): pl.pallas_call(assemble_kernel, in_specs=[vmem] * 3, out_specs=[vmem] * 2...  1.66 us
    pallas_call x1, Pallas kernels, own_products(): pl.pallas_call(functools.partial(own_kernel, slots=slots), in_specs=[vmem...  1.01 us
    pallas_call x1, Pallas kernels, tiles(): pl.pallas_call(functools.partial(tiles_kernel, features=features), in_spe...  0.87 us
  transfers between devices with their start and end apart: 4, of which 2 were waited for; matrix products, arithmetic and copies ran while one was open for 1% of the time, Pallas kernels for 36%

profile of v11, /device:TPU:6, one launch (start us, length us, event | category | flops | bytes accessed | tf_op | source)
XLA Modules:
  0.0 24.6 jit_solution(5803048957625940497)
XLA Ops:
  0.6 0.0 copy-start
  0.6 0.0 copy-start.1
  0.7 0.0 copy-start.2
  0.7 0.0 copy-start.3
  0.7 0.0 copy-start.5
  0.7 0.0 copy-start.6
  0.7 0.0 copy-start.7
  0.7 0.0 copy-start.8
  0.7 0.0 copy-start.11
  0.7 0.0 copy-start.10
  0.7 0.0 copy-start.9
  0.7 2.4 %outer_rows.1 = (bf16[160,512]{1,0:T(8,128)(2,1)}, bf16[160,512]{1,0:T(8,128)(2,1)}) custom-call(f32[8,4,4,8,128]{4,3,2,1,0:T(8,128)} %bitcast.21, f32[8,4,4,8,128]{4,3,2,1,0:T(8,128)} %bitcast.23, f32[8,4,4,8,128]{4,3,2,1,0:T(8,128)} %bitcast.25, f32[8,4,4,8,128]{4,3,2,1,0:T(8,128)} %bitcast.27, f32[32,512]{1,0:T(8,128)} %refs_4_.1, f32[32,512]{1,0:T(8,128)} %refs_5_.1, ...), custom_call_target="tpu_custom_call" | custom-call | tf_op jit(solution)/shard_map/outer_rows/pallas_call | solution.py:243
  3.1 0.0 copy-start.4
  3.1 0.6 %collective-permute-start = (bf16[160,512]{1,0:T(8,128)(2,1)}, bf16[160,512]{1,0:T(8,128)(2,1)S(1)}, u32[]{:S(2)}, u32[]{:S(2)}) collective-permute-start(bf16[160,512]{1,0:T(8,128)(2,1)} %get-tuple-element.25), channel_id=1, source_target_pairs={{0,1},{1,0},{2,3},{3,2},{4,5},{5,4},{6,7},{7,6},{8,9},{9,8},{10,11... | collective-permute-start | bytes 491528 | tf_op jit(solution)/shard_map/ppermute | solution.py:761
  3.7 4.4 %collective-permute-start.1 = (bf16[160,512]{1,0:T(8,128)(2,1)}, bf16[160,512]{1,0:T(8,128)(2,1)S(1)}, u32[]{:S(2)}, u32[]{:S(2)}) collective-permute-start(bf16[160,512]{1,0:T(8,128)(2,1)} %get-tuple-element.26), channel_id=1, source_target_pairs={{1,2},{2,1},{3,4},{4,3},{5,6},{6,5},{9,10},{10,9},{11,12},{12,11},... | collective-permute-start | bytes 491528 | tf_op jit(solution)/shard_map/ppermute | solution.py:761
  8.2 0.0 copy-done.11
  8.2 0.1 multiply_cosine_fusion
  8.3 0.0 copy-done.10
  8.3 0.0 copy-done
  8.3 0.0 copy-done.1
  8.3 0.0 copy-done.2
  8.3 0.0 copy-done.3
  8.3 0.0 copy-done.5
  8.4 0.0 copy-done.6
  8.4 0.0 copy-done.7
  8.4 0.0 copy-done.8
  8.4 0.0 copy-done.9
  8.4 6.2 %interior.1 = (f32[2,2,4,2,8,512]{5,4,3,2,1,0:T(8,128)S(1)}, f32[2,2,8,512]{3,2,1,0:T(8,128)S(1)}, f32[2,5,8,512]{3,2,1,0:T(8,128)S(1)}, f32[24,8,512]{2,1,0:T(8...) custom-call(f32[8,4,4,8,128]{4,3,2,1,0:T(8,128)S(1)} %bitcast.22, ...), custom_call_target="tpu_custom_call" | custom-call | flops 104857600 | bytes 8388608 | tf_op jit(solution)/shard_map/interior/pallas_call | solution.py:434
  14.6 0.1 pad_maximum_fusion
  14.7 0.0 collective-permute-done.even_ref
  14.7 0.0 collective-permute-done.1.odd_ref
  14.7 0.1 broadcast_in_dim.2.table_ref
  14.7 0.0 copy-done.4
  14.8 2.4 %finish.1 = (f32[256,512]{1,0:T(8,128)}, f32[2,2,4,8,512]{4,3,2,1,0:T(8,128)S(1)}, bf16[256,512]{1,0:T(8,128)(2,1)S(1)}, f32[400,128]{1,0:T(8,128)S(1)}) custom-call(bf16[160,512]{1,0:T(8,128)(2,1)S(1)} %collective-permute-done.even_ref, bf16[160,512]{1,0:T(8,128)(2,1)S(1)} %collective-permute-done.1.odd_ref, ...), custom_call_target="tpu_custom_call" | custom-call | tf_op jit(solution)/shard_map/finish/pallas_call | solution.py:637
  17.2 0.1 collective-permute-start.2
  17.3 1.0 %own_products.1 = (f32[200,128]{1,0:T(8,128)S(1)}, f32[200,128]{1,0:T(8,128)S(1)}) custom-call(bf16[1536,512]{1,0:T(8,128)(2,1)S(1)} %get-tuple-element.33.list_hot_ref, bf16[256,512]{1,0:T(8,128)(2,1)S(1)} %get-tuple-element.38.feature_ref), custom_call_target="tpu_custom_call" | custom-call | flops 536870912 | bytes 2097152 | tf_op jit(solution)/shard_map/own_products/pallas_call | solution.py:489
  18.3 0.4 %collective-permute-done.2.refs_1_ = f32[400,128]{1,0:T(8,128)S(1)} collective-permute-done((f32[400,128]{1,0:T(8,128)S(1)}, f32[400,128]{1,0:T(8,128)S(1)}, u32[]{:S(2)}, u32[]{:S(2)}) %collective-permute-start.2) | collective-permute-done | bytes 204832 | tf_op jit(solution)/shard_map/ppermute | solution.py:784
  18.7 0.6 %collective-permute-start.3 = (f32[200,128]{1,0:T(8,128)S(1)}, f32[200,128]{1,0:T(8,128)S(1)}, u32[]{:S(2)}, u32[]{:S(2)}) collective-permute-start(f32[200,128]{1,0:T(8,128)S(1)} %slice_add_fusion), channel_id=1, source_target_pairs={{0,16},{8,24},{16,0},{24,8},{1,17},{9,25},{17,1},{25,9},{2,18},{10... | collective-permute-start | bytes 307208 | tf_op jit(solution)/shard_map/ppermute | solution.py:791
  19.9 1.7 %assemble.1 = (f32[8,4,4,8,128]{4,3,2,1,0:T(8,128)}, f32[8,4,4,8,128]{4,3,2,1,0:T(8,128)}) custom-call(f32[24,8,512]{2,1,0:T(8,128)S(1)} %get-tuple-element.23.p_inner_ref, f32[24,8,512]{2,1,0:T(8,128)S(1)} %get-tuple-element.24.q_inner_ref, f32[2,2,4,8,512]{4,3,2,1,0:T(8,128)S(1)} %get-tuple-element.34.final_ref), custom_call_target="tpu_custom_call" | custom-call | flops 8388608 | bytes 4194304 | tf_op jit(solution)/shard_map/assemble/pallas_call | solution.py:684
  21.6 2.1 %collective-permute-done.3.refs_2_ = f32[200,128]{1,0:T(8,128)S(1)} collective-permute-done((f32[200,128]{1,0:T(8,128)S(1)}, f32[200,128]{1,0:T(8,128)S(1)}, u32[]{:S(2)}, u32[]{:S(2)}) %collective-permute-start.3) | collective-permute-done | bytes 102432 | tf_op jit(solution)/shard_map/ppermute | solution.py:791
  23.7 0.9 %tiles.1 = f32[1,1,3,128,128]{4,3,2,1,0:T(8,128)} custom-call(s32[1,1]{1,0:T(1,128)S(6)} %copy.18.counts_ref, f32[200,128]{1,0:T(8,128)S(1)} %get-tuple-element.39.refs_0_, f32[400,128]{1,0:T(8,128)S(1)} %collective-permute-done.2.refs_1_, f32[200,128]{1,0:T(8,128)S(1)} %collective-permute-done.3.refs_2_), custom_call_target="tpu_custom_call" | custom-call | tf_op jit(solution)/shard_map/tiles/pallas_call | solution.py:723
  (3 shorter events, 0.0 us)
Async XLA Ops:
  0.6 7.7 %copy-start = (f32[8,32,512]{2,1,0:T(8,128)S(1)}, f32[8,32,512]{2,1,0:T(8,128)}, u32[]{:S(2)}) copy-start(f32[8,32,512]{2,1,0:T(8,128)} %param.13) | copy-start | bytes 1572868
  0.6 7.7 %copy-start.1 = (f32[8,32,512]{2,1,0:T(8,128)S(1)}, f32[8,32,512]{2,1,0:T(8,128)}, u32[]{:S(2)}) copy-start(f32[8,32,512]{2,1,0:T(8,128)} %param.14) | copy-start | bytes 1572868
  0.7 7.7 %copy-start.2 = (f32[8,32,512]{2,1,0:T(8,128)S(1)}, f32[8,32,512]{2,1,0:T(8,128)}, u32[]{:S(2)}) copy-start(f32[8,32,512]{2,1,0:T(8,128)} %param.15) | copy-start | bytes 1572868
  0.7 7.7 %copy-start.3 = (f32[8,32,512]{2,1,0:T(8,128)S(1)}, f32[8,32,512]{2,1,0:T(8,128)}, u32[]{:S(2)}) copy-start(f32[8,32,512]{2,1,0:T(8,128)} %param.16) | copy-start | bytes 1572868
  0.7 7.7 %copy-start.5 = (f32[32,512]{1,0:T(8,128)S(1)}, f32[32,512]{1,0:T(8,128)}, u32[]{:S(2)}) copy-start(f32[32,512]{1,0:T(8,128)} %refs_4_.1) | copy-start | bytes 196612
  0.7 7.7 %copy-start.6 = (f32[32,512]{1,0:T(8,128)S(1)}, f32[32,512]{1,0:T(8,128)}, u32[]{:S(2)}) copy-start(f32[32,512]{1,0:T(8,128)} %refs_5_.1) | copy-start | bytes 196612
  0.7 7.7 %copy-start.7 = (f32[32,512]{1,0:T(8,128)S(1)}, f32[32,512]{1,0:T(8,128)}, u32[]{:S(2)}) copy-start(f32[32,512]{1,0:T(8,128)} %refs_6_.1) | copy-start | bytes 196612
  0.7 7.7 %copy-start.8 = (f32[32,512]{1,0:T(8,128)S(1)}, f32[32,512]{1,0:T(8,128)}, u32[]{:S(2)}) copy-start(f32[32,512]{1,0:T(8,128)} %refs_7_.1) | copy-start | bytes 196612
  0.7 7.5 %copy-start.11 = (f32[16]{0:T(128)S(1)}, f32[16]{0:T(128)}, u32[]{:S(2)}) copy-start(f32[16]{0:T(128)} %param.21) | copy-start | bytes 196
  0.7 7.6 %copy-start.10 = (s32[1,4,3,128]{3,1,2,0:T(4,128)S(1)}, s32[1,4,3,128]{3,1,2,0:T(4,128)}, u32[]{:S(2)}) copy-start(s32[1,4,3,128]{3,1,2,0:T(4,128)} %param.24) | copy-start | bytes 18436
  0.7 7.7 %copy-start.9 = (s32[512]{0:T(512)S(1)}, s32[512]{0:T(512)}, u32[]{:S(2)}) copy-start(s32[512]{0:T(512)} %param.23) | copy-start | bytes 6148
  3.1 11.6 %copy-start.4 = (f32[8,32,512]{2,1,0:T(8,128)S(1)}, f32[8,32,512]{2,1,0:T(8,128)}, u32[]{:S(2)}) copy-start(f32[8,32,512]{2,1,0:T(8,128)} %param.22) | copy-start | bytes 1572868
  3.1 11.5 %collective-permute-start = (bf16[160,512]{1,0:T(8,128)(2,1)}, bf16[160,512]{1,0:T(8,128)(2,1)S(1)}, u32[]{:S(2)}, u32[]{:S(2)}) collective-permute-start(bf16[160,512]{1,0:T(8,128)(2,1)} %get-tuple-element.25), channel_id=1, source_target_pairs={{0,1},{1,0},{2,3},{3,2},{4,5},{5,4},{6,7},{7,6},{8,9},{9,8},{10,11... | collective-permute-start | bytes 491528 | tf_op jit(solution)/shard_map/ppermute | solution.py:761
  3.7 10.9 %collective-permute-start.1 = (bf16[160,512]{1,0:T(8,128)(2,1)}, bf16[160,512]{1,0:T(8,128)(2,1)S(1)}, u32[]{:S(2)}, u32[]{:S(2)}) collective-permute-start(bf16[160,512]{1,0:T(8,128)(2,1)} %get-tuple-element.26), channel_id=1, source_target_pairs={{1,2},{2,1},{3,4},{4,3},{5,6},{6,5},{9,10},{10,9},{11,12},{12,11},... | collective-permute-start | bytes 491528 | tf_op jit(solution)/shard_map/ppermute | solution.py:761
  17.2 1.5 %collective-permute-start.2 = (f32[400,128]{1,0:T(8,128)S(1)}, f32[400,128]{1,0:T(8,128)S(1)}, u32[]{:S(2)}, u32[]{:S(2)}) collective-permute-start(f32[400,128]{1,0:T(8,128)S(1)} %get-tuple-element.40), channel_id=1, source_target_pairs={{0,8},{8,0},{16,24},{24,16},{1,9},{9,1},{17,25},{25,17},{2,10},{10... | collective-permute-start | bytes 614408 | tf_op jit(solution)/shard_map/ppermute | solution.py:784
  18.7 5.0 %collective-permute-start.3 = (f32[200,128]{1,0:T(8,128)S(1)}, f32[200,128]{1,0:T(8,128)S(1)}, u32[]{:S(2)}, u32[]{:S(2)}) collective-permute-start(f32[200,128]{1,0:T(8,128)S(1)} %slice_add_fusion), channel_id=1, source_target_pairs={{0,16},{8,24},{16,0},{24,8},{1,17},{9,25},{17,1},{25,9},{2,18},{10... | collective-permute-start | bytes 307208 | tf_op jit(solution)/shard_map/ppermute | solution.py:791

commit v12 on v11

--- a/solution.py
+++ b/solution.py
@@ -263,7 +263,7 @@
 
 
 def loop_rows(count):
-    sizes = range(10, 16, 2)
+    sizes = range(10, 32, 2)
     return min(sizes, key=lambda size: (-(-count // size) * (size + 1), size))
 
 

time: 24.8 us -> 23.6 us (0.952)
  the two profiles are of different devices: /device:TPU:6 before, /device:TPU:16 now
where the time goes in v12:
time: 23.6 us; the launch traced here: 23.3 us
  Pallas kernels  13.2 us (56%)
  starting transfers between devices  5.52 us (23%)
  waiting for transfers between devices  2.67 us (11%)
  between operations  1.54 us (7%)
    pallas_call x1, Pallas kernels, interior(): pl.pallas_call(interior_kernel, in_specs=[vmem] * 10, out_specs=[vmem] *...  4.85 us
    ppermute x2, starting transfers between devices, shards(): swapped.append(lax.ppermute(rows, 'brick', pairs))  3.87 us
    pallas_call x1, Pallas kernels, finish(): pl.pallas_call(functools.partial(finish_kernel, width=width, slots=slots)...  2.41 us
    pallas_call x1, Pallas kernels, outer_rows(): pl.pallas_call(outer_kernel, in_specs=[pl.BlockSpec(memory_space=pltpu.HB...  2.38 us
    pallas_call x1, Pallas kernels, assemble(): pl.pallas_call(assemble_kernel, in_specs=[vmem] * 3, out_specs=[vmem] * 2...  1.66 us
    ppermute x1, starting transfers between devices, shards(): received.append(lax.ppermute(both, 'shot', pairs))  1.58 us
    ppermute x2, waiting for transfers between devices, shards(): swapped.append(lax.ppermute(rows, 'brick', pairs))  1.15 us
    ppermute x1, waiting for transfers between devices, shards(): received.append(lax.ppermute(both, 'shot', pairs))  1.1 us
  transfers between devices with their start and end apart: 4, of which 3 were waited for; matrix products, arithmetic and copies ran while one was open for 1% of the time, Pallas kernels for 32%

profile of v12, /device:TPU:16, one launch (start us, length us, event | category | flops | bytes accessed | tf_op | source)
XLA Modules:
  0.0 23.3 jit_solution(11974082448018332972)
XLA Ops:
  0.6 0.0 copy-start
  0.6 0.0 copy-start.1
  0.7 0.0 copy-start.2
  0.7 0.0 copy-start.3
  0.7 0.0 copy-start.5
  0.7 0.0 copy-start.6
  0.7 0.0 copy-start.7
  0.7 0.0 copy-start.8
  0.7 0.0 copy-start.11
  0.7 0.0 copy-start.10
  0.7 0.0 copy-start.9
  0.7 2.4 %outer_rows.1 = (bf16[160,512]{1,0:T(8,128)(2,1)}, bf16[160,512]{1,0:T(8,128)(2,1)}) custom-call(f32[8,4,4,8,128]{4,3,2,1,0:T(8,128)} %bitcast.21, f32[8,4,4,8,128]{4,3,2,1,0:T(8,128)} %bitcast.23, f32[8,4,4,8,128]{4,3,2,1,0:T(8,128)} %bitcast.25, f32[8,4,4,8,128]{4,3,2,1,0:T(8,128)} %bitcast.27, f32[32,512]{1,0:T(8,128)} %refs_4_.1, f32[32,512]{1,0:T(8,128)} %refs_5_.1, ...), custom_call_target="tpu_custom_call" | custom-call | tf_op jit(solution)/shard_map/outer_rows/pallas_call | solution.py:243
  3.1 0.0 copy-start.4
  3.1 1.6 %collective-permute-start = (bf16[160,512]{1,0:T(8,128)(2,1)}, bf16[160,512]{1,0:T(8,128)(2,1)S(1)}, u32[]{:S(2)}, u32[]{:S(2)}) collective-permute-start(bf16[160,512]{1,0:T(8,128)(2,1)} %get-tuple-element.25), channel_id=1, source_target_pairs={{0,1},{1,0},{2,3},{3,2},{4,5},{5,4},{6,7},{7,6},{8,9},{9,8},{10,11... | collective-permute-start | bytes 491528 | tf_op jit(solution)/shard_map/ppermute | solution.py:761
  4.7 2.3 %collective-permute-start.1 = (bf16[160,512]{1,0:T(8,128)(2,1)}, bf16[160,512]{1,0:T(8,128)(2,1)S(1)}, u32[]{:S(2)}, u32[]{:S(2)}) collective-permute-start(bf16[160,512]{1,0:T(8,128)(2,1)} %get-tuple-element.26), channel_id=1, source_target_pairs={{1,2},{2,1},{3,4},{4,3},{5,6},{6,5},{9,10},{10,9},{11,12},{12,11},... | collective-permute-start | bytes 491528 | tf_op jit(solution)/shard_map/ppermute | solution.py:761
  7.0 0.0 copy-done.11
  7.0 0.1 multiply_cosine_fusion
  7.2 0.0 copy-done.10
  7.2 0.0 copy-done
  7.2 0.0 copy-done.1
  7.2 0.0 copy-done.2
  7.2 0.0 copy-done.3
  7.2 0.0 copy-done.5
  7.2 0.0 copy-done.6
  7.2 0.0 copy-done.7
  7.2 0.0 copy-done.8
  7.3 0.0 copy-done.9
  7.3 4.9 %interior.1 = (f32[2,2,4,2,8,512]{5,4,3,2,1,0:T(8,128)S(1)}, f32[2,2,8,512]{3,2,1,0:T(8,128)S(1)}, f32[2,5,8,512]{3,2,1,0:T(8,128)S(1)}, f32[24,8,512]{2,1,0:T(8...) custom-call(f32[8,4,4,8,128]{4,3,2,1,0:T(8,128)S(1)} %bitcast.22, ...), custom_call_target="tpu_custom_call" | custom-call | flops 104857600 | bytes 8388608 | tf_op jit(solution)/shard_map/interior/pallas_call | solution.py:434
  12.1 0.1 pad_maximum_fusion
  12.2 0.0 collective-permute-done.even_ref
  12.2 1.1 %collective-permute-done.1.odd_ref = bf16[160,512]{1,0:T(8,128)(2,1)S(1)} collective-permute-done((bf16[160,512]{1,0:T(8,128)(2,1)}, bf16[160,512]{1,0:T(8,128)(2,1)S(1)}, u32[]{:S(2)}, u32[]{:S(2)}) %collective-permute-start.1) | collective-permute-done | bytes 163872 | tf_op jit(solution)/shard_map/ppermute | solution.py:761
  13.4 0.1 broadcast_in_dim.2.table_ref
  13.4 0.0 copy-done.4
  13.4 2.4 %finish.1 = (f32[256,512]{1,0:T(8,128)}, f32[2,2,4,8,512]{4,3,2,1,0:T(8,128)S(1)}, bf16[256,512]{1,0:T(8,128)(2,1)S(1)}, f32[400,128]{1,0:T(8,128)S(1)}) custom-call(bf16[160,512]{1,0:T(8,128)(2,1)S(1)} %collective-permute-done.even_ref, bf16[160,512]{1,0:T(8,128)(2,1)S(1)} %collective-permute-done.1.odd_ref, ...), custom_call_target="tpu_custom_call" | custom-call | tf_op jit(solution)/shard_map/finish/pallas_call | solution.py:637
  15.9 0.1 collective-permute-start.2
  15.9 1.0 %own_products.1 = (f32[200,128]{1,0:T(8,128)S(1)}, f32[200,128]{1,0:T(8,128)S(1)}) custom-call(bf16[1536,512]{1,0:T(8,128)(2,1)S(1)} %get-tuple-element.33.list_hot_ref, bf16[256,512]{1,0:T(8,128)(2,1)S(1)} %get-tuple-element.38.feature_ref), custom_call_target="tpu_custom_call" | custom-call | flops 536870912 | bytes 2097152 | tf_op jit(solution)/shard_map/own_products/pallas_call | solution.py:489
  16.9 0.4 %collective-permute-done.2.refs_1_ = f32[400,128]{1,0:T(8,128)S(1)} collective-permute-done((f32[400,128]{1,0:T(8,128)S(1)}, f32[400,128]{1,0:T(8,128)S(1)}, u32[]{:S(2)}, u32[]{:S(2)}) %collective-permute-start.2) | collective-permute-done | bytes 204832 | tf_op jit(solution)/shard_map/ppermute | solution.py:784
  17.4 1.6 %collective-permute-start.3 = (f32[200,128]{1,0:T(8,128)S(1)}, f32[200,128]{1,0:T(8,128)S(1)}, u32[]{:S(2)}, u32[]{:S(2)}) collective-permute-start(f32[200,128]{1,0:T(8,128)S(1)} %slice_add_fusion), channel_id=1, source_target_pairs={{0,16},{8,24},{16,0},{24,8},{1,17},{9,25},{17,1},{25,9},{2,18},{10... | collective-permute-start | bytes 307208 | tf_op jit(solution)/shard_map/ppermute | solution.py:791
  19.6 1.7 %assemble.1 = (f32[8,4,4,8,128]{4,3,2,1,0:T(8,128)}, f32[8,4,4,8,128]{4,3,2,1,0:T(8,128)}) custom-call(f32[24,8,512]{2,1,0:T(8,128)S(1)} %get-tuple-element.23.p_inner_ref, f32[24,8,512]{2,1,0:T(8,128)S(1)} %get-tuple-element.24.q_inner_ref, f32[2,2,4,8,512]{4,3,2,1,0:T(8,128)S(1)} %get-tuple-element.34.final_ref), custom_call_target="tpu_custom_call" | custom-call | flops 8388608 | bytes 4194304 | tf_op jit(solution)/shard_map/assemble/pallas_call | solution.py:684
  21.3 1.1 %collective-permute-done.3.refs_2_ = f32[200,128]{1,0:T(8,128)S(1)} collective-permute-done((f32[200,128]{1,0:T(8,128)S(1)}, f32[200,128]{1,0:T(8,128)S(1)}, u32[]{:S(2)}, u32[]{:S(2)}) %collective-permute-start.3) | collective-permute-done | bytes 102432 | tf_op jit(solution)/shard_map/ppermute | solution.py:791
  22.4 0.9 %tiles.1 = f32[1,1,3,128,128]{4,3,2,1,0:T(8,128)} custom-call(s32[1,1]{1,0:T(1,128)S(6)} %copy.18.counts_ref, f32[200,128]{1,0:T(8,128)S(1)} %get-tuple-element.39.refs_0_, f32[400,128]{1,0:T(8,128)S(1)} %collective-permute-done.2.refs_1_, f32[200,128]{1,0:T(8,128)S(1)} %collective-permute-done.3.refs_2_), custom_call_target="tpu_custom_call" | custom-call | tf_op jit(solution)/shard_map/tiles/pallas_call | solution.py:723
  (3 shorter events, 0.0 us)
Async XLA Ops:
  0.6 6.5 %copy-start = (f32[8,32,512]{2,1,0:T(8,128)S(1)}, f32[8,32,512]{2,1,0:T(8,128)}, u32[]{:S(2)}) copy-start(f32[8,32,512]{2,1,0:T(8,128)} %param.13) | copy-start | bytes 1572868
  0.6 6.5 %copy-start.1 = (f32[8,32,512]{2,1,0:T(8,128)S(1)}, f32[8,32,512]{2,1,0:T(8,128)}, u32[]{:S(2)}) copy-start(f32[8,32,512]{2,1,0:T(8,128)} %param.14) | copy-start | bytes 1572868
  0.7 6.5 %copy-start.2 = (f32[8,32,512]{2,1,0:T(8,128)S(1)}, f32[8,32,512]{2,1,0:T(8,128)}, u32[]{:S(2)}) copy-start(f32[8,32,512]{2,1,0:T(8,128)} %param.15) | copy-start | bytes 1572868
  0.7 6.5 %copy-start.3 = (f32[8,32,512]{2,1,0:T(8,128)S(1)}, f32[8,32,512]{2,1,0:T(8,128)}, u32[]{:S(2)}) copy-start(f32[8,32,512]{2,1,0:T(8,128)} %param.16) | copy-start | bytes 1572868
  0.7 6.5 %copy-start.5 = (f32[32,512]{1,0:T(8,128)S(1)}, f32[32,512]{1,0:T(8,128)}, u32[]{:S(2)}) copy-start(f32[32,512]{1,0:T(8,128)} %refs_4_.1) | copy-start | bytes 196612
  0.7 6.5 %copy-start.6 = (f32[32,512]{1,0:T(8,128)S(1)}, f32[32,512]{1,0:T(8,128)}, u32[]{:S(2)}) copy-start(f32[32,512]{1,0:T(8,128)} %refs_5_.1) | copy-start | bytes 196612
  0.7 6.5 %copy-start.7 = (f32[32,512]{1,0:T(8,128)S(1)}, f32[32,512]{1,0:T(8,128)}, u32[]{:S(2)}) copy-start(f32[32,512]{1,0:T(8,128)} %refs_6_.1) | copy-start | bytes 196612
  0.7 6.5 %copy-start.8 = (f32[32,512]{1,0:T(8,128)S(1)}, f32[32,512]{1,0:T(8,128)}, u32[]{:S(2)}) copy-start(f32[32,512]{1,0:T(8,128)} %refs_7_.1) | copy-start | bytes 196612
  0.7 6.3 %copy-start.11 = (f32[16]{0:T(128)S(1)}, f32[16]{0:T(128)}, u32[]{:S(2)}) copy-start(f32[16]{0:T(128)} %param.21) | copy-start | bytes 196
  0.7 6.4 %copy-start.10 = (s32[1,4,3,128]{3,1,2,0:T(4,128)S(1)}, s32[1,4,3,128]{3,1,2,0:T(4,128)}, u32[]{:S(2)}) copy-start(s32[1,4,3,128]{3,1,2,0:T(4,128)} %param.24) | copy-start | bytes 18436
  0.7 6.5 %copy-start.9 = (s32[512]{0:T(512)S(1)}, s32[512]{0:T(512)}, u32[]{:S(2)}) copy-start(s32[512]{0:T(512)} %param.23) | copy-start | bytes 6148
  3.1 10.3 %copy-start.4 = (f32[8,32,512]{2,1,0:T(8,128)S(1)}, f32[8,32,512]{2,1,0:T(8,128)}, u32[]{:S(2)}) copy-start(f32[8,32,512]{2,1,0:T(8,128)} %param.22) | copy-start | bytes 1572868
  3.1 9.1 %collective-permute-start = (bf16[160,512]{1,0:T(8,128)(2,1)}, bf16[160,512]{1,0:T(8,128)(2,1)S(1)}, u32[]{:S(2)}, u32[]{:S(2)}) collective-permute-start(bf16[160,512]{1,0:T(8,128)(2,1)} %get-tuple-element.25), channel_id=1, source_target_pairs={{0,1},{1,0},{2,3},{3,2},{4,5},{5,4},{6,7},{7,6},{8,9},{9,8},{10,11... | collective-permute-start | bytes 491528 | tf_op jit(solution)/shard_map/ppermute | solution.py:761
  4.7 8.7 %collective-permute-start.1 = (bf16[160,512]{1,0:T(8,128)(2,1)}, bf16[160,512]{1,0:T(8,128)(2,1)S(1)}, u32[]{:S(2)}, u32[]{:S(2)}) collective-permute-start(bf16[160,512]{1,0:T(8,128)(2,1)} %get-tuple-element.26), channel_id=1, source_target_pairs={{1,2},{2,1},{3,4},{4,3},{5,6},{6,5},{9,10},{10,9},{11,12},{12,11},... | collective-permute-start | bytes 491528 | tf_op jit(solution)/shard_map/ppermute | solution.py:761
  15.9 1.5 %collective-permute-start.2 = (f32[400,128]{1,0:T(8,128)S(1)}, f32[400,128]{1,0:T(8,128)S(1)}, u32[]{:S(2)}, u32[]{:S(2)}) collective-permute-start(f32[400,128]{1,0:T(8,128)S(1)} %get-tuple-element.40), channel_id=1, source_target_pairs={{0,8},{8,0},{16,24},{24,16},{1,9},{9,1},{17,25},{25,17},{2,10},{10... | collective-permute-start | bytes 614408 | tf_op jit(solution)/shard_map/ppermute | solution.py:784
  17.4 5.0 %collective-permute-start.3 = (f32[200,128]{1,0:T(8,128)S(1)}, f32[200,128]{1,0:T(8,128)S(1)}, u32[]{:S(2)}, u32[]{:S(2)}) collective-permute-start(f32[200,128]{1,0:T(8,128)S(1)} %slice_add_fusion), channel_id=1, source_target_pairs={{0,16},{8,24},{16,0},{24,8},{1,17},{9,25},{17,1},{25,9},{2,18},{10... | collective-permute-start | bytes 307208 | tf_op jit(solution)/shard_map/ppermute | solution.py:791

commit v13 on v12

--- a/solution.py
+++ b/solution.py
@@ -307,8 +307,7 @@
     along = depth // LANES
     p_rows, q_rows, pp_rows, qq_rows = [ShotRows(ref) for ref in (p_ref, q_ref, pp_ref, qq_ref)]
 
-    @pl.loop(0, width, unroll=4)
-    def _(x):
+    for x in range(width):
         level_ref[0, 0, x] = p_rows[x]
         level_ref[0, 1, x] = q_rows[x]
 
@@ -364,9 +363,8 @@
         offset = offsets[-1]
         offsets.append(offset + high - low)
 
-        @pl.loop(0, -(-(high - low) // chunk))
-        def _(index):
-            at = jnp.minimum(chunk * index, high - low - chunk)
+        def run(index):
+            at = 0 if chunk == high - low else jnp.minimum(chunk * index, high - low - chunk)
             start = low + at
             held = []
 
@@ -394,6 +392,11 @@
                 lambda i, r, j: coefficients(i, start + r, j),
                 put,
             )
+
+        if chunk == high - low:
+            run(0)
+        else:
+            pl.loop(0, -(-(high - low) // chunk))(run)
 
     for step in range(STEPS):
         for field in range(2):

time: 23.6 us -> 23.6 us (level)
  no operation moved by 1% of the time
where the time goes in v13:
time: 23.6 us; the launch traced here: 23.3 us
  Pallas kernels  13 us (55%)
  starting transfers between devices  5.52 us (23%)
  waiting for transfers between devices  2.81 us (12%)
  between operations  1.54 us (7%)
    pallas_call x1, Pallas kernels, interior(): pl.pallas_call(interior_kernel, in_specs=[vmem] * 10, out_specs=[vmem] *...  4.71 us
    ppermute x2, starting transfers between devices, shards(): swapped.append(lax.ppermute(rows, 'brick', pairs))  3.87 us
    pallas_call x1, Pallas kernels, finish(): pl.pallas_call(functools.partial(finish_kernel, width=width, slots=slots)...  2.41 us
    pallas_call x1, Pallas kernels, outer_rows(): pl.pallas_call(outer_kernel, in_specs=[pl.BlockSpec(memory_space=pltpu.HB...  2.38 us
    pallas_call x1, Pallas kernels, assemble(): pl.pallas_call(assemble_kernel, in_specs=[vmem] * 3, out_specs=[vmem] * 2...  1.66 us
    ppermute x1, starting transfers between devices, shards(): received.append(lax.ppermute(both, 'shot', pairs))  1.58 us
    ppermute x2, waiting for transfers between devices, shards(): swapped.append(lax.ppermute(rows, 'brick', pairs))  1.29 us
    ppermute x1, waiting for transfers between devices, shards(): received.append(lax.ppermute(both, 'shot', pairs))  1.1 us
  transfers between devices with their start and end apart: 4, of which 3 were waited for; matrix products, arithmetic and copies ran while one was open for 1% of the time, Pallas kernels for 32%

profile of v13, /device:TPU:16, one launch (start us, length us, event | category | flops | bytes accessed | tf_op | source)
XLA Modules:
  0.0 23.3 jit_solution(8238437197544176959)
XLA Ops:
  0.6 0.0 copy-start
  0.6 0.0 copy-start.1
  0.7 0.0 copy-start.2
  0.7 0.0 copy-start.3
  0.7 0.0 copy-start.5
  0.7 0.0 copy-start.6
  0.7 0.0 copy-start.7
  0.7 0.0 copy-start.8
  0.7 0.0 copy-start.11
  0.7 0.0 copy-start.10
  0.7 0.0 copy-start.9
  0.7 2.4 %outer_rows.1 = (bf16[160,512]{1,0:T(8,128)(2,1)}, bf16[160,512]{1,0:T(8,128)(2,1)}) custom-call(f32[8,4,4,8,128]{4,3,2,1,0:T(8,128)} %bitcast.21, f32[8,4,4,8,128]{4,3,2,1,0:T(8,128)} %bitcast.23, f32[8,4,4,8,128]{4,3,2,1,0:T(8,128)} %bitcast.25, f32[8,4,4,8,128]{4,3,2,1,0:T(8,128)} %bitcast.27, f32[32,512]{1,0:T(8,128)} %refs_4_.1, f32[32,512]{1,0:T(8,128)} %refs_5_.1, ...), custom_call_target="tpu_custom_call" | custom-call | tf_op jit(solution)/shard_map/outer_rows/pallas_call | solution.py:243
  3.1 0.0 copy-start.4
  3.1 1.6 %collective-permute-start = (bf16[160,512]{1,0:T(8,128)(2,1)}, bf16[160,512]{1,0:T(8,128)(2,1)S(1)}, u32[]{:S(2)}, u32[]{:S(2)}) collective-permute-start(bf16[160,512]{1,0:T(8,128)(2,1)} %get-tuple-element.25), channel_id=1, source_target_pairs={{0,1},{1,0},{2,3},{3,2},{4,5},{5,4},{6,7},{7,6},{8,9},{9,8},{10,11... | collective-permute-start | bytes 491528 | tf_op jit(solution)/shard_map/ppermute | solution.py:764
  4.7 2.3 %collective-permute-start.1 = (bf16[160,512]{1,0:T(8,128)(2,1)}, bf16[160,512]{1,0:T(8,128)(2,1)S(1)}, u32[]{:S(2)}, u32[]{:S(2)}) collective-permute-start(bf16[160,512]{1,0:T(8,128)(2,1)} %get-tuple-element.26), channel_id=1, source_target_pairs={{1,2},{2,1},{3,4},{4,3},{5,6},{6,5},{9,10},{10,9},{11,12},{12,11},... | collective-permute-start | bytes 491528 | tf_op jit(solution)/shard_map/ppermute | solution.py:764
  7.0 0.0 copy-done.11
  7.0 0.1 multiply_cosine_fusion
  7.2 0.0 copy-done.10
  7.2 0.0 copy-done
  7.2 0.0 copy-done.1
  7.2 0.0 copy-done.2
  7.2 0.0 copy-done.3
  7.2 0.0 copy-done.5
  7.2 0.0 copy-done.6
  7.2 0.0 copy-done.7
  7.2 0.0 copy-done.8
  7.3 0.0 copy-done.9
  7.3 4.7 %interior.1 = (f32[2,2,4,2,8,512]{5,4,3,2,1,0:T(8,128)S(1)}, f32[2,2,8,512]{3,2,1,0:T(8,128)S(1)}, f32[2,5,8,512]{3,2,1,0:T(8,128)S(1)}, f32[24,8,512]{2,1,0:T(8...) custom-call(f32[8,4,4,8,128]{4,3,2,1,0:T(8,128)S(1)} %bitcast.22, ...), custom_call_target="tpu_custom_call" | custom-call | flops 104857600 | bytes 8388608 | tf_op jit(solution)/shard_map/interior/pallas_call | solution.py:437
  12.0 0.1 pad_maximum_fusion
  12.1 0.0 collective-permute-done.even_ref
  12.1 1.3 %collective-permute-done.1.odd_ref = bf16[160,512]{1,0:T(8,128)(2,1)S(1)} collective-permute-done((bf16[160,512]{1,0:T(8,128)(2,1)}, bf16[160,512]{1,0:T(8,128)(2,1)S(1)}, u32[]{:S(2)}, u32[]{:S(2)}) %collective-permute-start.1) | collective-permute-done | bytes 163872 | tf_op jit(solution)/shard_map/ppermute | solution.py:764
  13.4 0.1 broadcast_in_dim.2.table_ref
  13.4 0.0 copy-done.4
  13.4 2.4 %finish.1 = (f32[256,512]{1,0:T(8,128)}, f32[2,2,4,8,512]{4,3,2,1,0:T(8,128)S(1)}, bf16[256,512]{1,0:T(8,128)(2,1)S(1)}, f32[400,128]{1,0:T(8,128)S(1)}) custom-call(bf16[160,512]{1,0:T(8,128)(2,1)S(1)} %collective-permute-done.even_ref, bf16[160,512]{1,0:T(8,128)(2,1)S(1)} %collective-permute-done.1.odd_ref, ...), custom_call_target="tpu_custom_call" | custom-call | tf_op jit(solution)/shard_map/finish/pallas_call | solution.py:640
  15.9 0.1 collective-permute-start.2
  15.9 1.0 %own_products.1 = (f32[200,128]{1,0:T(8,128)S(1)}, f32[200,128]{1,0:T(8,128)S(1)}) custom-call(bf16[1536,512]{1,0:T(8,128)(2,1)S(1)} %get-tuple-element.33.list_hot_ref, bf16[256,512]{1,0:T(8,128)(2,1)S(1)} %get-tuple-element.38.feature_ref), custom_call_target="tpu_custom_call" | custom-call | flops 536870912 | bytes 2097152 | tf_op jit(solution)/shard_map/own_products/pallas_call | solution.py:492
  16.9 0.4 %collective-permute-done.2.refs_1_ = f32[400,128]{1,0:T(8,128)S(1)} collective-permute-done((f32[400,128]{1,0:T(8,128)S(1)}, f32[400,128]{1,0:T(8,128)S(1)}, u32[]{:S(2)}, u32[]{:S(2)}) %collective-permute-start.2) | collective-permute-done | bytes 204832 | tf_op jit(solution)/shard_map/ppermute | solution.py:787
  17.4 1.6 %collective-permute-start.3 = (f32[200,128]{1,0:T(8,128)S(1)}, f32[200,128]{1,0:T(8,128)S(1)}, u32[]{:S(2)}, u32[]{:S(2)}) collective-permute-start(f32[200,128]{1,0:T(8,128)S(1)} %slice_add_fusion), channel_id=1, source_target_pairs={{0,16},{8,24},{16,0},{24,8},{1,17},{9,25},{17,1},{25,9},{2,18},{10... | collective-permute-start | bytes 307208 | tf_op jit(solution)/shard_map/ppermute | solution.py:794
  19.6 1.7 %assemble.1 = (f32[8,4,4,8,128]{4,3,2,1,0:T(8,128)}, f32[8,4,4,8,128]{4,3,2,1,0:T(8,128)}) custom-call(f32[24,8,512]{2,1,0:T(8,128)S(1)} %get-tuple-element.23.p_inner_ref, f32[24,8,512]{2,1,0:T(8,128)S(1)} %get-tuple-element.24.q_inner_ref, f32[2,2,4,8,512]{4,3,2,1,0:T(8,128)S(1)} %get-tuple-element.34.final_ref), custom_call_target="tpu_custom_call" | custom-call | flops 8388608 | bytes 4194304 | tf_op jit(solution)/shard_map/assemble/pallas_call | solution.py:687
  21.3 1.1 %collective-permute-done.3.refs_2_ = f32[200,128]{1,0:T(8,128)S(1)} collective-permute-done((f32[200,128]{1,0:T(8,128)S(1)}, f32[200,128]{1,0:T(8,128)S(1)}, u32[]{:S(2)}, u32[]{:S(2)}) %collective-permute-start.3) | collective-permute-done | bytes 102432 | tf_op jit(solution)/shard_map/ppermute | solution.py:794
  22.4 0.9 %tiles.1 = f32[1,1,3,128,128]{4,3,2,1,0:T(8,128)} custom-call(s32[1,1]{1,0:T(1,128)S(6)} %copy.18.counts_ref, f32[200,128]{1,0:T(8,128)S(1)} %get-tuple-element.39.refs_0_, f32[400,128]{1,0:T(8,128)S(1)} %collective-permute-done.2.refs_1_, f32[200,128]{1,0:T(8,128)S(1)} %collective-permute-done.3.refs_2_), custom_call_target="tpu_custom_call" | custom-call | tf_op jit(solution)/shard_map/tiles/pallas_call | solution.py:726
  (3 shorter events, 0.0 us)
Async XLA Ops:
  0.6 6.5 %copy-start = (f32[8,32,512]{2,1,0:T(8,128)S(1)}, f32[8,32,512]{2,1,0:T(8,128)}, u32[]{:S(2)}) copy-start(f32[8,32,512]{2,1,0:T(8,128)} %param.13) | copy-start | bytes 1572868
  0.6 6.5 %copy-start.1 = (f32[8,32,512]{2,1,0:T(8,128)S(1)}, f32[8,32,512]{2,1,0:T(8,128)}, u32[]{:S(2)}) copy-start(f32[8,32,512]{2,1,0:T(8,128)} %param.14) | copy-start | bytes 1572868
  0.7 6.5 %copy-start.2 = (f32[8,32,512]{2,1,0:T(8,128)S(1)}, f32[8,32,512]{2,1,0:T(8,128)}, u32[]{:S(2)}) copy-start(f32[8,32,512]{2,1,0:T(8,128)} %param.15) | copy-start | bytes 1572868
  0.7 6.5 %copy-start.3 = (f32[8,32,512]{2,1,0:T(8,128)S(1)}, f32[8,32,512]{2,1,0:T(8,128)}, u32[]{:S(2)}) copy-start(f32[8,32,512]{2,1,0:T(8,128)} %param.16) | copy-start | bytes 1572868
  0.7 6.5 %copy-start.5 = (f32[32,512]{1,0:T(8,128)S(1)}, f32[32,512]{1,0:T(8,128)}, u32[]{:S(2)}) copy-start(f32[32,512]{1,0:T(8,128)} %refs_4_.1) | copy-start | bytes 196612
  0.7 6.5 %copy-start.6 = (f32[32,512]{1,0:T(8,128)S(1)}, f32[32,512]{1,0:T(8,128)}, u32[]{:S(2)}) copy-start(f32[32,512]{1,0:T(8,128)} %refs_5_.1) | copy-start | bytes 196612
  0.7 6.5 %copy-start.7 = (f32[32,512]{1,0:T(8,128)S(1)}, f32[32,512]{1,0:T(8,128)}, u32[]{:S(2)}) copy-start(f32[32,512]{1,0:T(8,128)} %refs_6_.1) | copy-start | bytes 196612
  0.7 6.5 %copy-start.8 = (f32[32,512]{1,0:T(8,128)S(1)}, f32[32,512]{1,0:T(8,128)}, u32[]{:S(2)}) copy-start(f32[32,512]{1,0:T(8,128)} %refs_7_.1) | copy-start | bytes 196612
  0.7 6.3 %copy-start.11 = (f32[16]{0:T(128)S(1)}, f32[16]{0:T(128)}, u32[]{:S(2)}) copy-start(f32[16]{0:T(128)} %param.21) | copy-start | bytes 196
  0.7 6.4 %copy-start.10 = (s32[1,4,3,128]{3,1,2,0:T(4,128)S(1)}, s32[1,4,3,128]{3,1,2,0:T(4,128)}, u32[]{:S(2)}) copy-start(s32[1,4,3,128]{3,1,2,0:T(4,128)} %param.24) | copy-start | bytes 18436
  0.7 6.5 %copy-start.9 = (s32[512]{0:T(512)S(1)}, s32[512]{0:T(512)}, u32[]{:S(2)}) copy-start(s32[512]{0:T(512)} %param.23) | copy-start | bytes 6148
  3.1 10.3 %copy-start.4 = (f32[8,32,512]{2,1,0:T(8,128)S(1)}, f32[8,32,512]{2,1,0:T(8,128)}, u32[]{:S(2)}) copy-start(f32[8,32,512]{2,1,0:T(8,128)} %param.22) | copy-start | bytes 1572868
  3.1 8.9 %collective-permute-start = (bf16[160,512]{1,0:T(8,128)(2,1)}, bf16[160,512]{1,0:T(8,128)(2,1)S(1)}, u32[]{:S(2)}, u32[]{:S(2)}) collective-permute-start(bf16[160,512]{1,0:T(8,128)(2,1)} %get-tuple-element.25), channel_id=1, source_target_pairs={{0,1},{1,0},{2,3},{3,2},{4,5},{5,4},{6,7},{7,6},{8,9},{9,8},{10,11... | collective-permute-start | bytes 491528 | tf_op jit(solution)/shard_map/ppermute | solution.py:764
  4.7 8.7 %collective-permute-start.1 = (bf16[160,512]{1,0:T(8,128)(2,1)}, bf16[160,512]{1,0:T(8,128)(2,1)S(1)}, u32[]{:S(2)}, u32[]{:S(2)}) collective-permute-start(bf16[160,512]{1,0:T(8,128)(2,1)} %get-tuple-element.26), channel_id=1, source_target_pairs={{1,2},{2,1},{3,4},{4,3},{5,6},{6,5},{9,10},{10,9},{11,12},{12,11},... | collective-permute-start | bytes 491528 | tf_op jit(solution)/shard_map/ppermute | solution.py:764
  15.9 1.5 %collective-permute-start.2 = (f32[400,128]{1,0:T(8,128)S(1)}, f32[400,128]{1,0:T(8,128)S(1)}, u32[]{:S(2)}, u32[]{:S(2)}) collective-permute-start(f32[400,128]{1,0:T(8,128)S(1)} %get-tuple-element.40), channel_id=1, source_target_pairs={{0,8},{8,0},{16,24},{24,16},{1,9},{9,1},{17,25},{25,17},{2,10},{10... | collective-permute-start | bytes 614408 | tf_op jit(solution)/shard_map/ppermute | solution.py:787
  17.4 5.0 %collective-permute-start.3 = (f32[200,128]{1,0:T(8,128)S(1)}, f32[200,128]{1,0:T(8,128)S(1)}, u32[]{:S(2)}, u32[]{:S(2)}) collective-permute-start(f32[200,128]{1,0:T(8,128)S(1)} %slice_add_fusion), channel_id=1, source_target_pairs={{0,16},{8,24},{16,0},{24,8},{1,17},{9,25},{17,1},{25,9},{2,18},{10... | collective-permute-start | bytes 307208 | tf_op jit(solution)/shard_map/ppermute | solution.py:794

commit v14 on v13

--- a/solution.py
+++ b/solution.py
@@ -155,11 +155,11 @@
     sources, outs, (field_ref, param_ref, field_sem, param_sem) = refs[:8], refs[8:10], refs[10:]
     shots, across, along, tile, lanes = sources[0].shape
     depth = along * lanes
-    copies = []
+    field_copies, param_copies = [], []
     for side in range(2):
         place = side * (across - 1)
         for i in range(4):
-            copies.append(
+            field_copies.append(
                 pltpu.make_async_copy(
                     sources[i].at[:, pl.ds(place, 1), :, pl.ds(side * STEPS, STEPS)],
                     field_ref.at[side, i, :, :, :, pl.ds(side * STEPS, STEPS)],
@@ -167,19 +167,19 @@
                 )
             )
         for i in range(4):
-            copies.append(
+            param_copies.append(
                 pltpu.make_async_copy(
                     sources[4 + i].at[pl.ds(place * tile, tile)],
                     param_ref.at[side, i],
                     param_sem.at[side, i],
                 )
             )
-    for copy in copies:
+    for copy in param_copies + field_copies:
         copy.start()
+    for copy in param_copies:
+        copy.wait()
     tiles_by_side = []
     for side in range(2):
-        for copy in copies[8 * side : 8 * side + 8]:
-            copy.wait()
         terms = tilt_coefficients(*[param_ref[side, i] for i in range(4)])
         rows = []
         for index, term in enumerate(terms):
@@ -191,6 +191,8 @@
             rows.append(jnp.zeros((1, depth), jnp.float32))
         tiles_by_side.append(jnp.concatenate(rows, 0))
 
+    for copy in field_copies:
+        copy.wait()
     stride = along * tile
     flat = field_ref.reshape(2 * 4 * shots * stride, lanes)
     for turn in range(2):

time: 23.6 us -> 23.5 us (level)
  no operation moved by 1% of the time
where the time goes in v14:
time: 23.5 us; the launch traced here: 23.2 us
  Pallas kernels  13 us (55%)
  starting transfers between devices  5.53 us (24%)
  waiting for transfers between devices  2.81 us (12%)
  between operations  1.54 us (7%)
    pallas_call x1, Pallas kernels, interior(): pl.pallas_call(interior_kernel, in_specs=[vmem] * 10, out_specs=[vmem] *...  4.71 us
    ppermute x2, starting transfers between devices, shards(): swapped.append(lax.ppermute(rows, 'brick', pairs))  3.87 us
    pallas_call x1, Pallas kernels, finish(): pl.pallas_call(functools.partial(finish_kernel, width=width, slots=slots)...  2.41 us
    pallas_call x1, Pallas kernels, outer_rows(): pl.pallas_call(outer_kernel, in_specs=[pl.BlockSpec(memory_space=pltpu.HB...  2.35 us
    pallas_call x1, Pallas kernels, assemble(): pl.pallas_call(assemble_kernel, in_specs=[vmem] * 3, out_specs=[vmem] * 2...  1.66 us
    ppermute x1, starting transfers between devices, shards(): received.append(lax.ppermute(both, 'shot', pairs))  1.58 us
    ppermute x2, waiting for transfers between devices, shards(): swapped.append(lax.ppermute(rows, 'brick', pairs))  1.29 us
    ppermute x1, waiting for transfers between devices, shards(): received.append(lax.ppermute(both, 'shot', pairs))  1.09 us
  transfers between devices with their start and end apart: 4, of which 3 were waited for; matrix products, arithmetic and copies ran while one was open for 1% of the time, Pallas kernels for 32%

profile of v14, /device:TPU:16, one launch (start us, length us, event | category | flops | bytes accessed | tf_op | source)
XLA Modules:
  0.0 23.2 jit_solution(9735821736994229287)
XLA Ops:
  0.6 0.0 copy-start
  0.6 0.0 copy-start.1
  0.7 0.0 copy-start.2
  0.7 0.0 copy-start.3
  0.7 0.0 copy-start.5
  0.7 0.0 copy-start.6
  0.7 0.0 copy-start.7
  0.7 0.0 copy-start.8
  0.7 0.0 copy-start.11
  0.7 0.0 copy-start.10
  0.7 0.0 copy-start.9
  0.7 2.4 %outer_rows.1 = (bf16[160,512]{1,0:T(8,128)(2,1)}, bf16[160,512]{1,0:T(8,128)(2,1)}) custom-call(f32[8,4,4,8,128]{4,3,2,1,0:T(8,128)} %bitcast.21, f32[8,4,4,8,128]{4,3,2,1,0:T(8,128)} %bitcast.23, f32[8,4,4,8,128]{4,3,2,1,0:T(8,128)} %bitcast.25, f32[8,4,4,8,128]{4,3,2,1,0:T(8,128)} %bitcast.27, f32[32,512]{1,0:T(8,128)} %refs_4_.1, f32[32,512]{1,0:T(8,128)} %refs_5_.1, ...), custom_call_target="tpu_custom_call" | custom-call | tf_op jit(solution)/shard_map/outer_rows/pallas_call | solution.py:245
  3.1 0.0 copy-start.4
  3.1 1.6 %collective-permute-start = (bf16[160,512]{1,0:T(8,128)(2,1)}, bf16[160,512]{1,0:T(8,128)(2,1)S(1)}, u32[]{:S(2)}, u32[]{:S(2)}) collective-permute-start(bf16[160,512]{1,0:T(8,128)(2,1)} %get-tuple-element.25), channel_id=1, source_target_pairs={{0,1},{1,0},{2,3},{3,2},{4,5},{5,4},{6,7},{7,6},{8,9},{9,8},{10,11... | collective-permute-start | bytes 491528 | tf_op jit(solution)/shard_map/ppermute | solution.py:766
  4.7 2.3 %collective-permute-start.1 = (bf16[160,512]{1,0:T(8,128)(2,1)}, bf16[160,512]{1,0:T(8,128)(2,1)S(1)}, u32[]{:S(2)}, u32[]{:S(2)}) collective-permute-start(bf16[160,512]{1,0:T(8,128)(2,1)} %get-tuple-element.26), channel_id=1, source_target_pairs={{1,2},{2,1},{3,4},{4,3},{5,6},{6,5},{9,10},{10,9},{11,12},{12,11},... | collective-permute-start | bytes 491528 | tf_op jit(solution)/shard_map/ppermute | solution.py:766
  7.0 0.0 copy-done.11
  7.0 0.1 multiply_cosine_fusion
  7.1 0.0 copy-done.10
  7.2 0.0 copy-done
  7.2 0.0 copy-done.1
  7.2 0.0 copy-done.2
  7.2 0.0 copy-done.3
  7.2 0.0 copy-done.5
  7.2 0.0 copy-done.6
  7.2 0.0 copy-done.7
  7.2 0.0 copy-done.8
  7.2 0.0 copy-done.9
  7.2 4.7 %interior.1 = (f32[2,2,4,2,8,512]{5,4,3,2,1,0:T(8,128)S(1)}, f32[2,2,8,512]{3,2,1,0:T(8,128)S(1)}, f32[2,5,8,512]{3,2,1,0:T(8,128)S(1)}, f32[24,8,512]{2,1,0:T(8...) custom-call(f32[8,4,4,8,128]{4,3,2,1,0:T(8,128)S(1)} %bitcast.22, ...), custom_call_target="tpu_custom_call" | custom-call | flops 104857600 | bytes 8388608 | tf_op jit(solution)/shard_map/interior/pallas_call | solution.py:439
  12.0 0.1 pad_maximum_fusion
  12.0 0.0 collective-permute-done.even_ref
  12.0 1.3 %collective-permute-done.1.odd_ref = bf16[160,512]{1,0:T(8,128)(2,1)S(1)} collective-permute-done((bf16[160,512]{1,0:T(8,128)(2,1)}, bf16[160,512]{1,0:T(8,128)(2,1)S(1)}, u32[]{:S(2)}, u32[]{:S(2)}) %collective-permute-start.1) | collective-permute-done | bytes 163872 | tf_op jit(solution)/shard_map/ppermute | solution.py:766
  13.3 0.1 broadcast_in_dim.2.table_ref
  13.4 0.0 copy-done.4
  13.4 2.4 %finish.1 = (f32[256,512]{1,0:T(8,128)}, f32[2,2,4,8,512]{4,3,2,1,0:T(8,128)S(1)}, bf16[256,512]{1,0:T(8,128)(2,1)S(1)}, f32[400,128]{1,0:T(8,128)S(1)}) custom-call(bf16[160,512]{1,0:T(8,128)(2,1)S(1)} %collective-permute-done.even_ref, bf16[160,512]{1,0:T(8,128)(2,1)S(1)} %collective-permute-done.1.odd_ref, ...), custom_call_target="tpu_custom_call" | custom-call | tf_op jit(solution)/shard_map/finish/pallas_call | solution.py:642
  15.8 0.1 collective-permute-start.2
  15.9 1.0 %own_products.1 = (f32[200,128]{1,0:T(8,128)S(1)}, f32[200,128]{1,0:T(8,128)S(1)}) custom-call(bf16[1536,512]{1,0:T(8,128)(2,1)S(1)} %get-tuple-element.33.list_hot_ref, bf16[256,512]{1,0:T(8,128)(2,1)S(1)} %get-tuple-element.38.feature_ref), custom_call_target="tpu_custom_call" | custom-call | flops 536870912 | bytes 2097152 | tf_op jit(solution)/shard_map/own_products/pallas_call | solution.py:494
  16.9 0.4 %collective-permute-done.2.refs_1_ = f32[400,128]{1,0:T(8,128)S(1)} collective-permute-done((f32[400,128]{1,0:T(8,128)S(1)}, f32[400,128]{1,0:T(8,128)S(1)}, u32[]{:S(2)}, u32[]{:S(2)}) %collective-permute-start.2) | collective-permute-done | bytes 204832 | tf_op jit(solution)/shard_map/ppermute | solution.py:789
  17.4 1.6 %collective-permute-start.3 = (f32[200,128]{1,0:T(8,128)S(1)}, f32[200,128]{1,0:T(8,128)S(1)}, u32[]{:S(2)}, u32[]{:S(2)}) collective-permute-start(f32[200,128]{1,0:T(8,128)S(1)} %slice_add_fusion), channel_id=1, source_target_pairs={{0,16},{8,24},{16,0},{24,8},{1,17},{9,25},{17,1},{25,9},{2,18},{10... | collective-permute-start | bytes 307208 | tf_op jit(solution)/shard_map/ppermute | solution.py:796
  19.6 1.7 %assemble.1 = (f32[8,4,4,8,128]{4,3,2,1,0:T(8,128)}, f32[8,4,4,8,128]{4,3,2,1,0:T(8,128)}) custom-call(f32[24,8,512]{2,1,0:T(8,128)S(1)} %get-tuple-element.23.p_inner_ref, f32[24,8,512]{2,1,0:T(8,128)S(1)} %get-tuple-element.24.q_inner_ref, f32[2,2,4,8,512]{4,3,2,1,0:T(8,128)S(1)} %get-tuple-element.34.final_ref), custom_call_target="tpu_custom_call" | custom-call | flops 8388608 | bytes 4194304 | tf_op jit(solution)/shard_map/assemble/pallas_call | solution.py:689
  21.3 1.1 %collective-permute-done.3.refs_2_ = f32[200,128]{1,0:T(8,128)S(1)} collective-permute-done((f32[200,128]{1,0:T(8,128)S(1)}, f32[200,128]{1,0:T(8,128)S(1)}, u32[]{:S(2)}, u32[]{:S(2)}) %collective-permute-start.3) | collective-permute-done | bytes 102432 | tf_op jit(solution)/shard_map/ppermute | solution.py:796
  22.4 0.9 %tiles.1 = f32[1,1,3,128,128]{4,3,2,1,0:T(8,128)} custom-call(s32[1,1]{1,0:T(1,128)S(6)} %copy.18.counts_ref, f32[200,128]{1,0:T(8,128)S(1)} %get-tuple-element.39.refs_0_, f32[400,128]{1,0:T(8,128)S(1)} %collective-permute-done.2.refs_1_, f32[200,128]{1,0:T(8,128)S(1)} %collective-permute-done.3.refs_2_), custom_call_target="tpu_custom_call" | custom-call | tf_op jit(solution)/shard_map/tiles/pallas_call | solution.py:728
  (3 shorter events, 0.0 us)
Async XLA Ops:
  0.6 6.5 %copy-start = (f32[8,32,512]{2,1,0:T(8,128)S(1)}, f32[8,32,512]{2,1,0:T(8,128)}, u32[]{:S(2)}) copy-start(f32[8,32,512]{2,1,0:T(8,128)} %param.13) | copy-start | bytes 1572868
  0.6 6.5 %copy-start.1 = (f32[8,32,512]{2,1,0:T(8,128)S(1)}, f32[8,32,512]{2,1,0:T(8,128)}, u32[]{:S(2)}) copy-start(f32[8,32,512]{2,1,0:T(8,128)} %param.14) | copy-start | bytes 1572868
  0.7 6.5 %copy-start.2 = (f32[8,32,512]{2,1,0:T(8,128)S(1)}, f32[8,32,512]{2,1,0:T(8,128)}, u32[]{:S(2)}) copy-start(f32[8,32,512]{2,1,0:T(8,128)} %param.15) | copy-start | bytes 1572868
  0.7 6.5 %copy-start.3 = (f32[8,32,512]{2,1,0:T(8,128)S(1)}, f32[8,32,512]{2,1,0:T(8,128)}, u32[]{:S(2)}) copy-start(f32[8,32,512]{2,1,0:T(8,128)} %param.16) | copy-start | bytes 1572868
  0.7 6.5 %copy-start.5 = (f32[32,512]{1,0:T(8,128)S(1)}, f32[32,512]{1,0:T(8,128)}, u32[]{:S(2)}) copy-start(f32[32,512]{1,0:T(8,128)} %refs_4_.1) | copy-start | bytes 196612
  0.7 6.5 %copy-start.6 = (f32[32,512]{1,0:T(8,128)S(1)}, f32[32,512]{1,0:T(8,128)}, u32[]{:S(2)}) copy-start(f32[32,512]{1,0:T(8,128)} %refs_5_.1) | copy-start | bytes 196612
  0.7 6.5 %copy-start.7 = (f32[32,512]{1,0:T(8,128)S(1)}, f32[32,512]{1,0:T(8,128)}, u32[]{:S(2)}) copy-start(f32[32,512]{1,0:T(8,128)} %refs_6_.1) | copy-start | bytes 196612
  0.7 6.5 %copy-start.8 = (f32[32,512]{1,0:T(8,128)S(1)}, f32[32,512]{1,0:T(8,128)}, u32[]{:S(2)}) copy-start(f32[32,512]{1,0:T(8,128)} %refs_7_.1) | copy-start | bytes 196612
  0.7 6.3 %copy-start.11 = (f32[16]{0:T(128)S(1)}, f32[16]{0:T(128)}, u32[]{:S(2)}) copy-start(f32[16]{0:T(128)} %param.21) | copy-start | bytes 196
  0.7 6.4 %copy-start.10 = (s32[1,4,3,128]{3,1,2,0:T(4,128)S(1)}, s32[1,4,3,128]{3,1,2,0:T(4,128)}, u32[]{:S(2)}) copy-start(s32[1,4,3,128]{3,1,2,0:T(4,128)} %param.24) | copy-start | bytes 18436
  0.7 6.5 %copy-start.9 = (s32[512]{0:T(512)S(1)}, s32[512]{0:T(512)}, u32[]{:S(2)}) copy-start(s32[512]{0:T(512)} %param.23) | copy-start | bytes 6148
  3.1 10.3 %copy-start.4 = (f32[8,32,512]{2,1,0:T(8,128)S(1)}, f32[8,32,512]{2,1,0:T(8,128)}, u32[]{:S(2)}) copy-start(f32[8,32,512]{2,1,0:T(8,128)} %param.22) | copy-start | bytes 1572868
  3.1 8.9 %collective-permute-start = (bf16[160,512]{1,0:T(8,128)(2,1)}, bf16[160,512]{1,0:T(8,128)(2,1)S(1)}, u32[]{:S(2)}, u32[]{:S(2)}) collective-permute-start(bf16[160,512]{1,0:T(8,128)(2,1)} %get-tuple-element.25), channel_id=1, source_target_pairs={{0,1},{1,0},{2,3},{3,2},{4,5},{5,4},{6,7},{7,6},{8,9},{9,8},{10,11... | collective-permute-start | bytes 491528 | tf_op jit(solution)/shard_map/ppermute | solution.py:766
  4.7 8.7 %collective-permute-start.1 = (bf16[160,512]{1,0:T(8,128)(2,1)}, bf16[160,512]{1,0:T(8,128)(2,1)S(1)}, u32[]{:S(2)}, u32[]{:S(2)}) collective-permute-start(bf16[160,512]{1,0:T(8,128)(2,1)} %get-tuple-element.26), channel_id=1, source_target_pairs={{1,2},{2,1},{3,4},{4,3},{5,6},{6,5},{9,10},{10,9},{11,12},{12,11},... | collective-permute-start | bytes 491528 | tf_op jit(solution)/shard_map/ppermute | solution.py:766
  15.8 1.5 %collective-permute-start.2 = (f32[400,128]{1,0:T(8,128)S(1)}, f32[400,128]{1,0:T(8,128)S(1)}, u32[]{:S(2)}, u32[]{:S(2)}) collective-permute-start(f32[400,128]{1,0:T(8,128)S(1)} %get-tuple-element.40), channel_id=1, source_target_pairs={{0,8},{8,0},{16,24},{24,16},{1,9},{9,1},{17,25},{25,17},{2,10},{10... | collective-permute-start | bytes 614408 | tf_op jit(solution)/shard_map/ppermute | solution.py:789
  17.4 5.0 %collective-permute-start.3 = (f32[200,128]{1,0:T(8,128)S(1)}, f32[200,128]{1,0:T(8,128)S(1)}, u32[]{:S(2)}, u32[]{:S(2)}) collective-permute-start(f32[200,128]{1,0:T(8,128)S(1)} %slice_add_fusion), channel_id=1, source_target_pairs={{0,16},{8,24},{16,0},{24,8},{1,17},{9,25},{17,1},{25,9},{2,18},{10... | collective-permute-start | bytes 307208 | tf_op jit(solution)/shard_map/ppermute | solution.py:796
